TPU v7x, 128 devices: a whole 4x4x4 slice. The times are simulated.
128 devices in a mesh: gx: 32 (over y, z, core), gy: 4 (over x).
Axes of the slice: x: 4, y: 4, z: 4, core: 2. Of those that a mesh axis runs over, the one named last changes fastest.
Arguments:
- features: bfloat16 [256, 8, 8, 8, 256], P(('gx', 'gy')), may hold values from -6 to 6
- cotangent: bfloat16 [256, 8, 8, 8, 256], P(('gx', 'gy')), may hold values from -6 to 6
- kernel: bfloat16 [27, 256, 256], replicated, may hold values from -0.078125 to 0.078125
- occupancy: int32 [256, 512], P(('gx', 'gy')), may hold values 0 or 1
- neighbors: int32 [256, 27], P(('gx', 'gy')), may hold values from -1 to 1, as said below
Outputs:
- out_features: bfloat16 [256, 8, 8, 8, 256], P(('gx', 'gy'))
- in_grad: bfloat16 [256, 8, 8, 8, 256], P(('gx', 'gy'))
- kernel_grad: float32 [27, 256, 256], replicated
Inputs may be any that keep to these rules, and one draw needn't show every extreme that they name: neighbors[b, k] is the slot of the occupied brick at level L + oz in column (cx + ox, cy + oy), where L is brick b's level, and -1 where that column lies outside the 32 x 4 grid or that brick is not occupied; each column holds 2 occupied bricks among 4 levels, slots in rising level; the offset k = 13 entry of a brick is its own slot.
All inputs are finite; a program needn't handle non-finite values. No bound on the sum of `occupancy` on one device may be relied on, other than what follows from the above.
Results may differ from a plain program's by a relative error of at most 0.001.
Values may be sent and summed in bfloat16 or wider, within the bound.
No kernel may reach another device: no remote copies, remote signals or barrier semaphores. Data moves between devices by JAX's collectives and lax.ppermute only.
A program may use at most 128 MiB of HBM per device.

v0:
```python
import jax
import jax.numpy as jnp
from jax import lax
from jax.sharding import PartitionSpec as P

layer_pick = {-1: slice(7, 8), 0: slice(0, 8), 1: slice(0, 1)}


def extended(cells, sides, width):
    for axis, dim in sides:
        count = lax.axis_size(axis)
        ends = count - 1
        head = lax.slice_in_dim(cells, 0, width, axis=dim)
        tail = lax.slice_in_dim(cells, cells.shape[dim] - width, cells.shape[dim], axis=dim)
        cells = jnp.concatenate(
            [
                lax.ppermute(tail, axis, [(i, (i + 1) % count) for i in range(ends)]),
                cells,
                lax.ppermute(head, axis, [((i + 1) % count, i) for i in range(ends)]),
            ],
            axis=dim,
        )
    return cells


def assemble(source_of, neighbors, slots):
    chosen = jnp.where(neighbors >= 0, neighbors, slots)
    x_parts = []
    for ox in (-1, 0, 1):
        y_parts = []
        for oy in (-1, 0, 1):
            source = source_of(ox, oy)
            source = jnp.concatenate([source, jnp.zeros_like(source[:, :1])], 1)
            z_parts = []
            for oz in (-1, 0, 1):
                offset = 9 * (ox + 1) + 3 * (oy + 1) + (oz + 1)
                picked = jnp.take(source, chosen[:, offset], axis=1)
                z_parts.append(picked[:, :, :, :, layer_pick[oz]])
            y_parts.append(jnp.concatenate(z_parts, 4))
        x_parts.append(jnp.concatenate(y_parts, 3))
    return jnp.concatenate(x_parts, 2)


def combine_terms(terms, scale):
    return lax.psum(terms, ("gx", "gy")) * scale


def shards(features, cotangent, kernel, occupancy, neighbors):
    slots = features.shape[0]
    width = features.shape[-1]
    mask_b = occupancy.reshape(slots, 8, 8, 8, 1).astype(jnp.bfloat16)
    mask_f = occupancy.reshape(slots * 512, 1).astype(jnp.float32)
    masked = features * mask_b
    masked_grad = cotangent * mask_b
    both = jnp.stack([masked, masked_grad])
    beside_all = extended(both[None, None], (("gx", 0), ("gy", 1)), 1)

    def source_of(ox, oy):
        return beside_all[ox + 1, oy + 1][:, :, layer_pick[ox], layer_pick[oy]]

    padded = assemble(source_of, neighbors, slots)
    padded_in = padded[0]
    padded_grad = padded[1]
    flat_grad = masked_grad.reshape(-1, width)
    scale = jnp.float32(1.0 / (512.0 * slots * lax.axis_size("gx") * lax.axis_size("gy")) ** 0.5)
    forward = jnp.zeros((slots * 512, width), jnp.float32)
    terms = []
    for step_x in range(3):
        for step_y in range(3):
            for step_z in range(3):
                offset = 9 * step_x + 3 * step_y + step_z
                window = padded_in[
                    :, step_x : step_x + 8, step_y : step_y + 8, step_z : step_z + 8
                ].reshape(-1, width)
                forward = forward + jnp.dot(
                    window, kernel[offset], preferred_element_type=jnp.float32
                )
                terms.append(
                    lax.dot_general(
                        window,
                        flat_grad,
                        (((0,), (0,)), ((), ())),
                        preferred_element_type=jnp.float32,
                    )
                )
    forward, terms = (forward, jnp.stack(terms))
    backward = jnp.zeros((slots * 512, width), jnp.float32)
    for step_x in range(3):
        for step_y in range(3):
            for step_z in range(3):
                offset = 9 * step_x + 3 * step_y + step_z
                back_window = padded_grad[
                    :, 2 - step_x : 10 - step_x, 2 - step_y : 10 - step_y, 2 - step_z : 10 - step_z
                ].reshape(-1, width)
                backward = backward + lax.dot_general(
                    back_window,
                    kernel[offset],
                    (((1,), (1,)), ((), ())),
                    preferred_element_type=jnp.float32,
                )
    kernel_grad = combine_terms(terms, scale)
    out_features = (forward * mask_f).astype(jnp.bfloat16).reshape(slots, 8, 8, 8, width)
    in_grad = (backward * mask_f).astype(jnp.bfloat16).reshape(slots, 8, 8, 8, width)
    return (out_features, in_grad, kernel_grad)


def solution(mesh):
    placed = (
        P(("gx", "gy"), None, None, None, None),
        P(("gx", "gy"), None, None, None, None),
        P(),
        P(("gx", "gy"), None),
        P(("gx", "gy"), None),
    )
    return jax.shard_map(
        shards,
        mesh=mesh,
        in_specs=placed,
        out_specs=(
            P(("gx", "gy"), None, None, None, None),
            P(("gx", "gy"), None, None, None, None),
            P(),
        ),
        check_vma=False,
    )
```

profile of v0, /device:TPU:1, one launch (start us, length us, event | category | flops | bytes accessed | tf_op | source)
XLA Modules:
  0.0 376.9 jit_solution(6523150212637886183)
XLA Ops:
  8.1 1.4 fusion.34
  10.3 1.1 pad_maximum_fusion.1
  11.5 3.3 collective-permute-start.1
  14.8 3.5 collective-permute-start
  26.7 1.6 gather_fusion.14
  33.0 1.4 fusion.31
  34.4 3.9 %pad_maximum_fusion = bf16[3,1,2,2,8,8,8,256]{7,6,3,2,5,4,1,0:T(8,128)(2,1)} fusion(bf16[1,1,2,2,8,8,8,256]{7,6,3,2,5,4,1,0:T(8,128)(2,1)} %collective-permute-done.1, bf16[1,1,2,2,8,8,8,256]{7,6,3,2,5,4,1,0:T(8,128)(2,1)} %get-tuple-element.97, bf16[1,1,2,2,8,8,8,256]{7,6,3,2,5,4,1,0:T(8,128)(2,1)} %collective-permute-done), kind=kLoop, calls=%fused_computation.29 | loop fusion | flops 3145728 | bytes 6291456 | tf_op jit(solution)/shard_map/concatenate | solution.py:15
  38.3 1.3 collective-permute-start.3
  40.2 1.1 fusion.33
  41.3 5.7 %collective-permute-start.2 = (bf16[3,1,2,2,8,8,8,256]{7,6,3,2,5,4,1,0:T(8,128)(2,1)}, bf16[3,1,2,2,8,8,8,256]{7,6,3,2,5,4,1,0:T(8,128)(2,1)}, u32[]{:S(2)}, u32[]{:S(2)}) collective-permute-start(bf16[3,1,2,2,8,8,8,256]{7,6,3,2,5,4,1,0:T(8,128)(2,1)} %pad_maximum_fusion), channel_id=1, source_target_pairs={{0,1},{1,2},{2,3},{4,5},{5,6},{6,7},{8,9},{9,10},{10,11},{12,13},{... | collective-permute-start | bytes 9437192 | tf_op jit(solution)/shard_map/ppermute | solution.py:17
  48.4 2.2 slice.664
  62.1 48.2 %collective-permute-done.3 = bf16[3,1,2,2,8,8,8,256]{7,6,3,2,5,4,1,0:T(8,128)(2,1)} collective-permute-done((bf16[3,1,2,2,8,8,8,256]{7,6,3,2,5,4,1,0:T(8,128)(2,1)}, bf16[3,1,2,2,8,8,8,256]{7,6,3,2,5,4,1,0:T(8,128)(2,1)}, u32[]{:S(2)}, u32[]{:S(2)}) %collective-permute-start.3) | collective-permute-done | bytes 3145760 | tf_op jit(solution)/shard_map/ppermute | solution.py:19
  110.3 3.3 slice_bitcast_fusion.6
  116.4 3.2 slice_bitcast_fusion.7
  120.3 2.0 gather_fusion.20
  122.3 1.3 copy.211
  123.6 2.0 gather_fusion.19
  125.6 2.0 gather_fusion.18
  127.6 1.3 copy.212
  153.6 2.7 maximum_maximum_fusion
  156.6 2.5 fusion.203
  159.1 4.4 %fusion.202 = (bf16[2,8,8,8,256]{4,3,2,1,0:T(8,128)(2,1)}, bf16[2,8,8,8,256]{4,3,2,1,0:T(8,128)(2,1)}, bf16[2,8,8,8,256]{4,3,2,1,0:T(8,128)(2,1)}, bf16[2,8,8,8,...) fusion(bf16[2,10,10,10,256]{4,3,2,1,0:T(8,128)(2,1)S(1)} %get-t, ...), kind=kLoop, calls=%fused_computation.483 | loop fusion | bytes 19922944 | tf_op jit(solution)/shard_map/slice | solution.py:72
  163.5 2.3 fusion.201
  165.7 4.2 %fusion.200 = (bf16[2,8,8,8,256]{4,3,2,1,0:T(8,128)(2,1)}, bf16[2,8,8,8,256]{4,3,2,1,0:T(8,128)(2,1)}, bf16[2,8,8,8,256]{4,3,2,1,0:T(8,128)(2,1)}, bf16[2,8,8,8,...) fusion(bf16[2,10,10,10,256]{4,3,2,1,0:T(8,128)(2,1)S(1)} %get-t, ...), kind=kLoop, calls=%fused_computation.481 | loop fusion | bytes 19922944 | tf_op jit(solution)/shard_map/slice | solution.py:92
  172.0 1.3 fusion.89
  173.3 1.3 fusion.87
  174.6 1.1 fusion.29
  178.9 1.1 fusion.25
  181.0 1.1 fusion.23
  182.0 1.1 fusion.22
  184.2 1.1 fusion.20
  185.2 1.1 fusion.19
  187.3 1.1 fusion.17
  188.4 1.1 fusion.16
  190.5 1.1 fusion.14
  191.6 1.1 fusion.13
  193.7 1.1 fusion.11
  194.8 1.1 fusion.10
  196.9 1.1 fusion.8
  197.9 1.1 fusion.7
  200.1 1.1 fusion.5
  201.1 1.1 fusion.4
  202.2 1.8 convolution_add_fusion.51
  204.0 1.4 convolution_add_fusion.50
  219.8 1.1 fusion.2
  225.0 1.1 fusion.3
  226.2 137.0 %all-reduce.11.cloned.1.call-done = f32[27,256,256]{2,1,0:T(8,128)} async-done(((f32[27,256,256]{2,1,0:T(8,128)}), f32[27,256,256]{2,1,0:T(8,128)}) %all-reduce.11.cloned.1.call-update) | async-done | bytes 7077904 | tf_op jit(solution)/shard_map/psum | solution.py:45
  363.1 6.9 %broadcast_multiply_fusion = f32[27,256,256]{2,1,0:T(8,128)} fusion(f32[27,256,256]{2,1,0:T(8,128)} %all-reduce.11.cloned.1.call-done), kind=kLoop, calls=%fused_computation.27 | loop fusion | flops 1769472 | bytes 14155776 | tf_op jit(solution)/shard_map/mul | solution.py:45
  (338 shorter events, 86.6 us)
Async XLA Ops:
  7.2 11.2 %copy-start.61 = (s32[2,27]{1,0:T(2,128)S(1)}, s32[2,27]{1,0:T(2,128)}, u32[]{:S(2)}) copy-start(s32[2,27]{1,0:T(2,128)} %param.17) | copy-start | bytes 652
  7.2 356.0 %all-reduce.11.cloned.1.call-start = ((), (), s32[]{:S(2)}) async-start(), calls=%async_computation | async-start | bytes 14155776 | tf_op jit(solution)/shard_map/psum | solution.py:45
  11.5 22.9 %collective-permute-start.1 = (bf16[1,1,2,2,8,8,8,256]{7,6,3,2,5,4,1,0:T(8,128)(2,1)}, bf16[1,1,2,2,8,8,8,256]{7,6,3,2,5,4,1,0:T(8,128)(2,1)}, u32[]{:S(2)}, u32[]{:S(2)}) collective-permute-start(bf16[1,1,2,2,8,8,8,256]{7,6,3,2,5,4,1,0:T(8,128)(2,1)} %get-tuple-element.97), channel_id=1, source_target_pairs={{4,0},{8,4},{12,8},{16,12},{20,16},{24,20},{28,24},{32,28},{36,32}... | collective-permute-start | bytes 3145736 | tf_op jit(solution)/shard_map/ppermute | solution.py:19
  14.8 19.6 %collective-permute-start = (bf16[1,1,2,2,8,8,8,256]{7,6,3,2,5,4,1,0:T(8,128)(2,1)}, bf16[1,1,2,2,8,8,8,256]{7,6,3,2,5,4,1,0:T(8,128)(2,1)}, u32[]{:S(2)}, u32[]{:S(2)}) collective-permute-start(bf16[1,1,2,2,8,8,8,256]{7,6,3,2,5,4,1,0:T(8,128)(2,1)} %get-tuple-element.97), channel_id=1, source_target_pairs={{0,4},{4,8},{8,12},{12,16},{16,20},{20,24},{24,28},{28,32},{32,36}... | collective-permute-start | bytes 3145736 | tf_op jit(solution)/shard_map/ppermute | solution.py:17
  38.3 72.0 %collective-permute-start.3 = (bf16[3,1,2,2,8,8,8,256]{7,6,3,2,5,4,1,0:T(8,128)(2,1)}, bf16[3,1,2,2,8,8,8,256]{7,6,3,2,5,4,1,0:T(8,128)(2,1)}, u32[]{:S(2)}, u32[]{:S(2)}) collective-permute-start(bf16[3,1,2,2,8,8,8,256]{7,6,3,2,5,4,1,0:T(8,128)(2,1)} %pad_maximum_fusion), channel_id=1, source_target_pairs={{1,0},{2,1},{3,2},{5,4},{6,5},{7,6},{9,8},{10,9},{11,10},{13,12},{... | collective-permute-start | bytes 9437192 | tf_op jit(solution)/shard_map/ppermute | solution.py:19
  41.3 75.1 %collective-permute-start.2 = (bf16[3,1,2,2,8,8,8,256]{7,6,3,2,5,4,1,0:T(8,128)(2,1)}, bf16[3,1,2,2,8,8,8,256]{7,6,3,2,5,4,1,0:T(8,128)(2,1)}, u32[]{:S(2)}, u32[]{:S(2)}) collective-permute-start(bf16[3,1,2,2,8,8,8,256]{7,6,3,2,5,4,1,0:T(8,128)(2,1)} %pad_maximum_fusion), channel_id=1, source_target_pairs={{0,1},{1,2},{2,3},{4,5},{5,6},{6,7},{8,9},{9,10},{10,11},{12,13},{... | collective-permute-start | bytes 9437192 | tf_op jit(solution)/shard_map/ppermute | solution.py:17
  128.9 24.6 %copy-start.54 = (bf16[2,2,8,8,1,256]{5,4,3,2,1,0:T(2,128)(2,1)S(1)}, bf16[2,2,8,8,1,256]{5,4,3,2,1,0:T(2,128)(2,1)}, u32[]{:S(2)}) copy-start(bf16[2,2,8,8,1,256]{5,4,3,2,1,0:T(2,128)(2,1)} %slice.664) | copy-start | bytes 393220
  128.9 24.6 %copy-start.55 = (bf16[2,2,1,8,8,256]{5,4,3,2,1,0:T(8,128)(2,1)S(1)}, bf16[2,2,1,8,8,256]{5,4,3,2,1,0:T(8,128)(2,1)}, u32[]{:S(2)}) copy-start(bf16[2,2,1,8,8,256]{5,4,3,2,1,0:T(8,128)(2,1)} %bitcast_select_fusion.3) | copy-start | bytes 393220
  132.5 20.9 %copy-start.62 = (pred[2]{0:T(512)(128)(4,1)S(1)}, pred[2]{0:T(512)(128)(4,1)}, u32[]{:S(2)}) copy-start(pred[2]{0:T(512)(128)(4,1)} %compare_and_fusion.26) | copy-start | bytes 10
  132.5 21.0 %copy-start.56 = (bf16[2,2,1,8,1,256]{5,4,3,2,1,0:T(2,128)(2,1)S(1)}, bf16[2,2,1,8,1,256]{5,4,3,2,1,0:T(2,128)(2,1)}, u32[]{:S(2)}) copy-start(bf16[2,2,1,8,1,256]{5,4,3,2,1,0:T(2,128)(2,1)} %broadcast_select_fusion) | copy-start | bytes 49156
  132.5 21.0 %copy-start.57 = (bf16[2,2,1,8,1,256]{5,4,3,2,1,0:T(2,128)(2,1)S(1)}, bf16[2,2,1,8,1,256]{5,4,3,2,1,0:T(2,128)(2,1)}, u32[]{:S(2)}) copy-start(bf16[2,2,1,8,1,256]{5,4,3,2,1,0:T(2,128)(2,1)} %broadcast_select_fusion.1) | copy-start | bytes 49156
  132.5 21.0 %copy-start.58 = (bf16[2,2,1,8,1,256]{5,4,3,2,1,0:T(2,128)(2,1)S(1)}, bf16[2,2,1,8,1,256]{5,4,3,2,1,0:T(2,128)(2,1)}, u32[]{:S(2)}) copy-start(bf16[2,2,1,8,1,256]{5,4,3,2,1,0:T(2,128)(2,1)} %broadcast_select_fusion.6) | copy-start | bytes 49156
  132.5 21.0 %copy-start.59 = (bf16[2,2,1,8,1,256]{5,4,3,2,1,0:T(2,128)(2,1)S(1)}, bf16[2,2,1,8,1,256]{5,4,3,2,1,0:T(2,128)(2,1)}, u32[]{:S(2)}) copy-start(bf16[2,2,1,8,1,256]{5,4,3,2,1,0:T(2,128)(2,1)} %broadcast_select_fusion.7) | copy-start | bytes 49156
  165.7 4.2 %copy-start.53 = (bf16[2,8,8,8,256]{4,3,0,2,1:T(8,128)(2,1)S(1)}, bf16[2,8,8,8,256]{4,3,0,2,1:T(8,128)(2,1)}, u32[]{:S(2)}) copy-start(bf16[2,8,8,8,256]{4,3,0,2,1:T(8,128)(2,1)} %copy-done.52) | copy-start | bytes 1572868
  169.9 2.1 copy-start
  202.2 3.2 copy-start.51
  202.2 3.5 copy-start.50
  204.0 2.1 copy-start.49
  209.1 1.3 copy-start.38
  209.5 1.2 copy-start.37
  209.8 1.2 copy-start.36
  210.4 1.1 copy-start.35
  211.5 1.2 copy-start.32
  211.8 1.3 copy-start.31
  212.1 1.3 copy-start.29
  212.7 1.1 copy-start.27
  213.1 1.3 copy-start.1
  213.1 1.4 copy-start.30
  213.4 1.5 copy-start.28
  213.9 1.4 copy-start.26
  215.7 1.1 copy-start.22
  216.0 1.1 copy-start.21
  216.4 1.1 copy-start.20
  216.8 1.2 copy-start.19
  217.2 1.1 copy-start.18
  217.5 1.1 copy-start.17
  218.0 1.1 copy-start.16
  218.3 1.1 copy-start.15
  218.7 1.1 copy-start.3
  218.7 1.1 copy-start.60
  219.1 1.8 copy-start.14
  219.4 1.8 copy-start.13
  219.8 1.8 copy-start.12
  221.6 1.1 copy-start.9
  222.0 1.1 copy-start.8
  222.4 1.1 copy-start.7
  222.8 1.1 copy-start.6
  223.1 1.1 copy-start.5
  (20 other events, 21.9 us)
Sparse Core Ops, SparseCore 0:
  202.3 160.7 all-reduce.10
where the time goes:
time: 379 us; the launch traced here: 377 us
  waiting for transfers between devices  185 us (49%)
  local copies, waits for them, and re-layouts  59.9 us (16%)
  matrix products  51.9 us (14%)
  other arithmetic  50.5 us (13%)
  between operations  15.5 us (4%)
  starting transfers between devices  13.8 us (4%)
    psum x1, waiting for transfers between devices, combine_terms(): return lax.psum(terms, ('gx', 'gy')) * scale  137 us
    ppermute x2, waiting for transfers between devices, extended(): lax.ppermute(head, axis, [((i + 1) % count, i) for i in range(ends)])  48.2 us
    dot_general x27, matrix products, shards(): lax.dot_general(window, flat_grad, (((0,), (0,)), ((), ())), preferred_el...  28.6 us
    gather x43, local copies, waits for them, and re-layouts, assemble(): picked = jnp.take(source, chosen[:, offset], axis=1)  27.2 us
    select_n x45, other arithmetic, assemble(): picked = jnp.take(source, chosen[:, offset], axis=1)  19.6 us
    dot_general x27, matrix products, shards(): jnp.dot(window, kernel[offset], preferred_element_type=jnp.float32)  12.5 us
    dot_general x27, matrix products, shards(): lax.dot_general(back_window, kernel[offset], (((1,), (1,)), ((), ())), pr...  10.8 us
    ppermute x2, starting transfers between devices, extended(): lax.ppermute(tail, axis, [(i, (i + 1) % count) for i in range(ends)])  9.2 us
  transfers between devices with their start and end apart: 5, of which 2 were waited for; matrix products, arithmetic and copies ran while one was open for 16% of the time, Pallas kernels for 0%

commit v1 on v0

v1 whole, which is shorter than its diff:
```python
import functools

import jax
import jax.numpy as jnp
import numpy as np
from jax import lax
from jax.experimental import pallas as pl
from jax.experimental.pallas import tpu as pltpu
from jax.sharding import PartitionSpec as P

BOTH = ("gx", "gy")
C = 256
HALF = 128
K = 27
ROWS = 432
BLOCK = 48
BLOCKS = ROWS // BLOCK
CODED = ROWS + 16

VMEM = pl.BlockSpec(memory_space=pltpu.VMEM)
SMEM = pl.BlockSpec(memory_space=pltpu.SMEM)
PARAMS = pltpu.CompilerParams(vmem_limit_bytes=50 * 2**20)

FIRST, SECOND = 0, 1
GROUPS = (
    ((("x", FIRST), ("y", FIRST)), (("z", FIRST), ("x", SECOND)), (("y", SECOND), ("z", SECOND))),
    ((("x", SECOND), ("y", SECOND)), (("z", SECOND), ("x", FIRST)), (("y", FIRST), ("z", FIRST))),
)


def paired(v, pairing):
    return v ^ 1 if pairing == FIRST else 3 - v


def pair_bit(v, pairing):
    return (v ^ (v >> 1)) & 1 if pairing == FIRST else v >> 1


def number(at):
    return ((at["y"] * 4 + at["z"]) * 2 + at["core"]) * 4 + at["x"]


def places():
    for y in range(4):
        for z in range(4):
            for core in range(2):
                for x in range(4):
                    yield {"x": x, "y": y, "z": z, "core": core}


def partners(level, member):
    pairs = []
    for at in places():
        to = dict(at)
        for bit, (axis, pairing) in enumerate(GROUPS[at["core"]][level]):
            if member >> bit & 1:
                to[axis] = paired(to[axis], pairing)
        pairs.append((number(at), number(to)))
    return pairs


def other_core():
    return [(number(at), number({**at, "core": 1 - at["core"]})) for at in places()]


def rank_in(level, core, at):
    ranks = []
    for c in range(2):
        (a, pa), (b, pb) = GROUPS[c][level]
        ranks.append(pair_bit(at[a], pa) + 2 * pair_bit(at[b], pb))
    return jnp.where(core == 0, ranks[0], ranks[1])


def exchange(arrays, level):
    return [lax.ppermute(a, BOTH, partners(level, m + 1)) for m, a in enumerate(arrays)]


def call(kernel, outs, ins, *args, flops=0, scratch=()):
    size = sum(a.size * a.dtype.itemsize for a in args) + sum(o.size * o.dtype.itemsize for o in outs)
    return pl.pallas_call(
        kernel,
        out_shape=list(outs),
        in_specs=list(ins),
        out_specs=[VMEM] * len(outs),
        scratch_shapes=list(scratch),
        compiler_params=PARAMS,
        cost_estimate=pl.CostEstimate(flops=flops, bytes_accessed=size, transcendentals=0),
    )(*args)


def shape(dims, dtype):
    return jax.ShapeDtypeStruct(dims, dtype)


def put_coded(read, write):
    row = lax.broadcasted_iota(jnp.int32, (16, HALF), 0)
    exponents = jnp.zeros((16, HALF), jnp.float32)
    for b in range(BLOCKS):
        x = read(b)
        top = jnp.max(jnp.abs(x), axis=0, keepdims=True)
        e = jnp.ceil(jnp.log2(jnp.maximum(top, 2.0**-110)))
        q = jnp.clip(jnp.round(x * jnp.exp2(15.0 - e)), -32767.0, 32767.0)
        write(b * BLOCK, q.astype(jnp.int16))
        exponents = jnp.where(row == b, e, exponents)
    write(ROWS, exponents.astype(jnp.int16))


def scales_of(tile):
    return jnp.exp2(tile.astype(jnp.float32) - 15.0)


def block_of(ref, index, b):
    return ref[index, b * BLOCK : (b + 1) * BLOCK, :]


def coded_block(ref, index, scales, b):
    return block_of(ref, index, b).astype(jnp.float32) * scales[b : b + 1, :]


def coded_scales(ref, index):
    return scales_of(ref[index, ROWS:CODED, :])


def coded_writer(ref, index):
    def write(start, rows):
        ref[index, start : start + rows.shape[0], :] = rows

    return write


def pair_sum_kernel(rank, own, got, keep, first, second, third):
    g = rank[0]
    for m, out in enumerate((keep, first, second, third)):

        def chunk(c, _, m=m, out=out):
            at = (g ^ m) * 4 + c
            scales = coded_scales(got, at)

            def read(b):
                return block_of(own, at, b) + coded_block(got, at, scales, b)

            if m == 0:
                for b in range(BLOCKS):
                    out[c, b * BLOCK : (b + 1) * BLOCK, :] = read(b)
            else:
                put_coded(read, coded_writer(out, c))
            return 0

        lax.fori_loop(0, 4, chunk, 0)


def group_sum_kernel(rank, own, got_1, got_2, got_3, keep, first, second, third):
    g = rank[0]
    for m, out in enumerate((keep, first, second, third)):
        at = g ^ m
        scales = [coded_scales(r, at) for r in (got_1, got_2, got_3)]

        def read(b, at=at, scales=scales):
            x = block_of(own, at, b)
            for r, s in zip((got_1, got_2, got_3), scales):
                x = x + coded_block(r, at, s, b)
            return x

        if m == 0:
            for b in range(BLOCKS):
                out[0, b * BLOCK : (b + 1) * BLOCK, :] = read(b)
        else:
            put_coded(read, coded_writer(out, 0))


def last_group_kernel(own, got_1, got_2, got_3, out):
    scales = [coded_scales(r, 0) for r in (got_1, got_2, got_3)]

    def read(b):
        x = block_of(own, 0, b)
        for r, s in zip((got_1, got_2, got_3), scales):
            x = x + coded_block(r, 0, s, b)
        return x

    put_coded(read, coded_writer(out, 0))


def total_kernel(own, got_1, got_2, got_3, out):
    refs = (own, got_1, got_2, got_3)
    scales = [coded_scales(r, 0) for r in refs]

    def read(b):
        a = [coded_block(r, 0, s, b) for r, s in zip(refs, scales)]
        return (a[0] + a[1]) + (a[2] + a[3])

    put_coded(read, coded_writer(out, 0))


def finish_kernel(scale, where, a0, a1, a2, a3, b0, b1, b2, b3, out):
    core, inner = where[0], where[1]
    for side, refs in enumerate(((a0, a1, a2, a3), (b0, b1, b2, b3))):
        column = pl.multiple_of((core ^ side) * HALF, HALF)
        outer = where[2 + side]
        inner = where[4 + side]
        for m, ref in enumerate(refs):

            def chunk(c, _, ref=ref, m=m, outer=outer, inner=inner, column=column):
                scales = coded_scales(ref, c) * scale
                start = ((outer ^ m) * 4 + (inner ^ c)) * ROWS
                for b in range(BLOCKS):
                    rows = pl.ds(pl.multiple_of(start + b * BLOCK, 16), BLOCK)
                    out[rows, pl.ds(column, HALF)] = coded_block(ref, c, scales, b)
                return 0

            lax.fori_loop(0, 4, chunk, 0)


def widen(pick, cells, y_low, y_high, x_low, x_high, wide):
    for x in range(10):
        if x == 0:
            layer, side = x_low[...].reshape(160, C), 0
        elif x == 9:
            layer, side = x_high[...].reshape(160, C), 2
        else:
            layer = jnp.concatenate([y_low[x - 1], cells[x - 1].reshape(128, C), y_high[x - 1]], axis=0)
            side = 1
        moved = jnp.dot(pick[side], layer, preferred_element_type=jnp.float32).astype(jnp.bfloat16)
        for oz in range(3):
            wide[oz, x] = moved[160 * oz : 160 * (oz + 1)].reshape(10, 16, C)


def window_of(wide, ox, oy, oz, start, count):
    return wide[oz, pl.ds(ox + start, count), pl.ds(oy, 8)].reshape(count * 128, C)


def kernel_grad_kernel(pick, cells, y_low, y_high, x_low, x_high, grad, own, coded, wide, terms):
    widen(pick, cells, y_low, y_high, x_low, x_high, wide)
    g = grad[...].reshape(1024, C)

    def step(k, _):
        w = window_of(wide, k // 9, (k // 3) % 3, k % 3, 0, 8)
        t = lax.dot_general(w, g, (((0,), (0,)), ((), ())), preferred_element_type=jnp.float32)
        terms[pl.ds(pl.multiple_of(k * C, C), C), :] = t
        return 0

    lax.fori_loop(0, K, step, 0)

    def chunk(c, _):
        def read(b, lanes):
            return terms[pl.ds(pl.multiple_of(c * ROWS + b * BLOCK, 16), BLOCK), lanes]

        for b in range(BLOCKS):
            own[c, b * BLOCK : (b + 1) * BLOCK, :] = read(b, slice(0, HALF))
        put_coded(lambda b: read(b, slice(HALF, C)), coded_writer(coded, c))
        return 0

    lax.fori_loop(0, 16, chunk, 0)


def convolve_kernel(back, pick, cells, y_low, y_high, x_low, x_high, mask, kernel, out, wide, total):
    widen(pick, cells, y_low, y_high, x_low, x_high, wide)
    total[...] = jnp.zeros_like(total)

    def step(k, _):
        ox, oy, oz = k // 9, (k // 3) % 3, k % 3
        if back:
            ox, oy, oz = 2 - ox, 2 - oy, 2 - oz
        w = window_of(wide, ox, oy, oz, 0, 8)
        total[...] += lax.dot_general(
            w, kernel[k], (((1,), (1 if back else 0,)), ((), ())), preferred_element_type=jnp.float32
        )
        return 0

    lax.fori_loop(0, K, step, 0)
    out[...] = (total[...] * mask[...].reshape(1024, 1)).astype(jnp.bfloat16).reshape(8, 8, 16, C)


def picks(neighbors):
    n = neighbors.reshape(2, 3, 3, 3).transpose(1, 2, 0, 3)
    n = jnp.concatenate([n[:, :1]] + [n[:, 1:2]] * 8 + [n[:, 2:]], axis=1)
    z = np.arange(8)[None, :] + np.arange(3)[:, None] - 1
    beyond = (z > 7).astype(np.int32) - (z < 0).astype(np.int32)
    beyond = jnp.asarray(beyond)[None, :, None, None, :]
    n = n[:, None, :, :, None, :]
    slot = jnp.where(beyond < 0, n[..., 0], jnp.where(beyond > 0, n[..., 2], n[..., 1]))
    inside = jnp.asarray(z % 8)[None, :, None, None, :]
    target = slot * 8 + inside + jnp.arange(10, dtype=jnp.int32)[None, None, :, None, None] * 16
    target = jnp.where(slot >= 0, target, -1).reshape(3, 480, 1)
    return (target == jnp.arange(160, dtype=jnp.int32)).astype(jnp.bfloat16)


def shards(features, cotangent, kernel, occupancy, neighbors):
    gx, gy = lax.axis_index("gx"), lax.axis_index("gy")
    core = gx % 2
    at = {"x": gy, "y": gx // 8, "z": (gx // 2) % 4}
    scale = 1.0 / (512.0 * 256.0) ** 0.5

    def cells_of(a):
        return a.transpose(1, 2, 0, 3, 4).reshape(8, 8, 16, C)

    mask = occupancy.reshape(2, 8, 8, 8).transpose(1, 2, 0, 3).reshape(8, 8, 16, 1)
    mask_b = mask.astype(jnp.bfloat16)
    mask_f = mask.astype(jnp.float32)
    cells = cells_of(features) * mask_b
    grad = cells_of(cotangent) * mask_b
    both = jnp.stack([cells, grad])
    up_x = [(i, i + 1) for i in range(31)]
    down_x = [(i + 1, i) for i in range(31)]
    up_y = [(i, i + 1) for i in range(3)]
    down_y = [(i + 1, i) for i in range(3)]
    y_low = lax.ppermute(both[:, :, 7], "gy", up_y)
    y_high = lax.ppermute(both[:, :, 0], "gy", down_y)

    def layer(x):
        return jnp.concatenate([y_low[:, x, None], both[:, x], y_high[:, x, None]], axis=1)

    x_low = lax.ppermute(layer(7), "gx", up_x)
    x_high = lax.ppermute(layer(0), "gx", down_x)
    pick = picks(neighbors)

    grad_halves = jnp.where(core == 0, grad, jnp.concatenate([grad[..., HALF:], grad[..., :HALF]], axis=-1))
    wide = pltpu.VMEM((3, 10, 10, 16, C), jnp.bfloat16)
    flops = 2 * K * 1024 * C * C
    own, coded = call(
        kernel_grad_kernel,
        [shape((16, ROWS, HALF), jnp.float32), shape((16, CODED, HALF), jnp.int16)],
        [VMEM] * 7,
        pick, cells, y_low[0], y_high[0], x_low[0], x_high[0], grad_halves,
        flops=flops,
        scratch=[wide, pltpu.VMEM((K * C, C), jnp.float32)],
    )

    def convolve(back, a, index):
        return call(
            functools.partial(convolve_kernel, back),
            [shape((8, 8, 16, C), jnp.bfloat16)],
            [VMEM] * 8,
            pick, a, y_low[index], y_high[index], x_low[index], x_high[index], mask_f, kernel,
            flops=flops,
            scratch=[wide, pltpu.VMEM((1024, C), jnp.float32)],
        )[0]

    forward = convolve(False, cells, 0)
    backward = convolve(True, grad, 1)

    got = lax.ppermute(coded, BOTH, other_core())
    outer, inner = rank_in(0, core, at), rank_in(1, core, at)
    coded_4 = shape((4, CODED, HALF), jnp.int16)
    coded_1 = shape((1, CODED, HALF), jnp.int16)
    keep, *sent = call(
        pair_sum_kernel,
        [shape((4, ROWS, HALF), jnp.float32)] + [coded_4] * 3,
        [SMEM, VMEM, VMEM],
        outer.reshape(1), own, got,
    )
    keep, *sent = call(
        group_sum_kernel,
        [shape((1, ROWS, HALF), jnp.float32)] + [coded_1] * 3,
        [SMEM] + [VMEM] * 4,
        inner.reshape(1), keep, *exchange(sent, 0),
    )
    (part,) = call(last_group_kernel, [coded_1], [VMEM] * 4, keep, *exchange(sent, 1))
    (whole,) = call(total_kernel, [coded_1], [VMEM] * 4, part, *exchange([part] * 3, 2))
    four = jnp.concatenate([whole] + exchange([whole] * 3, 1))
    sets = [four] + exchange([four] * 3, 0)
    others = [lax.ppermute(s, BOTH, other_core()) for s in sets]
    where = jnp.stack(
        [core, inner, outer, rank_in(0, 1 - core, at), inner, rank_in(1, 1 - core, at)]
    ).astype(jnp.int32)
    (kernel_grad,) = call(
        functools.partial(finish_kernel, scale),
        [shape((K * C, C), jnp.float32)],
        [SMEM] + [VMEM] * 8,
        where, *sets, *others,
    )

    def bricks_of(a):
        return a.reshape(8, 8, 2, 8, C).transpose(2, 0, 1, 3, 4)

    return bricks_of(forward), bricks_of(backward), kernel_grad.reshape(K, C, C)


def solution(mesh):
    placed = (
        P(BOTH, None, None, None, None),
        P(BOTH, None, None, None, None),
        P(),
        P(BOTH, None),
        P(BOTH, None),
    )
    return jax.shard_map(
        shards,
        mesh=mesh,
        in_specs=placed,
        out_specs=(P(BOTH, None, None, None, None), P(BOTH, None, None, None, None), P()),
        check_vma=False,
    )
```

time: 379 us -> 145 us (0.38)
  waiting for transfers between devices: 185 us -> 29.7 us
  matrix products: 51.9 us -> 0 us
  Pallas kernels: 0 us -> 48.4 us
  other arithmetic: 50.5 us -> 4.2 us
  local copies, waits for them, and re-layouts: 59.9 us -> 19.2 us
  starting transfers between devices: 13.8 us -> 41.8 us
  between operations: 15.5 us -> 1.11 us
    psum x1 -> x0, waiting for transfers between devices: 137 us -> none  [combine_terms(): return lax.psum(terms, ('gx', 'gy')) * scale]
    dot_general x81 -> x0, matrix products: 51.9 us -> none  [the longest x27 28.6 us: shards(): lax.dot_general(window, flat_grad, (((0,), (0,)), ((), ())), preferred_el...]
    pallas_call x0 -> x8, Pallas kernels: none -> 48.4 us  [call(): pl.pallas_call(kernel, out_shape=list(outs), in_specs=list(ins), out_spec...]
    ppermute x4 -> x24, starting transfers between devices: 13.8 us -> 41.8 us  [the longest x15 23.7 us: exchange(): lax.ppermute(a, BOTH, partners(level, m + 1))]
    gather x43 -> x0, local copies, waits for them, and re-layouts: 27.2 us -> none  [assemble(): picked = jnp.take(source, chosen[:, offset], axis=1)]
    select_n x46 -> x2, other arithmetic: 19.6 us -> 0.15 us  [the longest x1 0.14 us: shards(): jnp.where(core == 0, grad, jnp.concatenate([grad[..., HALF:], grad[..., :...]
    ppermute x4 -> x24, waiting for transfers between devices: 48.2 us -> 29.7 us  [the longest x15 21.7 us: exchange(): lax.ppermute(a, BOTH, partners(level, m + 1))]
    slice x16 -> x8, local copies, waits for them, and re-layouts: 19.8 us -> 3.76 us  [the longest x5 3.62 us: picks(): n = jnp.concatenate([n[:, :1]] + [n[:, 1:2]] * 8 + [n[:, 2:]], axis=1)]
  transfers between devices with their start and end apart: 5 -> 24, of which waited for: 2 -> 13; matrix products, arithmetic and copies ran while one was open for 16% -> 9% of each run, Pallas kernels for 0% -> 16%
where the time goes in v1:
time: 145 us; the launch traced here: 144 us
  Pallas kernels  48.4 us (33%)
  starting transfers between devices  41.8 us (29%)
  waiting for transfers between devices  29.7 us (20%)
  local copies, waits for them, and re-layouts  19.2 us (13%)
  other arithmetic  4.2 us (3%)
    pallas_call x8, Pallas kernels, call(): pl.pallas_call(kernel, out_shape=list(outs), in_specs=list(ins), out_spec...  48.4 us
    ppermute x15, starting transfers between devices, exchange(): lax.ppermute(a, BOTH, partners(level, m + 1))  23.7 us
    ppermute x15, waiting for transfers between devices, exchange(): lax.ppermute(a, BOTH, partners(level, m + 1))  21.7 us
    unnamed x41, local copies, waits for them, and re-layouts  6.69 us
    ppermute x4, starting transfers between devices, shards(): others = [lax.ppermute(s, BOTH, other_core()) for s in sets]  6.48 us
    ppermute x1, starting transfers between devices, shards(): x_low = lax.ppermute(layer(7), 'gx', up_x)  4.39 us
    ppermute x1, waiting for transfers between devices, shards(): x_high = lax.ppermute(layer(0), 'gx', down_x)  4.01 us
    ppermute x1, waiting for transfers between devices, shards(): got = lax.ppermute(coded, BOTH, other_core())  3.95 us
  transfers between devices with their start and end apart: 24, of which 13 were waited for; matrix products, arithmetic and copies ran while one was open for 9% of the time, Pallas kernels for 16%

profile of v1, /device:TPU:1, one launch (start us, length us, event | category | flops | bytes accessed | tf_op | source)
XLA Modules:
  0.0 144.4 jit_solution(6377099339849092441)
XLA Ops:
  0.6 1.4 fusion.5
  2.3 1.4 bitcast_multiply_fusion.2
  4.4 3.9 %collective-permute-start = (bf16[2,8,16,256]{3,2,0,1:T(8,128)(2,1)}, bf16[2,8,16,256]{3,2,0,1:T(8,128)(2,1)S(1)}, u32[]{:S(2)}, u32[]{:S(2)}) collective-permute-start(bf16[2,8,16,256]{3,2,0,1:T(8,128)(2,1)} %bitcast.73), channel_id=1, source_target_pairs={{0,1},{1,2},{2,3},{4,5},{5,6},{6,7},{8,9},{9,10},{10,11},{12,13},{... | collective-permute-start | bytes 393224 | tf_op jit(solution)/shard_map/ppermute | solution.py:306
  8.4 1.3 collective-permute-start.1
  11.9 0.8 copy.57
  12.7 0.8 copy.51
  13.5 0.8 copy.50
  16.4 0.8 add.61
  17.2 0.7 add.57
  18.4 0.7 broadcast_in_dim.83
  19.2 0.7 broadcast_in_dim.86
  21.1 4.4 %collective-permute-start.2 = (bf16[2,10,16,256]{3,2,0,1:T(8,128)(2,1)S(1)}, bf16[2,10,16,256]{3,2,0,1:T(8,128)(2,1)S(1)}, u32[]{:S(2)}, u32[]{:S(2)}) collective-permute-start(bf16[2,10,16,256]{3,2,0,1:T(8,128)(2,1)S(1)} %pad_maximum_fusion), channel_id=1, source_target_pairs={{0,4},{4,8},{8,12},{12,16},{16,20},{20,24},{24,28},{28,32},{32,36}... | collective-permute-start | bytes 491528 | tf_op jit(solution)/shard_map/ppermute | solution.py:312
  25.5 1.9 %collective-permute-start.3 = (bf16[2,10,16,256]{3,2,1,0:T(8,128)(2,1)S(1)}, bf16[2,10,16,256]{3,2,1,0:T(8,128)(2,1)S(1)}, u32[]{:S(2)}, u32[]{:S(2)}) collective-permute-start(bf16[2,10,16,256]{3,2,1,0:T(8,128)(2,1)S(1)} %pad_maximum_fusion.1), channel_id=1, source_target_pairs={{4,0},{8,4},{12,8},{16,12},{20,16},{24,20},{28,24},{32,28},{36,32}... | collective-permute-start | bytes 491528 | tf_op jit(solution)/shard_map/ppermute | solution.py:313
  28.1 4.0 %collective-permute-done.3 = bf16[2,10,16,256]{3,2,1,0:T(8,128)(2,1)S(1)} collective-permute-done((bf16[2,10,16,256]{3,2,1,0:T(8,128)(2,1)S(1)}, bf16[2,10,16,256]{3,2,1,0:T(8,128)(2,1)S(1)}, u32[]{:S(2)}, u32[]{:S(2)}) %collective-permute-start.3) | collective-permute-done | bytes 163872 | tf_op jit(solution)/shard_map/ppermute | solution.py:313
  32.8 14.7 %shard_map.96 = (f32[16,432,128]{2,1,0:T(8,128)}, s16[16,448,128]{2,1,0:T(8,128)(2,1)}) custom-call(bf16[3,480,160]{2,1,0:T(8,128)(2,1)S(1)} %fusion.pick, bf16[8,8,16,256]{3,2,1,0:T(8,128)(2,1)S(1)} %get-tuple-element.42.cells, bf16[8,16,256]{2,1,0:T(8,128)(2,1)S(1)} %get-tuple-element.36.y_low, bf16[8,16,256]{2,1,0:T(8,128)(2,1)S(1)} %get-tuple-element.34.y_high, ...), custom_call_target="tpu_custom_call" | custom-call | flops 3623878656 | bytes 7178240 | tf_op jit(solution)/shard_map/pallas_call | solution.py:80
  47.6 4.0 %collective-permute-done.4.got = s16[16,448,128]{2,1,0:T(8,128)(2,1)S(1)} collective-permute-done((s16[16,448,128]{2,1,0:T(8,128)(2,1)}, s16[16,448,128]{2,1,0:T(8,128)(2,1)S(1)}, u32[]{:S(2)}, u32[]{:S(2)}) %collective-permute-start.4) | collective-permute-done | bytes 1835040 | tf_op jit(solution)/shard_map/ppermute | solution.py:341
  51.6 4.3 %shard_map.97 = (f32[4,432,128]{2,1,0:T(8,128)S(1)}, s16[4,448,128]{2,1,0:T(8,128)(2,1)}, s16[4,448,128]{2,1,0:T(8,128)(2,1)}, s16[4,448,128]{2,1,0:T(8,128)(2,1)}) custom-call(s32[1]{0:T(128)} %bitcast.33.rank, f32[16,432,128]{2,1,0:T(8,128)} %get-tuple-element.13.own, s16[16,448,128]{2,1,0:T(8,128)(2,1)S(1)} %collective-permute-done.4.got), custom_call_target="tpu_custom_call" | custom-call | bytes 7634948 | tf_op jit(solution)/shard_map/pallas_call | solution.py:80
  55.9 0.9 copy-done.1
  56.8 3.6 %collective-permute-start.5 = (s16[4,448,128]{2,1,0:T(8,128)(2,1)}, s16[4,448,128]{2,1,0:T(8,128)(2,1)S(1)}, u32[]{:S(2)}, u32[]{:S(2)}) collective-permute-start(s16[4,448,128]{2,1,0:T(8,128)(2,1)} %get-tuple-element.16), channel_id=1, source_target_pairs={{0,1},{1,0},{2,3},{3,2},{4,7},{5,6},{6,5},{7,4},{8,9},{9,8},{10,11... | collective-permute-start | bytes 1376264 | tf_op jit(solution)/shard_map/ppermute | solution.py:75
  60.4 2.8 %collective-permute-start.6 = (s16[4,448,128]{2,1,0:T(8,128)(2,1)}, s16[4,448,128]{2,1,0:T(8,128)(2,1)S(1)}, u32[]{:S(2)}, u32[]{:S(2)}) collective-permute-start(s16[4,448,128]{2,1,0:T(8,128)(2,1)} %get-tuple-element.17), channel_id=1, source_target_pairs={{0,32},{1,33},{2,34},{3,35},{4,100},{5,101},{6,102},{7,103},{8,40}... | collective-permute-start | bytes 1376264 | tf_op jit(solution)/shard_map/ppermute | solution.py:75
  63.2 3.3 %collective-permute-done.5.got_1 = s16[4,448,128]{2,1,0:T(8,128)(2,1)S(1)} collective-permute-done((s16[4,448,128]{2,1,0:T(8,128)(2,1)}, s16[4,448,128]{2,1,0:T(8,128)(2,1)S(1)}, u32[]{:S(2)}, u32[]{:S(2)}) %collective-permute-start.5) | collective-permute-done | bytes 458784 | tf_op jit(solution)/shard_map/ppermute | solution.py:75
  66.5 7.7 %collective-permute-done.6.got_2 = s16[4,448,128]{2,1,0:T(8,128)(2,1)S(1)} collective-permute-done((s16[4,448,128]{2,1,0:T(8,128)(2,1)}, s16[4,448,128]{2,1,0:T(8,128)(2,1)S(1)}, u32[]{:S(2)}, u32[]{:S(2)}) %collective-permute-start.6) | collective-permute-done | bytes 458784 | tf_op jit(solution)/shard_map/ppermute | solution.py:75
  74.2 1.2 copy-done.2
  75.9 4.1 %collective-permute-start.8 = (s16[1,448,128]{2,1,0:T(8,128)(2,1)S(1)}, s16[1,448,128]{2,1,0:T(8,128)(2,1)S(1)}, u32[]{:S(2)}, u32[]{:S(2)}) collective-permute-start(s16[1,448,128]{2,1,0:T(8,128)(2,1)S(1)} %get-tuple-element.20), channel_id=1, source_target_pairs={{0,8},{1,9},{2,10},{3,11},{4,28},{5,29},{6,30},{7,31},{8,0},{9,1},... | collective-permute-start | bytes 344072 | tf_op jit(solution)/shard_map/ppermute | solution.py:75
  80.0 1.3 collective-permute-start.10
  81.3 1.2 collective-permute-done.8.got_1
  82.5 1.2 collective-permute-done.9.got_2
  83.7 2.1 %collective-permute-done.10.got_3 = s16[1,448,128]{2,1,0:T(8,128)(2,1)S(1)} collective-permute-done((s16[1,448,128]{2,1,0:T(8,128)(2,1)S(1)}, s16[1,448,128]{2,1,0:T(8,128)(2,1)S(1)}, u32[]{:S(2)}, u32[]{:S(2)}) %collective-permute-start.10) | collective-permute-done | bytes 114720 | tf_op jit(solution)/shard_map/ppermute | solution.py:75
  86.0 1.6 %collective-permute-start.12 = (s16[1,448,128]{2,1,0:T(8,128)(2,1)S(1)}, s16[1,448,128]{2,1,0:T(8,128)(2,1)S(1)}, u32[]{:S(2)}, u32[]{:S(2)}) collective-permute-start(s16[1,448,128]{2,1,0:T(8,128)(2,1)S(1)} %shard_map.99.own), channel_id=1, source_target_pairs={{0,24},{1,25},{2,26},{3,27},{4,12},{5,13},{6,14},{7,15},{8,16},{9,... | collective-permute-start | bytes 344072 | tf_op jit(solution)/shard_map/ppermute | solution.py:75
  87.6 1.1 collective-permute-start.11
  88.7 2.0 %collective-permute-done.13.got_3 = s16[1,448,128]{2,1,0:T(8,128)(2,1)S(1)} collective-permute-done((s16[1,448,128]{2,1,0:T(8,128)(2,1)S(1)}, s16[1,448,128]{2,1,0:T(8,128)(2,1)S(1)}, u32[]{:S(2)}, u32[]{:S(2)}) %collective-permute-start.13) | collective-permute-done | bytes 114720 | tf_op jit(solution)/shard_map/ppermute | solution.py:75
  91.4 1.1 collective-permute-start.16
  92.5 1.7 %collective-permute-start.15 = (s16[1,448,128]{2,1,0:T(8,128)(2,1)S(1)}, s16[1,448,128]{2,1,0:T(8,128)(2,1)S(1)}, u32[]{:S(2)}, u32[]{:S(2)}) collective-permute-start(s16[1,448,128]{2,1,0:T(8,128)(2,1)S(1)} %shard_map.100), channel_id=1, source_target_pairs={{0,3},{1,2},{2,1},{3,0},{4,5},{5,4},{6,7},{7,6},{8,11},{9,10},{10,... | collective-permute-start | bytes 344072 | tf_op jit(solution)/shard_map/ppermute | solution.py:75
  94.3 1.2 collective-permute-start.14
  95.4 1.9 %collective-permute-done.16 = s16[1,448,128]{2,1,0:T(8,128)(2,1)S(1)} collective-permute-done((s16[1,448,128]{2,1,0:T(8,128)(2,1)S(1)}, s16[1,448,128]{2,1,0:T(8,128)(2,1)S(1)}, u32[]{:S(2)}, u32[]{:S(2)}) %collective-permute-start.16) | collective-permute-done | bytes 114720 | tf_op jit(solution)/shard_map/ppermute | solution.py:75
  97.7 1.4 %collective-permute-done.14 = s16[1,448,128]{2,1,0:T(8,128)(2,1)S(1)} collective-permute-done((s16[1,448,128]{2,1,0:T(8,128)(2,1)S(1)}, s16[1,448,128]{2,1,0:T(8,128)(2,1)S(1)}, u32[]{:S(2)}, u32[]{:S(2)}) %collective-permute-start.14) | collective-permute-done | bytes 114720 | tf_op jit(solution)/shard_map/ppermute | solution.py:75
  99.1 2.4 %collective-permute-start.19 = (s16[4,448,128]{2,1,0:T(8,128)(2,1)S(1)}, s16[4,448,128]{2,1,0:T(8,128)(2,1)}, u32[]{:S(2)}, u32[]{:S(2)}) collective-permute-start(s16[4,448,128]{2,1,0:T(8,128)(2,1)S(1)} %pad_add_fusion.a0), channel_id=1, source_target_pairs={{0,33},{1,32},{2,35},{3,34},{4,103},{5,102},{6,101},{7,100},{8,41}... | collective-permute-start | bytes 1376264 | tf_op jit(solution)/shard_map/ppermute | solution.py:75
  101.6 1.9 %collective-permute-start.18 = (s16[4,448,128]{2,1,0:T(8,128)(2,1)S(1)}, s16[4,448,128]{2,1,0:T(8,128)(2,1)}, u32[]{:S(2)}, u32[]{:S(2)}) collective-permute-start(s16[4,448,128]{2,1,0:T(8,128)(2,1)S(1)} %pad_add_fusion.a0), channel_id=1, source_target_pairs={{0,32},{1,33},{2,34},{3,35},{4,100},{5,101},{6,102},{7,103},{8,40}... | collective-permute-start | bytes 1376264 | tf_op jit(solution)/shard_map/ppermute | solution.py:75
  103.5 0.8 collective-permute-start.17
  104.8 0.9 copy-done.7
  105.7 0.9 copy-done.9
  106.5 0.8 copy-done.12
  107.4 0.8 copy-done.14
  108.2 11.1 %shard_map.94 = bf16[8,8,16,256]{3,2,1,0:T(8,128)(2,1)S(1)} custom-call(bf16[3,480,160]{2,1,0:T(8,128)(2,1)S(1)} %copy-done.4, bf16[8,8,16,256]{3,2,1,0:T(8,128)(2,1)S(1)} %get-tuple-element.42.cells, bf16[8,16,256]{2,1,0:T(8,128)(2,1)S(1)} %copy-done.12, bf16[8,16,256]{2,1,0:T(8,128)(2,1)S(1)} %copy-done.14, bf16[10,16,256]{2,1,0:T(8,128)(2,1)S(1)} %copy-done.7, ...), custom_call_target="tpu_custom_call" | custom-call | flops 3623878656 | bytes 5347328 | tf_op jit(solution)/shard_map/pallas_call | solution.py:80
  119.4 5.9 %collective-permute-start.20 = (s16[4,448,128]{2,1,0:T(8,128)(2,1)S(1)}, s16[4,448,128]{2,1,0:T(8,128)(2,1)S(1)}, u32[]{:S(2)}, u32[]{:S(2)}) collective-permute-start(s16[4,448,128]{2,1,0:T(8,128)(2,1)S(1)} %pad_add_fusion.a0), channel_id=1, source_target_pairs={{0,4},{1,5},{2,6},{3,7},{4,0},{5,1},{6,2},{7,3},{8,12},{9,13},{10,... | collective-permute-start | bytes 1376264 | tf_op jit(solution)/shard_map/ppermute | solution.py:361
  125.9 12.0 %shard_map.95 = bf16[8,8,16,256]{3,2,1,0:T(8,128)(2,1)S(1)} custom-call(bf16[3,480,160]{2,1,0:T(8,128)(2,1)S(1)} %copy-done.4, bf16[8,8,16,256]{3,2,1,0:T(8,128)(2,1)S(1)} %get-tuple-element.41.cells, bf16[8,16,256]{2,1,0:T(8,128)(2,1)S(1)} %get-tuple-element.35.y_low, bf16[8,16,256]{2,1,0:T(8,128)(2,1)S(1)} %copy-done.10, ...), custom_call_target="tpu_custom_call" | custom-call | flops 3623878656 | bytes 5347328 | tf_op jit(solution)/shard_map/pallas_call | solution.py:80
  137.9 1.1 copy_bitcast_fusion
  139.0 5.4 %shard_map.101 = f32[6912,256]{1,0:T(8,128)} custom-call(s32[6]{0:T(128)S(1)} %stack.30.where, s16[4,448,128]{2,1,0:T(8,128)(2,1)S(1)} %pad_add_fusion.a0, s16[4,448,128]{2,1,0:T(8,128)(2,1)} %collective-permute-done.17.a1, s16[4,448,128]{2,1,0:T(8,128)(2,1)} %collective-permute-done.18.a2, s16[4,448,128]{2,1,0:T(8,128)(2,1)} %collective-permute-done.19.a3, ...), custom_call_target="tpu_custom_call" | custom-call | bytes 10747928 | tf_op jit(solution)/shard_map/pallas_call | solution.py:80
  (102 shorter events, 11.2 us)
Async XLA Ops:
  0.6 1.6 %copy-start = (bf16[2,8,8,8,256]{4,3,2,1,0:T(8,128)(2,1)S(1)}, bf16[2,8,8,8,256]{4,3,2,1,0:T(8,128)(2,1)}, u32[]{:S(2)}) copy-start(bf16[2,8,8,8,256]{4,3,2,1,0:T(8,128)(2,1)} %param.7) | copy-start | bytes 1572868
  2.3 8.0 %copy-start.19 = (s32[2,27]{1,0:T(2,128)S(1)}, s32[2,27]{1,0:T(2,128)}, u32[]{:S(2)}) copy-start(s32[2,27]{1,0:T(2,128)} %param.11) | copy-start | bytes 652
  2.3 9.3 %copy-start.15 = (bf16[2,8,8,8,256]{4,3,2,1,0:T(8,128)(2,1)S(1)}, bf16[2,8,8,8,256]{4,3,2,1,0:T(8,128)(2,1)}, u32[]{:S(2)}) copy-start(bf16[2,8,8,8,256]{4,3,2,1,0:T(8,128)(2,1)} %param.8) | copy-start | bytes 1572868
  4.4 16.6 %collective-permute-start = (bf16[2,8,16,256]{3,2,0,1:T(8,128)(2,1)}, bf16[2,8,16,256]{3,2,0,1:T(8,128)(2,1)S(1)}, u32[]{:S(2)}, u32[]{:S(2)}) collective-permute-start(bf16[2,8,16,256]{3,2,0,1:T(8,128)(2,1)} %bitcast.73), channel_id=1, source_target_pairs={{0,1},{1,2},{2,3},{4,5},{5,6},{6,7},{8,9},{9,10},{10,11},{12,13},{... | collective-permute-start | bytes 393224 | tf_op jit(solution)/shard_map/ppermute | solution.py:306
  8.4 12.7 %collective-permute-start.1 = (bf16[2,8,16,256]{3,2,1,0:T(8,128)(2,1)S(1)}, bf16[2,8,16,256]{3,2,1,0:T(8,128)(2,1)S(1)}, u32[]{:S(2)}, u32[]{:S(2)}) collective-permute-start(bf16[2,8,16,256]{3,2,1,0:T(8,128)(2,1)S(1)} %get-tuple-element.25), channel_id=1, source_target_pairs={{1,0},{2,1},{3,2},{5,4},{6,5},{7,6},{9,8},{10,9},{11,10},{13,12},{... | collective-permute-start | bytes 393224 | tf_op jit(solution)/shard_map/ppermute | solution.py:307
  20.0 0.7 copy-start.16
  20.0 0.7 copy-start.17
  21.0 26.5 %copy-start.3 = (bf16[3,480,160]{2,1,0:T(8,128)(2,1)}, bf16[3,480,160]{2,1,0:T(8,128)(2,1)S(1)}, u32[]{:S(2)}) copy-start(bf16[3,480,160]{2,1,0:T(8,128)(2,1)S(1)} %fusion.pick) | copy-start | bytes 1382404
  21.1 7.0 %collective-permute-start.2 = (bf16[2,10,16,256]{3,2,0,1:T(8,128)(2,1)S(1)}, bf16[2,10,16,256]{3,2,0,1:T(8,128)(2,1)S(1)}, u32[]{:S(2)}, u32[]{:S(2)}) collective-permute-start(bf16[2,10,16,256]{3,2,0,1:T(8,128)(2,1)S(1)} %pad_maximum_fusion), channel_id=1, source_target_pairs={{0,4},{4,8},{8,12},{12,16},{16,20},{20,24},{24,28},{28,32},{32,36}... | collective-permute-start | bytes 491528 | tf_op jit(solution)/shard_map/ppermute | solution.py:312
  25.5 6.6 %collective-permute-start.3 = (bf16[2,10,16,256]{3,2,1,0:T(8,128)(2,1)S(1)}, bf16[2,10,16,256]{3,2,1,0:T(8,128)(2,1)S(1)}, u32[]{:S(2)}, u32[]{:S(2)}) collective-permute-start(bf16[2,10,16,256]{3,2,1,0:T(8,128)(2,1)S(1)} %pad_maximum_fusion.1), channel_id=1, source_target_pairs={{4,0},{8,4},{12,8},{16,12},{20,16},{24,20},{28,24},{32,28},{36,32}... | collective-permute-start | bytes 491528 | tf_op jit(solution)/shard_map/ppermute | solution.py:313
  27.4 20.0 %copy-start.11 = (bf16[8,16,256]{2,1,0:T(8,128)(2,1)}, bf16[8,16,256]{2,1,0:T(8,128)(2,1)S(1)}, u32[]{:S(2)}) copy-start(bf16[8,16,256]{2,1,0:T(8,128)(2,1)S(1)} %get-tuple-element.36.y_low) | copy-start | bytes 196612
  28.1 19.4 %copy-start.13 = (bf16[8,16,256]{2,1,0:T(8,128)(2,1)}, bf16[8,16,256]{2,1,0:T(8,128)(2,1)S(1)}, u32[]{:S(2)}) copy-start(bf16[8,16,256]{2,1,0:T(8,128)(2,1)S(1)} %get-tuple-element.34.y_high) | copy-start | bytes 196612
  28.1 19.4 %copy-start.6 = (bf16[10,16,256]{2,1,0:T(8,128)(2,1)}, bf16[10,16,256]{2,1,0:T(8,128)(2,1)S(1)}, u32[]{:S(2)}) copy-start(bf16[10,16,256]{2,1,0:T(8,128)(2,1)S(1)} %get-tuple-element.32.x_low) | copy-start | bytes 245764
  32.8 14.7 %copy-start.8 = (bf16[10,16,256]{2,1,0:T(8,128)(2,1)}, bf16[10,16,256]{2,1,0:T(8,128)(2,1)S(1)}, u32[]{:S(2)}) copy-start(bf16[10,16,256]{2,1,0:T(8,128)(2,1)S(1)} %get-tuple-element.30.x_high) | copy-start | bytes 245764
  47.5 4.1 %collective-permute-start.4 = (s16[16,448,128]{2,1,0:T(8,128)(2,1)}, s16[16,448,128]{2,1,0:T(8,128)(2,1)S(1)}, u32[]{:S(2)}, u32[]{:S(2)}) collective-permute-start(s16[16,448,128]{2,1,0:T(8,128)(2,1)} %get-tuple-element.14), channel_id=1, source_target_pairs={{0,4},{1,5},{2,6},{3,7},{4,0},{5,1},{6,2},{7,3},{8,12},{9,13},{10,... | collective-permute-start | bytes 5505032 | tf_op jit(solution)/shard_map/ppermute | solution.py:341
  55.9 0.9 copy-start.1
  56.8 9.7 %collective-permute-start.5 = (s16[4,448,128]{2,1,0:T(8,128)(2,1)}, s16[4,448,128]{2,1,0:T(8,128)(2,1)S(1)}, u32[]{:S(2)}, u32[]{:S(2)}) collective-permute-start(s16[4,448,128]{2,1,0:T(8,128)(2,1)} %get-tuple-element.16), channel_id=1, source_target_pairs={{0,1},{1,0},{2,3},{3,2},{4,7},{5,6},{6,5},{7,4},{8,9},{9,8},{10,11... | collective-permute-start | bytes 1376264 | tf_op jit(solution)/shard_map/ppermute | solution.py:75
  60.4 13.8 %collective-permute-start.6 = (s16[4,448,128]{2,1,0:T(8,128)(2,1)}, s16[4,448,128]{2,1,0:T(8,128)(2,1)S(1)}, u32[]{:S(2)}, u32[]{:S(2)}) collective-permute-start(s16[4,448,128]{2,1,0:T(8,128)(2,1)} %get-tuple-element.17), channel_id=1, source_target_pairs={{0,32},{1,33},{2,34},{3,35},{4,100},{5,101},{6,102},{7,103},{8,40}... | collective-permute-start | bytes 1376264 | tf_op jit(solution)/shard_map/ppermute | solution.py:75
  63.2 11.0 %collective-permute-start.7 = (s16[4,448,128]{2,1,0:T(8,128)(2,1)}, s16[4,448,128]{2,1,0:T(8,128)(2,1)S(1)}, u32[]{:S(2)}, u32[]{:S(2)}) collective-permute-start(s16[4,448,128]{2,1,0:T(8,128)(2,1)} %get-tuple-element.18), channel_id=1, source_target_pairs={{0,33},{1,32},{2,35},{3,34},{4,103},{5,102},{6,101},{7,100},{8,41}... | collective-permute-start | bytes 1376264 | tf_op jit(solution)/shard_map/ppermute | solution.py:75
  74.2 1.2 copy-start.2
  75.4 28.9 %copy-start.18 = (f32[2,512]{1,0:T(2,128)S(1)}, f32[2,512]{1,0:T(2,128)}, u32[]{:S(2)}) copy-start(f32[2,512]{1,0:T(2,128)} %get-tuple-element.50) | copy-start | bytes 12292
  75.9 28.9 %copy-start.4 = (bf16[3,480,160]{2,1,0:T(8,128)(2,1)S(1)}, bf16[3,480,160]{2,1,0:T(8,128)(2,1)}, u32[]{:S(2)}) copy-start(bf16[3,480,160]{2,1,0:T(8,128)(2,1)} %copy-done.3) | copy-start | bytes 1382404
  75.9 6.6 %collective-permute-start.8 = (s16[1,448,128]{2,1,0:T(8,128)(2,1)S(1)}, s16[1,448,128]{2,1,0:T(8,128)(2,1)S(1)}, u32[]{:S(2)}, u32[]{:S(2)}) collective-permute-start(s16[1,448,128]{2,1,0:T(8,128)(2,1)S(1)} %get-tuple-element.20), channel_id=1, source_target_pairs={{0,8},{1,9},{2,10},{3,11},{4,28},{5,29},{6,30},{7,31},{8,0},{9,1},... | collective-permute-start | bytes 344072 | tf_op jit(solution)/shard_map/ppermute | solution.py:75
  80.0 3.6 %collective-permute-start.9 = (s16[1,448,128]{2,1,0:T(8,128)(2,1)S(1)}, s16[1,448,128]{2,1,0:T(8,128)(2,1)S(1)}, u32[]{:S(2)}, u32[]{:S(2)}) collective-permute-start(s16[1,448,128]{2,1,0:T(8,128)(2,1)S(1)} %get-tuple-element.21), channel_id=1, source_target_pairs={{0,3},{1,2},{2,1},{3,0},{4,5},{5,4},{6,7},{7,6},{8,11},{9,10},{10,... | collective-permute-start | bytes 344072 | tf_op jit(solution)/shard_map/ppermute | solution.py:75
  80.0 5.8 %collective-permute-start.10 = (s16[1,448,128]{2,1,0:T(8,128)(2,1)S(1)}, s16[1,448,128]{2,1,0:T(8,128)(2,1)S(1)}, u32[]{:S(2)}, u32[]{:S(2)}) collective-permute-start(s16[1,448,128]{2,1,0:T(8,128)(2,1)S(1)} %get-tuple-element.22), channel_id=1, source_target_pairs={{0,11},{1,10},{2,9},{3,8},{4,29},{5,28},{6,31},{7,30},{8,3},{9,2},... | collective-permute-start | bytes 344072 | tf_op jit(solution)/shard_map/ppermute | solution.py:75
  86.0 4.7 %collective-permute-start.13 = (s16[1,448,128]{2,1,0:T(8,128)(2,1)S(1)}, s16[1,448,128]{2,1,0:T(8,128)(2,1)S(1)}, u32[]{:S(2)}, u32[]{:S(2)}) collective-permute-start(s16[1,448,128]{2,1,0:T(8,128)(2,1)S(1)} %shard_map.99.own), channel_id=1, source_target_pairs={{0,120},{1,121},{2,122},{3,123},{4,44},{5,45},{6,46},{7,47},{8,112... | collective-permute-start | bytes 344072 | tf_op jit(solution)/shard_map/ppermute | solution.py:75
  86.0 5.0 %collective-permute-start.12 = (s16[1,448,128]{2,1,0:T(8,128)(2,1)S(1)}, s16[1,448,128]{2,1,0:T(8,128)(2,1)S(1)}, u32[]{:S(2)}, u32[]{:S(2)}) collective-permute-start(s16[1,448,128]{2,1,0:T(8,128)(2,1)S(1)} %shard_map.99.own), channel_id=1, source_target_pairs={{0,24},{1,25},{2,26},{3,27},{4,12},{5,13},{6,14},{7,15},{8,16},{9,... | collective-permute-start | bytes 344072 | tf_op jit(solution)/shard_map/ppermute | solution.py:75
  87.6 3.6 %collective-permute-start.11 = (s16[1,448,128]{2,1,0:T(8,128)(2,1)S(1)}, s16[1,448,128]{2,1,0:T(8,128)(2,1)S(1)}, u32[]{:S(2)}, u32[]{:S(2)}) collective-permute-start(s16[1,448,128]{2,1,0:T(8,128)(2,1)S(1)} %shard_map.99.own), channel_id=1, source_target_pairs={{0,96},{1,97},{2,98},{3,99},{4,36},{5,37},{6,38},{7,39},{8,104},{9... | collective-permute-start | bytes 344072 | tf_op jit(solution)/shard_map/ppermute | solution.py:75
  91.4 5.9 %collective-permute-start.16 = (s16[1,448,128]{2,1,0:T(8,128)(2,1)S(1)}, s16[1,448,128]{2,1,0:T(8,128)(2,1)S(1)}, u32[]{:S(2)}, u32[]{:S(2)}) collective-permute-start(s16[1,448,128]{2,1,0:T(8,128)(2,1)S(1)} %shard_map.100), channel_id=1, source_target_pairs={{0,11},{1,10},{2,9},{3,8},{4,29},{5,28},{6,31},{7,30},{8,3},{9,2},... | collective-permute-start | bytes 344072 | tf_op jit(solution)/shard_map/ppermute | solution.py:75
  92.5 5.1 %collective-permute-start.15 = (s16[1,448,128]{2,1,0:T(8,128)(2,1)S(1)}, s16[1,448,128]{2,1,0:T(8,128)(2,1)S(1)}, u32[]{:S(2)}, u32[]{:S(2)}) collective-permute-start(s16[1,448,128]{2,1,0:T(8,128)(2,1)S(1)} %shard_map.100), channel_id=1, source_target_pairs={{0,3},{1,2},{2,1},{3,0},{4,5},{5,4},{6,7},{7,6},{8,11},{9,10},{10,... | collective-permute-start | bytes 344072 | tf_op jit(solution)/shard_map/ppermute | solution.py:75
  94.3 4.9 %collective-permute-start.14 = (s16[1,448,128]{2,1,0:T(8,128)(2,1)S(1)}, s16[1,448,128]{2,1,0:T(8,128)(2,1)S(1)}, u32[]{:S(2)}, u32[]{:S(2)}) collective-permute-start(s16[1,448,128]{2,1,0:T(8,128)(2,1)S(1)} %shard_map.100), channel_id=1, source_target_pairs={{0,8},{1,9},{2,10},{3,11},{4,28},{5,29},{6,30},{7,31},{8,0},{9,1},... | collective-permute-start | bytes 344072 | tf_op jit(solution)/shard_map/ppermute | solution.py:75
  99.1 26.1 %collective-permute-start.19 = (s16[4,448,128]{2,1,0:T(8,128)(2,1)S(1)}, s16[4,448,128]{2,1,0:T(8,128)(2,1)}, u32[]{:S(2)}, u32[]{:S(2)}) collective-permute-start(s16[4,448,128]{2,1,0:T(8,128)(2,1)S(1)} %pad_add_fusion.a0), channel_id=1, source_target_pairs={{0,33},{1,32},{2,35},{3,34},{4,103},{5,102},{6,101},{7,100},{8,41}... | collective-permute-start | bytes 1376264 | tf_op jit(solution)/shard_map/ppermute | solution.py:75
  101.6 23.7 %collective-permute-start.18 = (s16[4,448,128]{2,1,0:T(8,128)(2,1)S(1)}, s16[4,448,128]{2,1,0:T(8,128)(2,1)}, u32[]{:S(2)}, u32[]{:S(2)}) collective-permute-start(s16[4,448,128]{2,1,0:T(8,128)(2,1)S(1)} %pad_add_fusion.a0), channel_id=1, source_target_pairs={{0,32},{1,33},{2,34},{3,35},{4,100},{5,101},{6,102},{7,103},{8,40}... | collective-permute-start | bytes 1376264 | tf_op jit(solution)/shard_map/ppermute | solution.py:75
  103.5 22.3 %collective-permute-start.17 = (s16[4,448,128]{2,1,0:T(8,128)(2,1)S(1)}, s16[4,448,128]{2,1,0:T(8,128)(2,1)}, u32[]{:S(2)}, u32[]{:S(2)}) collective-permute-start(s16[4,448,128]{2,1,0:T(8,128)(2,1)S(1)} %pad_add_fusion.a0), channel_id=1, source_target_pairs={{0,1},{1,0},{2,3},{3,2},{4,7},{5,6},{6,5},{7,4},{8,9},{9,8},{10,11... | collective-permute-start | bytes 1376264 | tf_op jit(solution)/shard_map/ppermute | solution.py:75
  104.8 0.9 copy-start.7
  105.7 0.9 copy-start.9
  106.5 0.8 copy-start.12
  107.4 0.8 copy-start.14
  108.2 17.6 %copy-start.5 = (bf16[10,16,256]{2,1,0:T(8,128)(2,1)S(1)}, bf16[10,16,256]{2,1,0:T(8,128)(2,1)}, u32[]{:S(2)}) copy-start(bf16[10,16,256]{2,1,0:T(8,128)(2,1)} %get-tuple-element.29.x_high) | copy-start | bytes 245764
  108.2 17.6 %copy-start.10 = (bf16[8,16,256]{2,1,0:T(8,128)(2,1)S(1)}, bf16[8,16,256]{2,1,0:T(8,128)(2,1)}, u32[]{:S(2)}) copy-start(bf16[8,16,256]{2,1,0:T(8,128)(2,1)} %get-tuple-element.33.y_high) | copy-start | bytes 196612
  119.4 19.6 %collective-permute-start.20 = (s16[4,448,128]{2,1,0:T(8,128)(2,1)S(1)}, s16[4,448,128]{2,1,0:T(8,128)(2,1)S(1)}, u32[]{:S(2)}, u32[]{:S(2)}) collective-permute-start(s16[4,448,128]{2,1,0:T(8,128)(2,1)S(1)} %pad_add_fusion.a0), channel_id=1, source_target_pairs={{0,4},{1,5},{2,6},{3,7},{4,0},{5,1},{6,2},{7,3},{8,12},{9,13},{10,... | collective-permute-start | bytes 1376264 | tf_op jit(solution)/shard_map/ppermute | solution.py:361
  125.2 13.7 %collective-permute-start.23 = (s16[4,448,128]{2,1,0:T(8,128)(2,1)}, s16[4,448,128]{2,1,0:T(8,128)(2,1)S(1)}, u32[]{:S(2)}, u32[]{:S(2)}) collective-permute-start(s16[4,448,128]{2,1,0:T(8,128)(2,1)} %collective-permute-done.19.a3), channel_id=1, source_target_pairs={{0,4},{1,5},{2,6},{3,7},{4,0},{5,1},{6,2},{7,3},{8,12},{9,13},{10,... | collective-permute-start | bytes 1376264 | tf_op jit(solution)/shard_map/ppermute | solution.py:361
  125.3 13.6 %collective-permute-start.22 = (s16[4,448,128]{2,1,0:T(8,128)(2,1)}, s16[4,448,128]{2,1,0:T(8,128)(2,1)S(1)}, u32[]{:S(2)}, u32[]{:S(2)}) collective-permute-start(s16[4,448,128]{2,1,0:T(8,128)(2,1)} %collective-permute-done.18.a2), channel_id=1, source_target_pairs={{0,4},{1,5},{2,6},{3,7},{4,0},{5,1},{6,2},{7,3},{8,12},{9,13},{10,... | collective-permute-start | bytes 1376264 | tf_op jit(solution)/shard_map/ppermute | solution.py:361
  125.8 13.2 %collective-permute-start.21 = (s16[4,448,128]{2,1,0:T(8,128)(2,1)}, s16[4,448,128]{2,1,0:T(8,128)(2,1)S(1)}, u32[]{:S(2)}, u32[]{:S(2)}) collective-permute-start(s16[4,448,128]{2,1,0:T(8,128)(2,1)} %collective-permute-done.17.a1), channel_id=1, source_target_pairs={{0,4},{1,5},{2,6},{3,7},{4,0},{5,1},{6,2},{7,3},{8,12},{9,13},{10,... | collective-permute-start | bytes 1376264 | tf_op jit(solution)/shard_map/ppermute | solution.py:361

commit v2 on v1

v2 whole, which is shorter than its diff:
```python
import functools

import jax
import jax.numpy as jnp
from jax import lax
from jax.experimental import pallas as pl
from jax.experimental.pallas import tpu as pltpu
from jax.sharding import PartitionSpec as P

BOTH = ("gx", "gy")
C = 256
HALF = 128
K = 27
EACH = 7
ROWS = 224
BLOCK = 32
BLOCKS = ROWS // BLOCK
CODED = ROWS + 16

CODED_4 = jax.ShapeDtypeStruct((4, CODED, C), jnp.int16)
CODED_1 = jax.ShapeDtypeStruct((1, CODED, C), jnp.int16)

VMEM = pl.BlockSpec(memory_space=pltpu.VMEM)
HBM = pl.BlockSpec(memory_space=pltpu.HBM)
SMEM = pl.BlockSpec(memory_space=pltpu.SMEM)
PARAMS = pltpu.CompilerParams(vmem_limit_bytes=28 * 2**20)

FIRST, SECOND = 0, 1
GROUPS = (
    ((("x", FIRST), ("y", FIRST)), (("z", FIRST), ("x", SECOND)), (("y", SECOND), ("z", SECOND))),
    ((("z", FIRST), ("y", SECOND)), (("x", FIRST), ("y", FIRST)), (("x", SECOND), ("z", SECOND))),
)


def paired(v, pairing):
    return v ^ 1 if pairing == FIRST else 3 - v


def pair_bit(v, pairing):
    return (v ^ (v >> 1)) & 1 if pairing == FIRST else v >> 1


def number(at):
    return ((at["y"] * 4 + at["z"]) * 2 + at["core"]) * 4 + at["x"]


def places():
    for y in range(4):
        for z in range(4):
            for core in range(2):
                for x in range(4):
                    yield {"x": x, "y": y, "z": z, "core": core}


def partners(level, member):
    pairs = []
    for at in places():
        to = dict(at)
        for i, (axis, pairing) in enumerate(GROUPS[at["core"]][level]):
            if member in ((1, 2), (1, 3))[i]:
                to[axis] = paired(to[axis], pairing)
        pairs.append((number(at), number(to)))
    return pairs


def other_core():
    return [(number(at), number({**at, "core": 1 - at["core"]})) for at in places()]


def rank_in(level, core, at):
    ranks = []
    for c in range(2):
        (a, pa), (b, pb) = GROUPS[c][level]
        u, v = pair_bit(at[a], pa), pair_bit(at[b], pb)
        ranks.append(2 * (u ^ v) + v)
    return jnp.where(core == 0, ranks[0], ranks[1])


def exchange(arrays, level):
    return [lax.ppermute(a, BOTH, partners(level, m + 1)) for m, a in enumerate(arrays)]


def after(value, *others):
    return lax.optimization_barrier((value, *others))[0]


def call(kernel, outs, *args, flops=0, scratch=(), space=None):
    size = sum(a.size * a.dtype.itemsize for a in args) + sum(o.size * o.dtype.itemsize for o in outs)
    return pl.pallas_call(
        kernel,
        out_shape=list(outs),
        in_specs=[SMEM if a.dtype == jnp.int32 and a.size < 100 else space or VMEM for a in args],
        out_specs=[VMEM] * len(outs),
        scratch_shapes=list(scratch),
        compiler_params=PARAMS,
        cost_estimate=pl.CostEstimate(flops=flops, bytes_accessed=size, transcendentals=0),
    )(*args)


def shape(dims, dtype):
    return jax.ShapeDtypeStruct(dims, dtype)


def put_coded(read, ref, index):
    row = lax.broadcasted_iota(jnp.int32, (16, C), 0)
    exponents = jnp.zeros((16, C), jnp.float32)
    for b in range(BLOCKS):
        x = read(b)
        top = jnp.max(jnp.abs(x), axis=0, keepdims=True)
        e = jnp.ceil(jnp.log2(jnp.maximum(top, 2.0**-110)))
        q = jnp.clip(jnp.round(x * jnp.exp2(15.0 - e)), -32767.0, 32767.0)
        ref[index, b * BLOCK : (b + 1) * BLOCK, :] = q.astype(jnp.int16)
        exponents = jnp.where(row == b, e, exponents)
    ref[index, ROWS:CODED, :] = exponents.astype(jnp.int16)


def coded_scales(ref, index):
    return jnp.exp2(ref[index, ROWS:CODED, :].astype(jnp.float32) - 15.0)


def block_of(ref, index, b):
    return ref[index, b * BLOCK : (b + 1) * BLOCK, :]


def coded_block(ref, index, scales, b):
    return block_of(ref, index, b).astype(jnp.float32) * scales[b : b + 1, :]


def pair_sum_kernel(last, own, got, out):
    for c in range(4):
        scales = coded_scales(got, c)

        def read(b, c=c, scales=scales):
            rows = slice(c * ROWS + b * BLOCK, c * ROWS + (b + 1) * BLOCK)
            return own[rows, :] + coded_block(got, c, scales, b)

        if last:
            for b in range(BLOCKS):
                out[c, b * BLOCK : (b + 1) * BLOCK, :] = read(b)
        else:
            put_coded(read, out, c)


def group_sum_kernel(rank, own, got_1, got_2, got_3, keep, first, second, third):
    g = rank[0]
    for m, out in enumerate((keep, first, second, third)):
        at = g ^ m
        scales = [coded_scales(r, at) for r in (got_1, got_2, got_3)]

        def read(b, at=at, scales=scales):
            x = block_of(own, at, b)
            for r, s in zip((got_1, got_2, got_3), scales):
                x = x + coded_block(r, at, s, b)
            return x

        if m == 0:
            for b in range(BLOCKS):
                out[0, b * BLOCK : (b + 1) * BLOCK, :] = read(b)
        else:
            put_coded(read, out, 0)


def last_group_kernel(own, got_1, got_2, got_3, out):
    scales = [coded_scales(r, 0) for r in (got_1, got_2, got_3)]

    def read(b):
        x = block_of(own, 0, b)
        for r, s in zip((got_1, got_2, got_3), scales):
            x = x + coded_block(r, 0, s, b)
        return x

    put_coded(read, out, 0)


def total_kernel(own, got_1, got_2, got_3, out):
    refs = (own, got_1, got_2, got_3)
    scales = [coded_scales(r, 0) for r in refs]

    def read(b):
        a = [coded_block(r, 0, s, b) for r, s in zip(refs, scales)]
        return (a[0] + a[1]) + (a[2] + a[3])

    put_coded(read, out, 0)


def finish_kernel(scale, parts, where, *refs):
    n = len(parts)
    out, stage, done = refs[-3:]

    def copy_of(s, j):
        side, member = parts[s]
        k = (where[2 + side] ^ member) * EACH + j
        rows = pl.ds(pl.multiple_of((where[0] ^ side) * HALF, HALF), HALF)
        copy = pltpu.make_async_copy(stage.at[s, j], out.at[jnp.minimum(k, K - 1), rows, :], done.at[s, j])
        return k, copy

    def each(s, j, act):
        k, copy = copy_of(s, j)
        if j < EACH - 1:
            act(copy)
        else:
            pl.when(k < K)(lambda: act(copy))

    for s in range(n):
        for place in range(4):
            c = where[4 + parts[s][0]] ^ place
            scales = coded_scales(refs[s], c) * scale
            for b in range(BLOCKS):
                at = place * BLOCKS + b
                stage[s, at // 4, at % 4 * BLOCK : (at % 4 + 1) * BLOCK, :] = coded_block(refs[s], c, scales, b)
                if at % 4 == 3:
                    each(s, at // 4, lambda copy: copy.start())
    for s in range(n):
        for j in range(EACH):
            each(s, j, lambda copy: copy.wait())


def finish(scale, where, parts, sets, before):
    more = [] if before is None else [before]
    n = len(sets)
    return pl.pallas_call(
        functools.partial(finish_kernel, scale, parts),
        out_shape=shape((K, C, C), jnp.float32),
        in_specs=[SMEM] + [VMEM] * n + [HBM] * len(more),
        out_specs=HBM,
        scratch_shapes=[pltpu.VMEM((n, EACH, HALF, C), jnp.float32), pltpu.SemaphoreType.DMA((n, EACH))],
        input_output_aliases={1 + n: 0} if more else {},
        compiler_params=PARAMS,
        cost_estimate=pl.CostEstimate(flops=0, bytes_accessed=n * EACH * HALF * C * 6, transcendentals=0),
    )(where, *sets, *more)


def prepare_kernel(odd, features, cotangent, occupancy, cells, grad, masks, y_a, y_b):
    r = lax.broadcasted_iota(jnp.int32, (128, 128), 0)
    c = lax.broadcasted_iota(jnp.int32, (128, 128), 1)
    same = (r >> 4 == (c >> 3) & 7) & ((r >> 3) & 1 == c >> 6) & (r & 7 == c & 7)
    low = lax.broadcasted_iota(jnp.int32, (1, 128), 1) < 64
    occupied = occupancy[...].astype(jnp.float32)
    turned = pltpu.roll(occupied, 64, 1)
    even = odd[0] == 0
    for x in range(8):
        lanes = slice(128 * (x // 2), 128 * (x // 2) + 128)
        if x % 2 == 0:
            row = jnp.where(low, occupied[0:1, lanes], turned[1:2, lanes])
        else:
            after_it = slice((lanes.start + 128) % 512, (lanes.start + 128) % 512 + 128)
            row = jnp.where(low, turned[0:1, after_it], occupied[1:2, lanes])
        pick = jnp.where(same, row, 0.0).astype(jnp.bfloat16)
        masks[x] = pick
        for index, (source, out) in enumerate(((features, cells), (cotangent, grad))):
            layer = jnp.concatenate([source[0, x], source[1, x]], axis=0)
            made = jnp.dot(pick, layer, preferred_element_type=jnp.float32).astype(jnp.bfloat16)
            made = made.reshape(8, 16, C)
            out[x] = made
            y_a[index, x] = jnp.where(even, made[7], made[0])
            y_b[index, x] = jnp.where(even, made[0], made[7])


def picks_kernel(neighbors, out):
    r = lax.broadcasted_iota(jnp.int32, (160, 160), 0)
    c = lax.broadcasted_iota(jnp.int32, (160, 160), 1)
    y, s, z = r >> 4, (r >> 3) & 1, r & 7
    same = y == c >> 4
    side_y = jnp.where(y == 0, 0, jnp.where(y == 9, 2, 1))
    which = side_y * 2 + s
    for ox in range(3):
        for oz in range(3):
            edge = z == (0 if oz == 0 else 7)
            slot = jnp.full((160, 160), -1, jnp.int32)
            for oy in range(3):
                for brick in range(2):
                    level = neighbors[brick, 9 * ox + 3 * oy + 1]
                    beyond = neighbors[brick, 9 * ox + 3 * oy + oz]
                    found = jnp.where(edge, beyond, level) if oz != 1 else level
                    slot = jnp.where(which == 2 * oy + brick, found, slot)
            hit = same & (slot >= 0) & ((c & 15) == slot * 8 + ((z + oz - 1) & 7))
            out[ox, 160 * oz : 160 * (oz + 1), :] = jnp.where(hit, 1.0, 0.0).astype(jnp.bfloat16)


def edges_kernel(odd, cells, grad, y_a, y_b, x_a, x_b):
    even = odd[0] == 0
    for out, x in ((x_a, jnp.where(odd[1] == 0, 7, 0)), (x_b, jnp.where(odd[1] == 0, 0, 7))):
        for i, a in enumerate((cells, grad)):
            out[i, 0] = jnp.where(even, y_b[i, x], y_a[i, x])
            out[i, 1:9] = a[x]
            out[i, 9] = jnp.where(even, y_a[i, x], y_b[i, x])


def widen(index, odd, pick, cells, y_a, y_b, x_a, x_b, wide):
    even, core_0 = odd[0] == 0, odd[1] == 0
    for x in range(10):
        if x == 0:
            layer, side = jnp.where(core_0, x_b[index], x_a[index]).reshape(160, C), 0
        elif x == 9:
            layer, side = jnp.where(core_0, x_a[index], x_b[index]).reshape(160, C), 2
        else:
            a, b = y_a[index, x - 1], y_b[index, x - 1]
            layer = jnp.concatenate(
                [jnp.where(even, b, a), cells[x - 1].reshape(128, C), jnp.where(even, a, b)], axis=0
            )
            side = 1
        moved = jnp.dot(pick[side], layer, preferred_element_type=jnp.float32).astype(jnp.bfloat16)
        for oz in range(3):
            wide[oz, x] = moved[160 * oz : 160 * (oz + 1)].reshape(10, 16, C)


def widen_kernel(odd, pick, cells, y_a, y_b, x_a, x_b, wide):
    widen(0, odd, pick, cells, y_a, y_b, x_a, x_b, wide)


def part_kernel(member, where, wide, grad, own, coded, terms):
    g = grad[...].reshape(1024, C)
    for j in range(EACH):
        sides = []
        for side in range(2):
            k = jnp.minimum((where[2 + side] ^ member) * EACH + j, K - 1)
            lanes = pl.ds(pl.multiple_of((where[0] ^ side) * HALF, HALF), HALF)
            w = wide[k % 3, pl.ds(k // 9, 8), pl.ds((k // 3) % 3, 8), :, lanes]
            sides.append(w.reshape(1024, HALF))
        t = lax.dot_general(
            jnp.concatenate(sides, axis=1), g, (((0,), (0,)), ((), ())), preferred_element_type=jnp.float32
        )
        own[j * HALF : (j + 1) * HALF, :] = t[:HALF]
        terms[j * HALF : (j + 1) * HALF, :] = t[HALF:]
    for c in range(4):
        put_coded(lambda b, c=c: terms[c * ROWS + b * BLOCK : c * ROWS + (b + 1) * BLOCK, :], coded, c)


def convolve(back, wide, kernel, masks, out, sums):
    for x in range(0, 8, 2):
        total = None
        for k in range(K):
            ox, oy, oz = k // 9, (k // 3) % 3, k % 3
            if back:
                ox, oy, oz = 2 - ox, 2 - oy, 2 - oz
            w = wide[oz, ox + x : ox + x + 2, oy : oy + 8].reshape(256, C)
            d = lax.dot_general(
                w, kernel[k], (((1,), (1 if back else 0,)), ((), ())), preferred_element_type=jnp.float32
            )
            total = d if total is None else total + d
        sums[x * 128 : (x + 2) * 128, :] = total.astype(jnp.bfloat16)
    for x in range(8):
        cells = lax.dot_general(
            masks[x], sums[x * 128 : (x + 1) * 128, :], (((0,), (0,)), ((), ())),
            preferred_element_type=jnp.float32,
        ).astype(jnp.bfloat16)
        out[0, x] = cells[:64]
        out[1, x] = cells[64:]


def forward_kernel(wide, kernel, masks, out, sums):
    convolve(False, wide, kernel, masks, out, sums)


def backward_kernel(odd, pick, grad, y_a, y_b, x_a, x_b, kernel, masks, out, sums, wide):
    widen(1, odd, pick, grad, y_a, y_b, x_a, x_b, wide)
    convolve(True, wide, kernel, masks, out, sums)


def shards(features, cotangent, kernel, occupancy, neighbors):
    gx, gy = lax.axis_index("gx"), lax.axis_index("gy")
    core = gx % 2
    at = {"x": gy, "y": gx // 8, "z": (gx // 2) % 4}
    scale = 1.0 / (512.0 * 256.0) ** 0.5
    outer, inner = rank_in(0, core, at), rank_in(1, core, at)
    where = jnp.stack([core, inner, outer, rank_in(0, 1 - core, at), inner, rank_in(1, 1 - core, at)])
    where = where.astype(jnp.int32)

    odd = jnp.stack([gy % 2, core]).astype(jnp.int32)

    y_pairs = ([(0, 1), (1, 0), (2, 3), (3, 2)], [(1, 2), (2, 1)])
    x_pairs = ([(i, i ^ 1) for i in range(32)], [(i, i + 1 if i % 2 else i - 1) for i in range(1, 31)])

    column = shape((8, 8, 16, C), jnp.bfloat16)
    wide_shape = (3, 10, 10, 16, C)
    side_y = shape((2, 8, 16, C), jnp.bfloat16)
    side_x = shape((2, 10, 16, C), jnp.bfloat16)
    cells, grad, masks, *sides = call(
        prepare_kernel,
        [column, column, shape((8, 128, 128), jnp.bfloat16)] + [side_y] * 2,
        odd, features.reshape(2, 8, 64, C), cotangent.reshape(2, 8, 64, C), occupancy,
    )
    y_halo = [lax.ppermute(a, "gy", pairs) for a, pairs in zip(sides, y_pairs)]
    (pick,) = call(picks_kernel, [shape((3, 480, 160), jnp.bfloat16)], after(neighbors, sides[0]))
    edges = call(edges_kernel, [side_x, side_x], odd, cells, grad, *y_halo)
    x_halo = [lax.ppermute(a, "gx", pairs) for a, pairs in zip(edges, x_pairs)]
    (wide,) = call(widen_kernel, [shape(wide_shape, jnp.bfloat16)], odd, pick, cells, *y_halo, *x_halo)

    flops = 2 * K * 1024 * C * C
    sums = {}
    got = {}
    for m in (1, 2, 3, 0):
        own, coded = call(
            functools.partial(part_kernel, m),
            [shape((EACH * HALF, C), jnp.float32), CODED_4],
            where, wide, grad,
            flops=flops // 4,
            scratch=[pltpu.VMEM((EACH * HALF, C), jnp.float32)],
        )
        other = lax.ppermute(coded, BOTH, other_core())
        out = CODED_4 if m else shape((4, ROWS, C), jnp.float32)
        (sums[m],) = call(functools.partial(pair_sum_kernel, m == 0), [out], own, other)
        if m:
            got[m] = lax.ppermute(sums[m], BOTH, partners(0, m))

    brick_rows = shape((2, 8, 64, C), jnp.bfloat16)
    totals = pltpu.VMEM((1024, C), jnp.bfloat16)
    (forward,) = call(
        forward_kernel, [brick_rows], after(wide, sums[0], sums[3]), kernel, masks, flops=flops, scratch=[totals]
    )
    keep, *sent = call(
        group_sum_kernel,
        [shape((1, ROWS, C), jnp.float32)] + [CODED_1] * 3,
        inner.reshape(1).astype(jnp.int32), after(sums[0], forward), got[1], got[2], got[3],
    )
    (part,) = call(last_group_kernel, [CODED_1], keep, *exchange(sent, 1))
    (whole,) = call(total_kernel, [CODED_1], part, *exchange([part] * 3, 2))
    four = jnp.concatenate([whole] + exchange([whole] * 3, 1))
    sets = [four] + exchange([four] * 3, 0)
    (backward,) = call(
        backward_kernel, [brick_rows], odd, pick, after(grad, four), *y_halo, *x_halo, kernel, masks,
        flops=flops, scratch=[totals, pltpu.VMEM(wide_shape, jnp.bfloat16)],
    )
    others = [lax.ppermute(sets[0], BOTH, other_core())]
    done = finish(scale, where, [(0, 0), (1, 0)], [sets[0], others[0]], None)
    sets[1:] = [after(s, backward, done) for s in sets[1:]]
    others += [lax.ppermute(s, BOTH, other_core()) for s in sets[1:3]]
    done = finish(scale, where, [(0, 1), (0, 2)], sets[1:3], done)
    others.append(lax.ppermute(after(sets[3], done), BOTH, other_core()))
    done = finish(scale, where, [(0, 3), (1, 1), (1, 2)], [sets[3], *others[1:3]], done)
    done = finish(scale, where, [(1, 3)], others[3:], done)
    return forward.reshape(2, 8, 8, 8, C), backward.reshape(2, 8, 8, 8, C), done


def solution(mesh):
    placed = (
        P(BOTH, None, None, None, None),
        P(BOTH, None, None, None, None),
        P(),
        P(BOTH, None),
        P(BOTH, None),
    )
    return jax.shard_map(
        shards,
        mesh=mesh,
        in_specs=placed,
        out_specs=(P(BOTH, None, None, None, None), P(BOTH, None, None, None, None), P()),
        check_vma=False,
    )
```

time: 145 us -> 107 us (0.74)
  Pallas kernels: 48.4 us -> 31.9 us
  local copies, waits for them, and re-layouts: 19.2 us -> 3.54 us
  waiting for transfers between devices: 29.7 us -> 23.3 us
  starting transfers between devices: 41.8 us -> 47.2 us
  other arithmetic: 4.2 us -> 0.11 us
    pallas_call x8 -> x21, Pallas kernels: 48.4 us -> 31.9 us  [the longest x17 24.4 us: call(): pl.pallas_call(kernel, out_shape=list(outs), in_specs=[SMEM if a.dtype ==...]
    ppermute x9 -> x15, starting transfers between devices: 18.1 us -> 29.1 us  [the longest x1 12 us: shards(): others = [lax.ppermute(sets[0], BOTH, other_core())]]
    ppermute x15 -> x12, waiting for transfers between devices: 21.7 us -> 15 us  [exchange(): lax.ppermute(a, BOTH, partners(level, m + 1))]
    ppermute x15 -> x12, starting transfers between devices: 23.7 us -> 18.1 us  [exchange(): lax.ppermute(a, BOTH, partners(level, m + 1))]
    broadcast_in_dim x14 -> x0, local copies, waits for them, and re-layouts: 3.78 us -> none  [the longest x9 2.67 us: picks(): jnp.where(beyond > 0, n[..., 2], n[..., 1])]
    slice x8 -> x0, local copies, waits for them, and re-layouts: 3.76 us -> none  [the longest x5 3.62 us: picks(): n = jnp.concatenate([n[:, :1]] + [n[:, 1:2]] * 8 + [n[:, 2:]], axis=1)]
    unnamed x41 -> x10, local copies, waits for them, and re-layouts: 6.69 us -> 3.45 us
    mul x3 -> x0, other arithmetic: 2.32 us -> none  [the longest x1 1.41 us: shards(): cells = cells_of(features) * mask_b]
  transfers between devices with their start and end apart: 24 -> 27, of which waited for: 13 -> 14; matrix products, arithmetic and copies ran while one was open for 9% -> 0% of each run, Pallas kernels for 16% -> 21%
where the time goes in v2:
time: 107 us
  starting transfers between devices  47.2 us (44%)
  Pallas kernels  31.9 us (30%)
  waiting for transfers between devices  23.3 us (22%)
  local copies, waits for them, and re-layouts  3.54 us (3%)
  between operations  1.09 us (1%)
    pallas_call x17, Pallas kernels, call(): pl.pallas_call(kernel, out_shape=list(outs), in_specs=[SMEM if a.dtype ==...  24.4 us
    ppermute x12, starting transfers between devices, exchange(): lax.ppermute(a, BOTH, partners(level, m + 1))  18.1 us
    ppermute x12, waiting for transfers between devices, exchange(): lax.ppermute(a, BOTH, partners(level, m + 1))  15 us
    ppermute x1, starting transfers between devices, shards(): others = [lax.ppermute(sets[0], BOTH, other_core())]  12 us
    pallas_call x4, Pallas kernels, finish(): pl.pallas_call(functools.partial(finish_kernel, scale, parts), out_shape=...  7.51 us
    ppermute x3, starting transfers between devices, shards(): got[m] = lax.ppermute(sums[m], BOTH, partners(0, m))  6.71 us
    ppermute x2, starting transfers between devices, shards(): x_halo = [lax.ppermute(a, 'gx', pairs) for a, pairs in zip(edges, x_pairs)]  5.5 us
    ppermute x3, waiting for transfers between devices, shards(): got[m] = lax.ppermute(sums[m], BOTH, partners(0, m))  5.48 us
  transfers between devices with their start and end apart: 27, of which 14 were waited for; matrix products, arithmetic and copies ran while one was open for 0% of the time, Pallas kernels for 21%

profile of v2, /device:TPU:1, one launch (start us, length us, event | category | flops | bytes accessed | tf_op | source)
XLA Modules:
  0.0 107.2 jit_solution(5819600001062573519)
XLA Ops:
  0.7 1.0 copy-done
  1.8 1.0 copy-done.1
  2.8 0.7 copy-done.2
  3.5 1.0 shard_map.76
  4.5 2.1 %collective-permute-start = (bf16[2,8,16,256]{3,2,1,0:T(8,128)(2,1)S(1)}, bf16[2,8,16,256]{3,2,1,0:T(8,128)(2,1)S(1)}, u32[]{:S(2)}, u32[]{:S(2)}) collective-permute-start(bf16[2,8,16,256]{3,2,1,0:T(8,128)(2,1)S(1)} %get-tuple-element.30), channel_id=1, source_target_pairs={{0,1},{1,0},{2,3},{3,2},{4,5},{5,4},{6,7},{7,6},{8,9},{9,8},{10,11... | collective-permute-start | bytes 393224 | tf_op jit(solution)/shard_map/ppermute | solution.py:383
  6.7 0.7 collective-permute-start.1
  7.3 2.1 %collective-permute-done.y_a = bf16[2,8,16,256]{3,2,1,0:T(8,128)(2,1)S(1)} collective-permute-done((bf16[2,8,16,256]{3,2,1,0:T(8,128)(2,1)S(1)}, bf16[2,8,16,256]{3,2,1,0:T(8,128)(2,1)S(1)}, u32[]{:S(2)}, u32[]{:S(2)}) %collective-permute-start) | collective-permute-done | bytes 131104 | tf_op jit(solution)/shard_map/ppermute | solution.py:383
  9.4 0.6 shard_map.78
  10.0 1.8 %collective-permute-start.2 = (bf16[2,10,16,256]{3,2,1,0:T(8,128)(2,1)S(1)}, bf16[2,10,16,256]{3,2,1,0:T(8,128)(2,1)S(1)}, u32[]{:S(2)}, u32[]{:S(2)}) collective-permute-start(bf16[2,10,16,256]{3,2,1,0:T(8,128)(2,1)S(1)} %get-tuple-element.35), channel_id=1, source_target_pairs={{0,4},{4,0},{8,12},{12,8},{16,20},{20,16},{24,28},{28,24},{32,36},... | collective-permute-start | bytes 491528 | tf_op jit(solution)/shard_map/ppermute | solution.py:386
  11.8 3.7 %collective-permute-start.3 = (bf16[2,10,16,256]{3,2,1,0:T(8,128)(2,1)S(1)}, bf16[2,10,16,256]{3,2,1,0:T(8,128)(2,1)S(1)}, u32[]{:S(2)}, u32[]{:S(2)}) collective-permute-start(bf16[2,10,16,256]{3,2,1,0:T(8,128)(2,1)S(1)} %get-tuple-element.36), channel_id=1, source_target_pairs={{4,8},{8,4},{12,16},{16,12},{20,24},{24,20},{28,32},{32,28},{36,40... | collective-permute-start | bytes 491528 | tf_op jit(solution)/shard_map/ppermute | solution.py:386
  15.5 0.7 copy-done.3
  16.2 1.3 %shard_map.77.pick = bf16[3,480,160]{2,1,0:T(8,128)(2,1)S(1)} custom-call(s32[2,27]{1,0:T(2,128)S(1)} %copy-done.3), custom_call_target="tpu_custom_call" | custom-call | bytes 461016 | tf_op jit(solution)/shard_map/pallas_call | solution.py:89
  17.6 0.8 collective-permute-done.3.x_b
  18.5 1.3 %shard_map.79.wide = bf16[3,10,10,16,256]{4,3,2,1,0:T(8,128)(2,1)S(1)} custom-call(s32[2]{0:T(128)S(1)} %pad_add_fusion.1.odd, bf16[3,480,160]{2,1,0:T(8,128)(2,1)S(1)} %shard_map.77.pick, bf16[8,8,16,256]{3,2,1,0:T(8,128)(2,1)S(1)} %get-tuple-element.32.cells, bf16[2,8,16,256]{3,2,1,0:T(8,128)(2,1)S(1)} %collective-permute-done.y_a, ...), custom_call_target="tpu_custom_call" | custom-call | bytes 4032520 | tf_op jit(solution)/shard_map/pallas_call | solution.py:89
  19.8 1.8 %shard_map.87 = (f32[896,256]{1,0:T(8,128)S(1)}, s16[4,240,256]{2,1,0:T(8,128)(2,1)S(1)}) custom-call(s32[6]{0:T(128)S(1)} %stack.33.where, bf16[3,10,10,16,256]{4,3,2,1,0:T(8,128)(2,1)S(1)} %shard_map.79.wide, bf16[8,8,16,256]{3,2,1,0:T(8,128)(2,1)S(1)} %get-tuple-element.52.grad), custom_call_target="tpu_custom_call" | custom-call | flops 905969664 | bytes 4390936 | tf_op jit(solution)/shard_map/pallas_call | solution.py:89
  21.6 1.8 %shard_map.85 = (f32[896,256]{1,0:T(8,128)S(1)}, s16[4,240,256]{2,1,0:T(8,128)(2,1)S(1)}) custom-call(s32[6]{0:T(128)S(1)} %stack.33.where, bf16[3,10,10,16,256]{4,3,2,1,0:T(8,128)(2,1)S(1)} %shard_map.79.wide, bf16[8,8,16,256]{3,2,1,0:T(8,128)(2,1)S(1)} %get-tuple-element.52.grad), custom_call_target="tpu_custom_call" | custom-call | flops 905969664 | bytes 4390936 | tf_op jit(solution)/shard_map/pallas_call | solution.py:89
  23.5 0.5 collective-permute-start.6
  24.0 1.8 %shard_map.82 = (f32[896,256]{1,0:T(8,128)S(1)}, s16[4,240,256]{2,1,0:T(8,128)(2,1)S(1)}) custom-call(s32[6]{0:T(128)S(1)} %stack.33.where, bf16[3,10,10,16,256]{4,3,2,1,0:T(8,128)(2,1)S(1)} %shard_map.79.wide, bf16[8,8,16,256]{3,2,1,0:T(8,128)(2,1)S(1)} %get-tuple-element.52.grad), custom_call_target="tpu_custom_call" | custom-call | flops 905969664 | bytes 4390936 | tf_op jit(solution)/shard_map/pallas_call | solution.py:89
  26.0 1.8 %shard_map.80 = (f32[896,256]{1,0:T(8,128)S(1)}, s16[4,240,256]{2,1,0:T(8,128)(2,1)S(1)}) custom-call(s32[6]{0:T(128)S(1)} %stack.33.where, bf16[3,10,10,16,256]{4,3,2,1,0:T(8,128)(2,1)S(1)} %shard_map.79.wide, bf16[8,8,16,256]{3,2,1,0:T(8,128)(2,1)S(1)} %get-tuple-element.52.grad), custom_call_target="tpu_custom_call" | custom-call | flops 905969664 | bytes 4390936 | tf_op jit(solution)/shard_map/pallas_call | solution.py:89
  28.6 1.9 %collective-permute-start.9 = (s16[4,240,256]{2,1,0:T(8,128)(2,1)S(1)}, s16[4,240,256]{2,1,0:T(8,128)(2,1)S(1)}, u32[]{:S(2)}, u32[]{:S(2)}) collective-permute-start(s16[4,240,256]{2,1,0:T(8,128)(2,1)S(1)} %shard_map.88), channel_id=1, source_target_pairs={{0,1},{1,0},{2,3},{3,2},{4,12},{5,13},{6,14},{7,15},{8,9},{9,8},{1... | collective-permute-start | bytes 1474568 | tf_op jit(solution)/shard_map/ppermute | solution.py:404
  30.9 4.5 %collective-permute-start.7 = (s16[4,240,256]{2,1,0:T(8,128)(2,1)S(1)}, s16[4,240,256]{2,1,0:T(8,128)(2,1)S(1)}, u32[]{:S(2)}, u32[]{:S(2)}) collective-permute-start(s16[4,240,256]{2,1,0:T(8,128)(2,1)S(1)} %shard_map.86), channel_id=1, source_target_pairs={{0,33},{1,32},{2,35},{3,34},{4,108},{5,109},{6,110},{7,111},{8,41}... | collective-permute-start | bytes 1474568 | tf_op jit(solution)/shard_map/ppermute | solution.py:404
  36.3 4.8 %shard_map.84 = bf16[2,8,64,256]{3,2,1,0:T(8,128)(2,1)} custom-call(bf16[3,10,10,16,256]{4,3,2,1,0:T(8,128)(2,1)S(1)} %shard_map.79.wide, bf16[27,256,256]{2,1,0:T(8,128)(2,1)S(1)} %copy-done.4, bf16[8,128,128]{2,1,0:T(8,128)(2,1)S(1)} %get-tuple-element.42.masks), custom_call_target="tpu_custom_call" | custom-call | flops 3623878656 | bytes 6782976 | tf_op jit(solution)/shard_map/pallas_call | solution.py:89
  41.0 1.3 %collective-permute-done.9.got_2 = s16[4,240,256]{2,1,0:T(8,128)(2,1)S(1)} collective-permute-done((s16[4,240,256]{2,1,0:T(8,128)(2,1)S(1)}, s16[4,240,256]{2,1,0:T(8,128)(2,1)S(1)}, u32[]{:S(2)}, u32[]{:S(2)}) %collective-permute-start.9) | collective-permute-done | bytes 491552 | tf_op jit(solution)/shard_map/ppermute | solution.py:404
  42.3 4.2 %collective-permute-done.10.got_3 = s16[4,240,256]{2,1,0:T(8,128)(2,1)S(1)} collective-permute-done((s16[4,240,256]{2,1,0:T(8,128)(2,1)S(1)}, s16[4,240,256]{2,1,0:T(8,128)(2,1)S(1)}, u32[]{:S(2)}, u32[]{:S(2)}) %collective-permute-start.10) | collective-permute-done | bytes 491552 | tf_op jit(solution)/shard_map/ppermute | solution.py:404
  46.5 0.6 shard_map.89
  47.1 4.0 %collective-permute-start.11 = (s16[1,240,256]{2,1,0:T(8,128)(2,1)S(1)}, s16[1,240,256]{2,1,0:T(8,128)(2,1)S(1)}, u32[]{:S(2)}, u32[]{:S(2)}) collective-permute-start(s16[1,240,256]{2,1,0:T(8,128)(2,1)S(1)} %get-tuple-element.49), channel_id=1, source_target_pairs={{0,11},{1,10},{2,9},{3,8},{4,37},{5,36},{6,39},{7,38},{8,3},{9,2},... | collective-permute-start | bytes 368648 | tf_op jit(solution)/shard_map/ppermute | solution.py:80
  51.2 1.0 collective-permute-start.13
  52.1 1.3 %collective-permute-done.11.got_1 = s16[1,240,256]{2,1,0:T(8,128)(2,1)S(1)} collective-permute-done((s16[1,240,256]{2,1,0:T(8,128)(2,1)S(1)}, s16[1,240,256]{2,1,0:T(8,128)(2,1)S(1)}, u32[]{:S(2)}, u32[]{:S(2)}) %collective-permute-start.11) | collective-permute-done | bytes 122912 | tf_op jit(solution)/shard_map/ppermute | solution.py:80
  53.4 1.5 %collective-permute-done.12.got_2 = s16[1,240,256]{2,1,0:T(8,128)(2,1)S(1)} collective-permute-done((s16[1,240,256]{2,1,0:T(8,128)(2,1)S(1)}, s16[1,240,256]{2,1,0:T(8,128)(2,1)S(1)}, u32[]{:S(2)}, u32[]{:S(2)}) %collective-permute-start.12) | collective-permute-done | bytes 122912 | tf_op jit(solution)/shard_map/ppermute | solution.py:80
  55.1 5.8 %collective-permute-start.14 = (s16[1,240,256]{2,1,0:T(8,128)(2,1)S(1)}, s16[1,240,256]{2,1,0:T(8,128)(2,1)S(1)}, u32[]{:S(2)}, u32[]{:S(2)}) collective-permute-start(s16[1,240,256]{2,1,0:T(8,128)(2,1)S(1)} %shard_map.90.own), channel_id=1, source_target_pairs={{0,120},{1,121},{2,122},{3,123},{4,31},{5,30},{6,29},{7,28},{8,112... | collective-permute-start | bytes 368648 | tf_op jit(solution)/shard_map/ppermute | solution.py:80
  60.9 0.6 collective-permute-start.15
  61.5 1.7 %collective-permute-done.14.got_1 = s16[1,240,256]{2,1,0:T(8,128)(2,1)S(1)} collective-permute-done((s16[1,240,256]{2,1,0:T(8,128)(2,1)S(1)}, s16[1,240,256]{2,1,0:T(8,128)(2,1)S(1)}, u32[]{:S(2)}, u32[]{:S(2)}) %collective-permute-start.14) | collective-permute-done | bytes 122912 | tf_op jit(solution)/shard_map/ppermute | solution.py:80
  63.2 2.7 %collective-permute-done.15.got_2 = s16[1,240,256]{2,1,0:T(8,128)(2,1)S(1)} collective-permute-done((s16[1,240,256]{2,1,0:T(8,128)(2,1)S(1)}, s16[1,240,256]{2,1,0:T(8,128)(2,1)S(1)}, u32[]{:S(2)}, u32[]{:S(2)}) %collective-permute-start.15) | collective-permute-done | bytes 122912 | tf_op jit(solution)/shard_map/ppermute | solution.py:80
  65.8 0.6 collective-permute-done.16.got_3
  66.7 1.7 %collective-permute-start.17 = (s16[1,240,256]{2,1,0:T(8,128)(2,1)S(1)}, s16[1,240,256]{2,1,0:T(8,128)(2,1)S(1)}, u32[]{:S(2)}, u32[]{:S(2)}) collective-permute-start(s16[1,240,256]{2,1,0:T(8,128)(2,1)S(1)} %shard_map.91), channel_id=1, source_target_pairs={{0,11},{1,10},{2,9},{3,8},{4,37},{5,36},{6,39},{7,38},{8,3},{9,2},... | collective-permute-start | bytes 368648 | tf_op jit(solution)/shard_map/ppermute | solution.py:80
  68.4 0.6 collective-permute-start.18
  69.4 2.0 %collective-permute-done.17 = s16[1,240,256]{2,1,0:T(8,128)(2,1)S(1)} collective-permute-done((s16[1,240,256]{2,1,0:T(8,128)(2,1)S(1)}, s16[1,240,256]{2,1,0:T(8,128)(2,1)S(1)}, u32[]{:S(2)}, u32[]{:S(2)}) %collective-permute-start.17) | collective-permute-done | bytes 122912 | tf_op jit(solution)/shard_map/ppermute | solution.py:80
  71.4 1.5 %collective-permute-done.18 = s16[1,240,256]{2,1,0:T(8,128)(2,1)S(1)} collective-permute-done((s16[1,240,256]{2,1,0:T(8,128)(2,1)S(1)}, s16[1,240,256]{2,1,0:T(8,128)(2,1)S(1)}, u32[]{:S(2)}, u32[]{:S(2)}) %collective-permute-start.18) | collective-permute-done | bytes 122912 | tf_op jit(solution)/shard_map/ppermute | solution.py:80
  73.1 12.0 %collective-permute-start.21 = (s16[4,240,256]{2,1,0:T(8,128)(2,1)S(1)}, s16[4,240,256]{2,1,0:T(8,128)(2,1)S(1)}, u32[]{:S(2)}, u32[]{:S(2)}) collective-permute-start(s16[4,240,256]{2,1,0:T(8,128)(2,1)S(1)} %pad_add_fusion.refs_0_), channel_id=1, source_target_pairs={{0,4},{1,5},{2,6},{3,7},{4,0},{5,1},{6,2},{7,3},{8,12},{9,13},{10,... | collective-permute-start | bytes 1474568 | tf_op jit(solution)/shard_map/ppermute | solution.py:424
  85.1 2.8 %collective-permute-start.22 = (s16[4,240,256]{2,1,0:T(8,128)(2,1)S(1)}, s16[4,240,256]{2,1,0:T(8,128)(2,1)S(1)}, u32[]{:S(2)}, u32[]{:S(2)}) collective-permute-start(s16[4,240,256]{2,1,0:T(8,128)(2,1)S(1)} %pad_add_fusion.refs_0_), channel_id=1, source_target_pairs={{0,33},{1,32},{2,35},{3,34},{4,108},{5,109},{6,110},{7,111},{8,41}... | collective-permute-start | bytes 1474568 | tf_op jit(solution)/shard_map/ppermute | solution.py:80
  87.9 1.1 collective-permute-start.20
  89.0 6.0 %shard_map.92 = bf16[2,8,64,256]{3,2,1,0:T(8,128)(2,1)} custom-call(s32[2]{0:T(128)S(1)} %pad_add_fusion.1.odd, bf16[3,480,160]{2,1,0:T(8,128)(2,1)S(1)} %shard_map.77.pick, bf16[8,8,16,256]{3,2,1,0:T(8,128)(2,1)S(1)} %get-tuple-element.52.grad, bf16[2,8,16,256]{3,2,1,0:T(8,128)(2,1)S(1)} %collective-permute-done.y_a, ...), custom_call_target="tpu_custom_call" | custom-call | flops 3623878656 | bytes 5900296 | tf_op jit(solution)/shard_map/pallas_call | solution.py:89
  94.9 1.9 %shard_map.93.refs_2_ = f32[27,256,256]{2,1,0:T(8,128)} custom-call(s32[6]{0:T(128)S(1)} %stack.33.where, s16[4,240,256]{2,1,0:T(8,128)(2,1)S(1)} %pad_add_fusion.refs_0_, s16[4,240,256]{2,1,0:T(8,128)(2,1)S(1)} %collective-permute-done.21.refs_1_), custom_call_target="tpu_custom_call" | custom-call | bytes 2752512 | tf_op jit(solution)/shard_map/pallas_call | solution.py:221
  96.8 1.5 %collective-permute-done.23.refs_1_ = s16[4,240,256]{2,1,0:T(8,128)(2,1)S(1)} collective-permute-done((s16[4,240,256]{2,1,0:T(8,128)(2,1)S(1)}, s16[4,240,256]{2,1,0:T(8,128)(2,1)S(1)}, u32[]{:S(2)}, u32[]{:S(2)}) %collective-permute-start.23) | collective-permute-done | bytes 491552 | tf_op jit(solution)/shard_map/ppermute | solution.py:80
  98.3 2.1 %collective-permute-done.20.refs_0_ = s16[4,240,256]{2,1,0:T(8,128)(2,1)S(1)} collective-permute-done((s16[4,240,256]{2,1,0:T(8,128)(2,1)S(1)}, s16[4,240,256]{2,1,0:T(8,128)(2,1)S(1)}, u32[]{:S(2)}, u32[]{:S(2)}) %collective-permute-start.20) | collective-permute-done | bytes 491552 | tf_op jit(solution)/shard_map/ppermute | solution.py:80
  101.0 1.9 %shard_map.94.refs_3_ = f32[27,256,256]{2,1,0:T(8,128)} custom-call(s32[6]{0:T(128)S(1)} %stack.33.where, s16[4,240,256]{2,1,0:T(8,128)(2,1)S(1)} %collective-permute-done.22.refs_0_, s16[4,240,256]{2,1,0:T(8,128)(2,1)S(1)} %collective-permute-done.23.refs_1_, f32[27,256,256]{2,1,0:T(8,128)} %shard_map.93.refs_2_), custom_call_target="tpu_custom_call", output_to_operand_aliasing={{}: (3, {})} | custom-call | bytes 2752512 | tf_op jit(solution)/shard_map/pallas_call | solution.py:221
  103.3 2.2 %shard_map.95.refs_1_ = f32[27,256,256]{2,1,0:T(8,128)} custom-call(s32[6]{0:T(128)S(1)} %stack.33.where, s16[4,240,256]{2,1,0:T(8,128)(2,1)S(1)} %collective-permute-done.20.refs_0_, s16[4,240,256]{2,1,0:T(8,128)(2,1)S(1)} %collective-permute-done.25.refs_1_, ...), custom_call_target="tpu_custom_call", output_to_operand_aliasing={{}: (4, {})} | custom-call | bytes 4128768 | tf_op jit(solution)/shard_map/pallas_call | solution.py:221
  105.5 1.5 %shard_map.96 = f32[27,256,256]{2,1,0:T(8,128)} custom-call(s32[6]{0:T(128)S(1)} %stack.33.where, s16[4,240,256]{2,1,0:T(8,128)(2,1)S(1)} %collective-permute-done.24.refs_0_, f32[27,256,256]{2,1,0:T(8,128)} %shard_map.95.refs_1_), custom_call_target="tpu_custom_call", output_to_operand_aliasing={{}: (2, {})} | custom-call | bytes 1376256 | tf_op jit(solution)/shard_map/pallas_call | solution.py:221
  (40 shorter events, 4.3 us)
Async XLA Ops:
  0.7 1.0 copy-start
  1.8 1.0 copy-start.1
  2.8 0.7 copy-start.2
  4.5 4.8 %collective-permute-start = (bf16[2,8,16,256]{3,2,1,0:T(8,128)(2,1)S(1)}, bf16[2,8,16,256]{3,2,1,0:T(8,128)(2,1)S(1)}, u32[]{:S(2)}, u32[]{:S(2)}) collective-permute-start(bf16[2,8,16,256]{3,2,1,0:T(8,128)(2,1)S(1)} %get-tuple-element.30), channel_id=1, source_target_pairs={{0,1},{1,0},{2,3},{3,2},{4,5},{5,4},{6,7},{7,6},{8,9},{9,8},{10,11... | collective-permute-start | bytes 393224 | tf_op jit(solution)/shard_map/ppermute | solution.py:383
  6.7 2.7 %collective-permute-start.1 = (bf16[2,8,16,256]{3,2,1,0:T(8,128)(2,1)S(1)}, bf16[2,8,16,256]{3,2,1,0:T(8,128)(2,1)S(1)}, u32[]{:S(2)}, u32[]{:S(2)}) collective-permute-start(bf16[2,8,16,256]{3,2,1,0:T(8,128)(2,1)S(1)} %get-tuple-element.33), channel_id=1, source_target_pairs={{1,2},{2,1},{5,6},{6,5},{9,10},{10,9},{13,14},{14,13},{17,18},{18,... | collective-permute-start | bytes 393224 | tf_op jit(solution)/shard_map/ppermute | solution.py:383
  10.0 7.7 %collective-permute-start.2 = (bf16[2,10,16,256]{3,2,1,0:T(8,128)(2,1)S(1)}, bf16[2,10,16,256]{3,2,1,0:T(8,128)(2,1)S(1)}, u32[]{:S(2)}, u32[]{:S(2)}) collective-permute-start(bf16[2,10,16,256]{3,2,1,0:T(8,128)(2,1)S(1)} %get-tuple-element.35), channel_id=1, source_target_pairs={{0,4},{4,0},{8,12},{12,8},{16,20},{20,16},{24,28},{28,24},{32,36},... | collective-permute-start | bytes 491528 | tf_op jit(solution)/shard_map/ppermute | solution.py:386
  11.8 6.7 %collective-permute-start.3 = (bf16[2,10,16,256]{3,2,1,0:T(8,128)(2,1)S(1)}, bf16[2,10,16,256]{3,2,1,0:T(8,128)(2,1)S(1)}, u32[]{:S(2)}, u32[]{:S(2)}) collective-permute-start(bf16[2,10,16,256]{3,2,1,0:T(8,128)(2,1)S(1)} %get-tuple-element.36), channel_id=1, source_target_pairs={{4,8},{8,4},{12,16},{16,12},{20,24},{24,20},{28,32},{32,28},{36,40... | collective-permute-start | bytes 491528 | tf_op jit(solution)/shard_map/ppermute | solution.py:386
  15.5 0.7 copy-start.3
  23.4 4.9 %collective-permute-start.8 = (s16[4,240,256]{2,1,0:T(8,128)(2,1)S(1)}, s16[4,240,256]{2,1,0:T(8,128)(2,1)S(1)}, u32[]{:S(2)}, u32[]{:S(2)}) collective-permute-start(s16[4,240,256]{2,1,0:T(8,128)(2,1)S(1)} %get-tuple-element.47), channel_id=1, source_target_pairs={{0,4},{1,5},{2,6},{3,7},{4,0},{5,1},{6,2},{7,3},{8,12},{9,13},{10,... | collective-permute-start | bytes 1474568 | tf_op jit(solution)/shard_map/ppermute | solution.py:400
  23.5 12.8 %copy-start.4 = (bf16[27,256,256]{2,1,0:T(8,128)(2,1)S(1)}, bf16[27,256,256]{2,1,0:T(8,128)(2,1)}, u32[]{:S(2)}) copy-start(bf16[27,256,256]{2,1,0:T(8,128)(2,1)} %kernel.3) | copy-start | bytes 10616836
  23.5 7.0 %collective-permute-start.6 = (s16[4,240,256]{2,1,0:T(8,128)(2,1)S(1)}, s16[4,240,256]{2,1,0:T(8,128)(2,1)S(1)}, u32[]{:S(2)}, u32[]{:S(2)}) collective-permute-start(s16[4,240,256]{2,1,0:T(8,128)(2,1)S(1)} %get-tuple-element.45), channel_id=1, source_target_pairs={{0,4},{1,5},{2,6},{3,7},{4,0},{5,1},{6,2},{7,3},{8,12},{9,13},{10,... | collective-permute-start | bytes 1474568 | tf_op jit(solution)/shard_map/ppermute | solution.py:400
  25.8 9.7 %collective-permute-start.5 = (s16[4,240,256]{2,1,0:T(8,128)(2,1)S(1)}, s16[4,240,256]{2,1,0:T(8,128)(2,1)S(1)}, u32[]{:S(2)}, u32[]{:S(2)}) collective-permute-start(s16[4,240,256]{2,1,0:T(8,128)(2,1)S(1)} %get-tuple-element.40), channel_id=1, source_target_pairs={{0,4},{1,5},{2,6},{3,7},{4,0},{5,1},{6,2},{7,3},{8,12},{9,13},{10,... | collective-permute-start | bytes 1474568 | tf_op jit(solution)/shard_map/ppermute | solution.py:400
  27.8 8.3 %collective-permute-start.4 = (s16[4,240,256]{2,1,0:T(8,128)(2,1)S(1)}, s16[4,240,256]{2,1,0:T(8,128)(2,1)S(1)}, u32[]{:S(2)}, u32[]{:S(2)}) collective-permute-start(s16[4,240,256]{2,1,0:T(8,128)(2,1)S(1)} %get-tuple-element.38), channel_id=1, source_target_pairs={{0,4},{1,5},{2,6},{3,7},{4,0},{5,1},{6,2},{7,3},{8,12},{9,13},{10,... | collective-permute-start | bytes 1474568 | tf_op jit(solution)/shard_map/ppermute | solution.py:400
  28.6 13.7 %collective-permute-start.9 = (s16[4,240,256]{2,1,0:T(8,128)(2,1)S(1)}, s16[4,240,256]{2,1,0:T(8,128)(2,1)S(1)}, u32[]{:S(2)}, u32[]{:S(2)}) collective-permute-start(s16[4,240,256]{2,1,0:T(8,128)(2,1)S(1)} %shard_map.88), channel_id=1, source_target_pairs={{0,1},{1,0},{2,3},{3,2},{4,12},{5,13},{6,14},{7,15},{8,9},{9,8},{1... | collective-permute-start | bytes 1474568 | tf_op jit(solution)/shard_map/ppermute | solution.py:404
  30.9 11.4 %collective-permute-start.7 = (s16[4,240,256]{2,1,0:T(8,128)(2,1)S(1)}, s16[4,240,256]{2,1,0:T(8,128)(2,1)S(1)}, u32[]{:S(2)}, u32[]{:S(2)}) collective-permute-start(s16[4,240,256]{2,1,0:T(8,128)(2,1)S(1)} %shard_map.86), channel_id=1, source_target_pairs={{0,33},{1,32},{2,35},{3,34},{4,108},{5,109},{6,110},{7,111},{8,41}... | collective-permute-start | bytes 1474568 | tf_op jit(solution)/shard_map/ppermute | solution.py:404
  35.8 10.7 %collective-permute-start.10 = (s16[4,240,256]{2,1,0:T(8,128)(2,1)S(1)}, s16[4,240,256]{2,1,0:T(8,128)(2,1)S(1)}, u32[]{:S(2)}, u32[]{:S(2)}) collective-permute-start(s16[4,240,256]{2,1,0:T(8,128)(2,1)S(1)} %shard_map.83), channel_id=1, source_target_pairs={{0,32},{1,33},{2,34},{3,35},{4,100},{5,101},{6,102},{7,103},{8,40}... | collective-permute-start | bytes 1474568 | tf_op jit(solution)/shard_map/ppermute | solution.py:404
  47.1 6.3 %collective-permute-start.11 = (s16[1,240,256]{2,1,0:T(8,128)(2,1)S(1)}, s16[1,240,256]{2,1,0:T(8,128)(2,1)S(1)}, u32[]{:S(2)}, u32[]{:S(2)}) collective-permute-start(s16[1,240,256]{2,1,0:T(8,128)(2,1)S(1)} %get-tuple-element.49), channel_id=1, source_target_pairs={{0,11},{1,10},{2,9},{3,8},{4,37},{5,36},{6,39},{7,38},{8,3},{9,2},... | collective-permute-start | bytes 368648 | tf_op jit(solution)/shard_map/ppermute | solution.py:80
  51.1 3.7 %collective-permute-start.12 = (s16[1,240,256]{2,1,0:T(8,128)(2,1)S(1)}, s16[1,240,256]{2,1,0:T(8,128)(2,1)S(1)}, u32[]{:S(2)}, u32[]{:S(2)}) collective-permute-start(s16[1,240,256]{2,1,0:T(8,128)(2,1)S(1)} %get-tuple-element.50), channel_id=1, source_target_pairs={{0,8},{1,9},{2,10},{3,11},{4,5},{5,4},{6,7},{7,6},{8,0},{9,1},{10,... | collective-permute-start | bytes 368648 | tf_op jit(solution)/shard_map/ppermute | solution.py:80
  51.2 3.7 %collective-permute-start.13 = (s16[1,240,256]{2,1,0:T(8,128)(2,1)S(1)}, s16[1,240,256]{2,1,0:T(8,128)(2,1)S(1)}, u32[]{:S(2)}, u32[]{:S(2)}) collective-permute-start(s16[1,240,256]{2,1,0:T(8,128)(2,1)S(1)} %get-tuple-element.51), channel_id=1, source_target_pairs={{0,3},{1,2},{2,1},{3,0},{4,36},{5,37},{6,38},{7,39},{8,11},{9,10},... | collective-permute-start | bytes 368648 | tf_op jit(solution)/shard_map/ppermute | solution.py:80
  55.1 8.1 %collective-permute-start.14 = (s16[1,240,256]{2,1,0:T(8,128)(2,1)S(1)}, s16[1,240,256]{2,1,0:T(8,128)(2,1)S(1)}, u32[]{:S(2)}, u32[]{:S(2)}) collective-permute-start(s16[1,240,256]{2,1,0:T(8,128)(2,1)S(1)} %shard_map.90.own), channel_id=1, source_target_pairs={{0,120},{1,121},{2,122},{3,123},{4,31},{5,30},{6,29},{7,28},{8,112... | collective-permute-start | bytes 368648 | tf_op jit(solution)/shard_map/ppermute | solution.py:80
  60.9 4.9 %collective-permute-start.15 = (s16[1,240,256]{2,1,0:T(8,128)(2,1)S(1)}, s16[1,240,256]{2,1,0:T(8,128)(2,1)S(1)}, u32[]{:S(2)}, u32[]{:S(2)}) collective-permute-start(s16[1,240,256]{2,1,0:T(8,128)(2,1)S(1)} %shard_map.90.own), channel_id=1, source_target_pairs={{0,96},{1,97},{2,98},{3,99},{4,7},{5,6},{6,5},{7,4},{8,104},{9,105... | collective-permute-start | bytes 368648 | tf_op jit(solution)/shard_map/ppermute | solution.py:80
  61.5 4.9 %collective-permute-start.16 = (s16[1,240,256]{2,1,0:T(8,128)(2,1)S(1)}, s16[1,240,256]{2,1,0:T(8,128)(2,1)S(1)}, u32[]{:S(2)}, u32[]{:S(2)}) collective-permute-start(s16[1,240,256]{2,1,0:T(8,128)(2,1)S(1)} %shard_map.90.own), channel_id=1, source_target_pairs={{0,24},{1,25},{2,26},{3,27},{4,28},{5,29},{6,30},{7,31},{8,16},{9,... | collective-permute-start | bytes 368648 | tf_op jit(solution)/shard_map/ppermute | solution.py:80
  66.7 4.7 %collective-permute-start.17 = (s16[1,240,256]{2,1,0:T(8,128)(2,1)S(1)}, s16[1,240,256]{2,1,0:T(8,128)(2,1)S(1)}, u32[]{:S(2)}, u32[]{:S(2)}) collective-permute-start(s16[1,240,256]{2,1,0:T(8,128)(2,1)S(1)} %shard_map.91), channel_id=1, source_target_pairs={{0,11},{1,10},{2,9},{3,8},{4,37},{5,36},{6,39},{7,38},{8,3},{9,2},... | collective-permute-start | bytes 368648 | tf_op jit(solution)/shard_map/ppermute | solution.py:80
  68.4 4.5 %collective-permute-start.18 = (s16[1,240,256]{2,1,0:T(8,128)(2,1)S(1)}, s16[1,240,256]{2,1,0:T(8,128)(2,1)S(1)}, u32[]{:S(2)}, u32[]{:S(2)}) collective-permute-start(s16[1,240,256]{2,1,0:T(8,128)(2,1)S(1)} %shard_map.91), channel_id=1, source_target_pairs={{0,8},{1,9},{2,10},{3,11},{4,5},{5,4},{6,7},{7,6},{8,0},{9,1},{10,... | collective-permute-start | bytes 368648 | tf_op jit(solution)/shard_map/ppermute | solution.py:80
  69.0 4.0 %collective-permute-start.19 = (s16[1,240,256]{2,1,0:T(8,128)(2,1)S(1)}, s16[1,240,256]{2,1,0:T(8,128)(2,1)S(1)}, u32[]{:S(2)}, u32[]{:S(2)}) collective-permute-start(s16[1,240,256]{2,1,0:T(8,128)(2,1)S(1)} %shard_map.91), channel_id=1, source_target_pairs={{0,3},{1,2},{2,1},{3,0},{4,36},{5,37},{6,38},{7,39},{8,11},{9,10},... | collective-permute-start | bytes 368648 | tf_op jit(solution)/shard_map/ppermute | solution.py:80
  73.1 21.9 %collective-permute-start.21 = (s16[4,240,256]{2,1,0:T(8,128)(2,1)S(1)}, s16[4,240,256]{2,1,0:T(8,128)(2,1)S(1)}, u32[]{:S(2)}, u32[]{:S(2)}) collective-permute-start(s16[4,240,256]{2,1,0:T(8,128)(2,1)S(1)} %pad_add_fusion.refs_0_), channel_id=1, source_target_pairs={{0,4},{1,5},{2,6},{3,7},{4,0},{5,1},{6,2},{7,3},{8,12},{9,13},{10,... | collective-permute-start | bytes 1474568 | tf_op jit(solution)/shard_map/ppermute | solution.py:424
  85.1 13.2 %collective-permute-start.23 = (s16[4,240,256]{2,1,0:T(8,128)(2,1)S(1)}, s16[4,240,256]{2,1,0:T(8,128)(2,1)S(1)}, u32[]{:S(2)}, u32[]{:S(2)}) collective-permute-start(s16[4,240,256]{2,1,0:T(8,128)(2,1)S(1)} %pad_add_fusion.refs_0_), channel_id=1, source_target_pairs={{0,1},{1,0},{2,3},{3,2},{4,12},{5,13},{6,14},{7,15},{8,9},{9,8},{1... | collective-permute-start | bytes 1474568 | tf_op jit(solution)/shard_map/ppermute | solution.py:80
  85.1 13.2 %collective-permute-start.22 = (s16[4,240,256]{2,1,0:T(8,128)(2,1)S(1)}, s16[4,240,256]{2,1,0:T(8,128)(2,1)S(1)}, u32[]{:S(2)}, u32[]{:S(2)}) collective-permute-start(s16[4,240,256]{2,1,0:T(8,128)(2,1)S(1)} %pad_add_fusion.refs_0_), channel_id=1, source_target_pairs={{0,33},{1,32},{2,35},{3,34},{4,108},{5,109},{6,110},{7,111},{8,41}... | collective-permute-start | bytes 1474568 | tf_op jit(solution)/shard_map/ppermute | solution.py:80
  87.9 12.6 %collective-permute-start.20 = (s16[4,240,256]{2,1,0:T(8,128)(2,1)S(1)}, s16[4,240,256]{2,1,0:T(8,128)(2,1)S(1)}, u32[]{:S(2)}, u32[]{:S(2)}) collective-permute-start(s16[4,240,256]{2,1,0:T(8,128)(2,1)S(1)} %pad_add_fusion.refs_0_), channel_id=1, source_target_pairs={{0,32},{1,33},{2,34},{3,35},{4,100},{5,101},{6,102},{7,103},{8,40}... | collective-permute-start | bytes 1474568 | tf_op jit(solution)/shard_map/ppermute | solution.py:80
  100.5 2.8 %collective-permute-start.26 = (s16[4,240,256]{2,1,0:T(8,128)(2,1)S(1)}, s16[4,240,256]{2,1,0:T(8,128)(2,1)S(1)}, u32[]{:S(2)}, u32[]{:S(2)}) collective-permute-start(s16[4,240,256]{2,1,0:T(8,128)(2,1)S(1)} %collective-permute-done.23.refs_1_), channel_id=1, source_target_pairs={{0,4},{1,5},{2,6},{3,7},{4,0},{5,1},{6,2},{7,3},{8,12},{9,13},{10,... | collective-permute-start | bytes 1474568 | tf_op jit(solution)/shard_map/ppermute | solution.py:427
  100.8 2.5 %collective-permute-start.25 = (s16[4,240,256]{2,1,0:T(8,128)(2,1)S(1)}, s16[4,240,256]{2,1,0:T(8,128)(2,1)S(1)}, u32[]{:S(2)}, u32[]{:S(2)}) collective-permute-start(s16[4,240,256]{2,1,0:T(8,128)(2,1)S(1)} %collective-permute-done.22.refs_0_), channel_id=1, source_target_pairs={{0,4},{1,5},{2,6},{3,7},{4,0},{5,1},{6,2},{7,3},{8,12},{9,13},{10,... | collective-permute-start | bytes 1474568 | tf_op jit(solution)/shard_map/ppermute | solution.py:427
  102.9 2.6 %collective-permute-start.24 = (s16[4,240,256]{2,1,0:T(8,128)(2,1)S(1)}, s16[4,240,256]{2,1,0:T(8,128)(2,1)S(1)}, u32[]{:S(2)}, u32[]{:S(2)}) collective-permute-start(s16[4,240,256]{2,1,0:T(8,128)(2,1)S(1)} %collective-permute-done.20.refs_0_), channel_id=1, source_target_pairs={{0,4},{1,5},{2,6},{3,7},{4,0},{5,1},{6,2},{7,3},{8,12},{9,13},{10,... | collective-permute-start | bytes 1474568 | tf_op jit(solution)/shard_map/ppermute | solution.py:429

commit v3 on v2

--- a/solution.py
+++ b/solution.py
@@ -23,12 +23,13 @@
 VMEM = pl.BlockSpec(memory_space=pltpu.VMEM)
 HBM = pl.BlockSpec(memory_space=pltpu.HBM)
 SMEM = pl.BlockSpec(memory_space=pltpu.SMEM)
+FREE = pl.CostEstimate(flops=0, bytes_accessed=0, transcendentals=0)
 PARAMS = pltpu.CompilerParams(vmem_limit_bytes=28 * 2**20)
 
 FIRST, SECOND = 0, 1
 GROUPS = (
-    ((("x", FIRST), ("y", FIRST)), (("z", FIRST), ("x", SECOND)), (("y", SECOND), ("z", SECOND))),
     ((("z", FIRST), ("y", SECOND)), (("x", FIRST), ("y", FIRST)), (("x", SECOND), ("z", SECOND))),
+    ((("x", SECOND), ("y", FIRST)), (("x", FIRST), ("z", FIRST)), (("y", SECOND), ("z", SECOND))),
 )
 
 
@@ -76,24 +77,25 @@
     return jnp.where(core == 0, ranks[0], ranks[1])
 
 
-def exchange(arrays, level):
-    return [lax.ppermute(a, BOTH, partners(level, m + 1)) for m, a in enumerate(arrays)]
+def exchange(arrays, level, order=(1, 2, 3)):
+    got = {m: lax.ppermute(arrays[m - 1], BOTH, partners(level, m)) for m in order}
+    return [got[1], got[2], got[3]]
 
 
 def after(value, *others):
     return lax.optimization_barrier((value, *others))[0]
 
 
-def call(kernel, outs, *args, flops=0, scratch=(), space=None):
-    size = sum(a.size * a.dtype.itemsize for a in args) + sum(o.size * o.dtype.itemsize for o in outs)
+def call(kernel, outs, *args, scratch=(), aliases=None):
     return pl.pallas_call(
         kernel,
         out_shape=list(outs),
-        in_specs=[SMEM if a.dtype == jnp.int32 and a.size < 100 else space or VMEM for a in args],
+        in_specs=[SMEM if a.dtype == jnp.int32 and a.size < 100 else VMEM for a in args],
         out_specs=[VMEM] * len(outs),
         scratch_shapes=list(scratch),
+        input_output_aliases=aliases or {},
         compiler_params=PARAMS,
-        cost_estimate=pl.CostEstimate(flops=flops, bytes_accessed=size, transcendentals=0),
+        cost_estimate=FREE,
     )(*args)
 
 
@@ -226,18 +228,19 @@
         scratch_shapes=[pltpu.VMEM((n, EACH, HALF, C), jnp.float32), pltpu.SemaphoreType.DMA((n, EACH))],
         input_output_aliases={1 + n: 0} if more else {},
         compiler_params=PARAMS,
-        cost_estimate=pl.CostEstimate(flops=0, bytes_accessed=n * EACH * HALF * C * 6, transcendentals=0),
+        cost_estimate=FREE,
     )(where, *sets, *more)
 
 
-def prepare_kernel(odd, features, cotangent, occupancy, cells, grad, masks, y_a, y_b):
+def prepare_kernel(odd, features, cotangent, occupancy, cells, grad, masks, x_a, x_b, y_a, y_b):
     r = lax.broadcasted_iota(jnp.int32, (128, 128), 0)
     c = lax.broadcasted_iota(jnp.int32, (128, 128), 1)
     same = (r >> 4 == (c >> 3) & 7) & ((r >> 3) & 1 == c >> 6) & (r & 7 == c & 7)
     low = lax.broadcasted_iota(jnp.int32, (1, 128), 1) < 64
     occupied = occupancy[...].astype(jnp.float32)
     turned = pltpu.roll(occupied, 64, 1)
-    even = odd[0] == 0
+    even, core_0 = odd[0] == 0, odd[1] == 0
+    ends = {}
     for x in range(8):
         lanes = slice(128 * (x // 2), 128 * (x // 2) + 128)
         if x % 2 == 0:
@@ -254,6 +257,10 @@
             out[x] = made
             y_a[index, x] = jnp.where(even, made[7], made[0])
             y_b[index, x] = jnp.where(even, made[0], made[7])
+            ends[index, x] = made
+    for index in range(2):
+        x_a[index] = jnp.where(core_0, ends[index, 7], ends[index, 0])
+        x_b[index] = jnp.where(core_0, ends[index, 0], ends[index, 7])
 
 
 def picks_kernel(neighbors, out):
@@ -277,35 +284,45 @@
             out[ox, 160 * oz : 160 * (oz + 1), :] = jnp.where(hit, 1.0, 0.0).astype(jnp.bfloat16)
 
 
-def edges_kernel(odd, cells, grad, y_a, y_b, x_a, x_b):
+def corners_kernel(odd, x_a, x_b, c_a, c_b):
     even = odd[0] == 0
-    for out, x in ((x_a, jnp.where(odd[1] == 0, 7, 0)), (x_b, jnp.where(odd[1] == 0, 0, 7))):
-        for i, a in enumerate((cells, grad)):
-            out[i, 0] = jnp.where(even, y_b[i, x], y_a[i, x])
-            out[i, 1:9] = a[x]
-            out[i, 9] = jnp.where(even, y_a[i, x], y_b[i, x])
-
-
-def widen(index, odd, pick, cells, y_a, y_b, x_a, x_b, wide):
+    for side, x in enumerate((x_a, x_b)):
+        for index in range(2):
+            c_a[side, index] = jnp.where(even, x[index, 7], x[index, 0])
+            c_b[side, index] = jnp.where(even, x[index, 0], x[index, 7])
+
+
+def spread(pick, layer, x, wide):
+    moved = jnp.dot(pick, layer, preferred_element_type=jnp.float32).astype(jnp.bfloat16)
+    for oz in range(3):
+        wide[oz, x] = moved[160 * oz : 160 * (oz + 1)].reshape(10, 16, C)
+
+
+def widen_inner(index, odd, pick, cells, y_a, y_b, wide):
+    even = odd[0] == 0
+    for x in range(8):
+        a, b = y_a[index, x], y_b[index, x]
+        layer = [jnp.where(even, b, a), cells[x].reshape(128, C), jnp.where(even, a, b)]
+        spread(pick[1], jnp.concatenate(layer, axis=0), x + 1, wide)
+
+
+def widen_outer(index, odd, pick, x_a, x_b, c_a, c_b, wide):
     even, core_0 = odd[0] == 0, odd[1] == 0
-    for x in range(10):
-        if x == 0:
-            layer, side = jnp.where(core_0, x_b[index], x_a[index]).reshape(160, C), 0
-        elif x == 9:
-            layer, side = jnp.where(core_0, x_a[index], x_b[index]).reshape(160, C), 2
-        else:
-            a, b = y_a[index, x - 1], y_b[index, x - 1]
-            layer = jnp.concatenate(
-                [jnp.where(even, b, a), cells[x - 1].reshape(128, C), jnp.where(even, a, b)], axis=0
-            )
-            side = 1
-        moved = jnp.dot(pick[side], layer, preferred_element_type=jnp.float32).astype(jnp.bfloat16)
-        for oz in range(3):
-            wide[oz, x] = moved[160 * oz : 160 * (oz + 1)].reshape(10, 16, C)
-
-
-def widen_kernel(odd, pick, cells, y_a, y_b, x_a, x_b, wide):
-    widen(0, odd, pick, cells, y_a, y_b, x_a, x_b, wide)
+    layers = []
+    for side, x in enumerate((x_a, x_b)):
+        a, b = c_a[side, index], c_b[side, index]
+        rows = [jnp.where(even, b, a), x[index].reshape(128, C), jnp.where(even, a, b)]
+        layers.append(jnp.concatenate(rows, axis=0))
+    spread(pick[0], jnp.where(core_0, layers[1], layers[0]), 0, wide)
+    spread(pick[2], jnp.where(core_0, layers[0], layers[1]), 9, wide)
+
+
+def inner_kernel(odd, pick, cells, y_a, y_b, wide):
+    widen_inner(0, odd, pick, cells, y_a, y_b, wide)
+
+
+def outer_kernel(odd, pick, x_a, x_b, c_a, c_b, _, wide):
+    widen_outer(0, odd, pick, x_a, x_b, c_a, c_b, wide)
 
 
 def part_kernel(member, where, wide, grad, own, coded, terms):
@@ -352,8 +369,9 @@
     convolve(False, wide, kernel, masks, out, sums)
 
 
-def backward_kernel(odd, pick, grad, y_a, y_b, x_a, x_b, kernel, masks, out, sums, wide):
-    widen(1, odd, pick, grad, y_a, y_b, x_a, x_b, wide)
+def backward_kernel(odd, pick, grad, y_a, y_b, x_a, x_b, c_a, c_b, kernel, masks, out, sums, wide):
+    widen_inner(1, odd, pick, grad, y_a, y_b, wide)
+    widen_outer(1, odd, pick, x_a, x_b, c_a, c_b, wide)
     convolve(True, wide, kernel, masks, out, sums)
 
 
@@ -373,62 +391,69 @@
 
     column = shape((8, 8, 16, C), jnp.bfloat16)
     wide_shape = (3, 10, 10, 16, C)
-    side_y = shape((2, 8, 16, C), jnp.bfloat16)
-    side_x = shape((2, 10, 16, C), jnp.bfloat16)
-    cells, grad, masks, *sides = call(
+    side = shape((2, 8, 16, C), jnp.bfloat16)
+    corner = shape((2, 2, 16, C), jnp.bfloat16)
+
+    def swap(arrays, axis, pairs):
+        return [lax.ppermute(a, axis, p) for a, p in zip(arrays, pairs)]
+
+    cells, grad, masks, x_a, x_b, y_a, y_b = call(
         prepare_kernel,
-        [column, column, shape((8, 128, 128), jnp.bfloat16)] + [side_y] * 2,
+        [column, column, shape((8, 128, 128), jnp.bfloat16)] + [side] * 4,
         odd, features.reshape(2, 8, 64, C), cotangent.reshape(2, 8, 64, C), occupancy,
     )
-    y_halo = [lax.ppermute(a, "gy", pairs) for a, pairs in zip(sides, y_pairs)]
-    (pick,) = call(picks_kernel, [shape((3, 480, 160), jnp.bfloat16)], after(neighbors, sides[0]))
-    edges = call(edges_kernel, [side_x, side_x], odd, cells, grad, *y_halo)
-    x_halo = [lax.ppermute(a, "gx", pairs) for a, pairs in zip(edges, x_pairs)]
-    (wide,) = call(widen_kernel, [shape(wide_shape, jnp.bfloat16)], odd, pick, cells, *y_halo, *x_halo)
-
-    flops = 2 * K * 1024 * C * C
+    x_halo = swap((x_a, x_b), "gx", x_pairs)
+    y_halo = swap((after(y_a, x_halo[0]), after(y_b, x_halo[0])), "gy", y_pairs)
+    (pick,) = call(picks_kernel, [shape((3, 480, 160), jnp.bfloat16)], after(neighbors, x_halo[0]))
+    corners = swap(call(corners_kernel, [corner, corner], odd, *x_halo), "gy", y_pairs)
+    (wide,) = call(inner_kernel, [shape(wide_shape, jnp.bfloat16)], odd, pick, cells, *y_halo)
+    halo = (*x_halo, *corners)
+    (wide,) = call(outer_kernel, [shape(wide_shape, jnp.bfloat16)], odd, pick, *halo, wide, aliases={6: 0})
+
     sums = {}
     got = {}
+    before = []
     for m in (1, 2, 3, 0):
         own, coded = call(
             functools.partial(part_kernel, m),
             [shape((EACH * HALF, C), jnp.float32), CODED_4],
-            where, wide, grad,
-            flops=flops // 4,
+            where, after(wide, *before), grad,
             scratch=[pltpu.VMEM((EACH * HALF, C), jnp.float32)],
         )
         other = lax.ppermute(coded, BOTH, other_core())
         out = CODED_4 if m else shape((4, ROWS, C), jnp.float32)
         (sums[m],) = call(functools.partial(pair_sum_kernel, m == 0), [out], own, other)
+        before = [own] + list(sums.values())[-2:-1]
         if m:
             got[m] = lax.ppermute(sums[m], BOTH, partners(0, m))
 
     brick_rows = shape((2, 8, 64, C), jnp.bfloat16)
     totals = pltpu.VMEM((1024, C), jnp.bfloat16)
     (forward,) = call(
-        forward_kernel, [brick_rows], after(wide, sums[0], sums[3]), kernel, masks, flops=flops, scratch=[totals]
+        forward_kernel, [brick_rows], after(wide, sums[0], sums[3]), kernel, masks, scratch=[totals]
+    )
+    (backward,) = call(
+        backward_kernel, [brick_rows], odd, pick, after(grad, forward), *y_halo, *halo, kernel, masks,
+        scratch=[totals, pltpu.VMEM(wide_shape, jnp.bfloat16)],
     )
     keep, *sent = call(
         group_sum_kernel,
         [shape((1, ROWS, C), jnp.float32)] + [CODED_1] * 3,
-        inner.reshape(1).astype(jnp.int32), after(sums[0], forward), got[1], got[2], got[3],
+        inner.reshape(1).astype(jnp.int32), after(sums[0], backward), got[1], got[2], got[3],
     )
     (part,) = call(last_group_kernel, [CODED_1], keep, *exchange(sent, 1))
-    (whole,) = call(total_kernel, [CODED_1], part, *exchange([part] * 3, 2))
-    four = jnp.concatenate([whole] + exchange([whole] * 3, 1))
+    (whole,) = call(total_kernel, [CODED_1], part, *exchange([part] * 3, 2, (2, 3, 1)))
+    four = jnp.concatenate([whole] + exchange([whole] * 3, 1, (2, 3, 1)))
     sets = [four] + exchange([four] * 3, 0)
-    (backward,) = call(
-        backward_kernel, [brick_rows], odd, pick, after(grad, four), *y_halo, *x_halo, kernel, masks,
-        flops=flops, scratch=[totals, pltpu.VMEM(wide_shape, jnp.bfloat16)],
-    )
-    others = [lax.ppermute(sets[0], BOTH, other_core())]
-    done = finish(scale, where, [(0, 0), (1, 0)], [sets[0], others[0]], None)
-    sets[1:] = [after(s, backward, done) for s in sets[1:]]
-    others += [lax.ppermute(s, BOTH, other_core()) for s in sets[1:3]]
-    done = finish(scale, where, [(0, 1), (0, 2)], sets[1:3], done)
-    others.append(lax.ppermute(after(sets[3], done), BOTH, other_core()))
-    done = finish(scale, where, [(0, 3), (1, 1), (1, 2)], [sets[3], *others[1:3]], done)
-    done = finish(scale, where, [(1, 3)], others[3:], done)
+
+    def other(a):
+        return lax.ppermute(a, BOTH, other_core())
+
+    done = finish(scale, where, [(0, 0)], [four], None)
+    *own, done = lax.optimization_barrier((*sets, done))
+    far = [other(a) for a in own]
+    done = finish(scale, where, [(0, 1), (0, 2), (0, 3)], own[1:], done)
+    done = finish(scale, where, [(1, 0), (1, 1), (1, 2), (1, 3)], far, done)
     return forward.reshape(2, 8, 8, 8, C), backward.reshape(2, 8, 8, 8, C), done
 
 

time: 107 us -> 101 us (0.944)
  starting transfers between devices: 47.2 us -> 38 us
  waiting for transfers between devices: 23.3 us -> 26.7 us
    ppermute x20 -> x22, starting transfers between devices: 39.2 us -> 30.1 us  [the longest x12 15.9 us: exchange(): lax.ppermute(arrays[m - 1], BOTH, partners(level, m))]
    ppermute x20 -> x22, waiting for transfers between devices: 17.9 us -> 24.7 us  [the longest x12 23.8 us: exchange(): lax.ppermute(arrays[m - 1], BOTH, partners(level, m))]
    ppermute x3, waiting for transfers between devices: 5.48 us -> 2.02 us  [shards(): got[m] = lax.ppermute(sums[m], BOTH, partners(0, m))]
    pallas_call x4 -> x3, Pallas kernels: 7.51 us -> 6.33 us  [finish(): pl.pallas_call(functools.partial(finish_kernel, scale, parts), out_shape=...]
    pallas_call x17 -> x18, Pallas kernels: 24.4 us -> 25 us  [call(): pl.pallas_call(kernel, out_shape=list(outs), in_specs=[SMEM if a.dtype ==...]
  transfers between devices with their start and end apart: 27 -> 29, of which waited for: 14 -> 13; matrix products, arithmetic and copies ran while one was open for 0% -> 0% of each run, Pallas kernels for 21% -> 24%
where the time goes in v3:
time: 101 us
  starting transfers between devices  38 us (38%)
  Pallas kernels  31.4 us (31%)
  waiting for transfers between devices  26.7 us (26%)
  local copies, waits for them, and re-layouts  3.54 us (4%)
  between operations  1.14 us (1%)
    pallas_call x18, Pallas kernels, call(): pl.pallas_call(kernel, out_shape=list(outs), in_specs=[SMEM if a.dtype ==...  25 us
    ppermute x12, waiting for transfers between devices, exchange(): lax.ppermute(arrays[m - 1], BOTH, partners(level, m))  23.8 us
    ppermute x12, starting transfers between devices, exchange(): lax.ppermute(arrays[m - 1], BOTH, partners(level, m))  15.9 us
    ppermute x6, starting transfers between devices, swap(): return [lax.ppermute(a, axis, p) for a, p in zip(arrays, pairs)]  10.2 us
    ppermute x3, starting transfers between devices, shards(): got[m] = lax.ppermute(sums[m], BOTH, partners(0, m))  6.59 us
    pallas_call x3, Pallas kernels, finish(): pl.pallas_call(functools.partial(finish_kernel, scale, parts), out_shape=...  6.33 us
    ppermute x4, starting transfers between devices, other(): return lax.ppermute(a, BOTH, other_core())  3.96 us
    unnamed x10, local copies, waits for them, and re-layouts  3.46 us
  transfers between devices with their start and end apart: 29, of which 13 were waited for; matrix products, arithmetic and copies ran while one was open for 0% of the time, Pallas kernels for 24%

profile of v3, /device:TPU:1, one launch (start us, length us, event | category | flops | bytes accessed | tf_op | source)
XLA Modules:
  0.0 100.9 jit_solution(1026850345276655884)
XLA Ops:
  0.7 1.0 %copy-done.1 = bf16[2,8,8,8,256]{4,3,2,1,0:T(8,128)(2,1)S(1)} copy-done((bf16[2,8,8,8,256]{4,3,2,1,0:T(8,128)(2,1)S(1)}, bf16[2,8,8,8,256]{4,3,2,1,0:T(8,128)(2,1)}, u32[]{:S(2)}) %copy-start.1) | copy-done | bytes 524312
  1.8 1.0 %copy-done.2 = bf16[2,8,8,8,256]{4,3,2,1,0:T(8,128)(2,1)S(1)} copy-done((bf16[2,8,8,8,256]{4,3,2,1,0:T(8,128)(2,1)S(1)}, bf16[2,8,8,8,256]{4,3,2,1,0:T(8,128)(2,1)}, u32[]{:S(2)}) %copy-start.2) | copy-done | bytes 524312
  2.8 0.7 copy-done.3
  3.5 1.0 %shard_map.76 = (bf16[8,8,16,256]{3,2,1,0:T(8,128)(2,1)S(1)}, bf16[8,8,16,256]{3,2,1,0:T(8,128)(2,1)S(1)}, bf16[8,128,128]{2,1,0:T(8,128)(2,1)S(1)}, bf16[2,8,16...) custom-call(s32[2]{0:T(128)S(1)} %pad_add_fusion.1.odd, ...), custom_call_target="tpu_custom_call" | custom-call | tf_op jit(solution)/shard_map/pallas_call | solution.py:90
  4.5 1.5 %collective-permute-start = (bf16[2,8,16,256]{3,2,1,0:T(8,128)(2,1)S(1)}, bf16[2,8,16,256]{3,2,1,0:T(8,128)(2,1)S(1)}, u32[]{:S(2)}, u32[]{:S(2)}) collective-permute-start(bf16[2,8,16,256]{3,2,1,0:T(8,128)(2,1)S(1)} %get-tuple-element.38), channel_id=1, source_target_pairs={{0,4},{4,0},{8,12},{12,8},{16,20},{20,16},{24,28},{28,24},{32,36},... | collective-permute-start | bytes 393224 | tf_op jit(solution)/shard_map/ppermute | solution.py:398
  6.0 3.5 %collective-permute-start.1 = (bf16[2,8,16,256]{3,2,1,0:T(8,128)(2,1)S(1)}, bf16[2,8,16,256]{3,2,1,0:T(8,128)(2,1)S(1)}, u32[]{:S(2)}, u32[]{:S(2)}) collective-permute-start(bf16[2,8,16,256]{3,2,1,0:T(8,128)(2,1)S(1)} %get-tuple-element.40), channel_id=1, source_target_pairs={{4,8},{8,4},{12,16},{16,12},{20,24},{24,20},{28,32},{32,28},{36,40... | collective-permute-start | bytes 393224 | tf_op jit(solution)/shard_map/ppermute | solution.py:398
  9.6 0.7 collective-permute-start.5
  10.3 3.7 %collective-permute-start.4 = (bf16[2,8,16,256]{3,2,1,0:T(8,128)(2,1)S(1)}, bf16[2,8,16,256]{3,2,1,0:T(8,128)(2,1)S(1)}, u32[]{:S(2)}, u32[]{:S(2)}) collective-permute-start(bf16[2,8,16,256]{3,2,1,0:T(8,128)(2,1)S(1)} %get-tuple-element.45), channel_id=1, source_target_pairs={{0,1},{1,0},{2,3},{3,2},{4,5},{5,4},{6,7},{7,6},{8,9},{9,8},{10,11... | collective-permute-start | bytes 393224 | tf_op jit(solution)/shard_map/ppermute | solution.py:398
  14.7 0.7 collective-permute-start.3
  15.5 0.7 copy-done.4
  16.2 1.3 %shard_map.77.pick = bf16[3,480,160]{2,1,0:T(8,128)(2,1)S(1)} custom-call(s32[2,27]{1,0:T(2,128)S(1)} %copy-done.4), custom_call_target="tpu_custom_call" | custom-call | tf_op jit(solution)/shard_map/pallas_call | solution.py:90
  17.5 1.2 %shard_map.79._ = bf16[3,10,10,16,256]{4,3,2,1,0:T(8,128)(2,1)S(1)} custom-call(s32[2]{0:T(128)S(1)} %pad_add_fusion.1.odd, bf16[3,480,160]{2,1,0:T(8,128)(2,1)S(1)} %shard_map.77.pick, bf16[8,8,16,256]{3,2,1,0:T(8,128)(2,1)S(1)} %get-tuple-element.43.cells, bf16[2,8,16,256]{3,2,1,0:T(8,128)(2,1)S(1)} %collective-permute-done.4.y_a, ...), custom_call_target="tpu_custom_call" | custom-call | tf_op jit(solution)/shard_map/pallas_call | solution.py:90
  18.8 0.8 shard_map.80.wide
  19.6 1.8 %shard_map.81 = (f32[896,256]{1,0:T(8,128)S(1)}, s16[4,240,256]{2,1,0:T(8,128)(2,1)S(1)}) custom-call(s32[6]{0:T(128)S(1)} %stack.33.where, bf16[3,10,10,16,256]{4,3,2,1,0:T(8,128)(2,1)S(1)} %shard_map.80.wide, bf16[8,8,16,256]{3,2,1,0:T(8,128)(2,1)S(1)} %get-tuple-element.62.grad), custom_call_target="tpu_custom_call" | custom-call | tf_op jit(solution)/shard_map/pallas_call | solution.py:90
  21.5 1.8 %shard_map.82 = (f32[896,256]{1,0:T(8,128)S(1)}, s16[4,240,256]{2,1,0:T(8,128)(2,1)S(1)}) custom-call(s32[6]{0:T(128)S(1)} %stack.33.where, bf16[3,10,10,16,256]{4,3,2,1,0:T(8,128)(2,1)S(1)} %shard_map.80.wide, bf16[8,8,16,256]{3,2,1,0:T(8,128)(2,1)S(1)} %get-tuple-element.62.grad), custom_call_target="tpu_custom_call" | custom-call | tf_op jit(solution)/shard_map/pallas_call | solution.py:90
  23.3 0.6 collective-permute-start.7
  24.2 1.8 %shard_map.84 = (f32[896,256]{1,0:T(8,128)S(1)}, s16[4,240,256]{2,1,0:T(8,128)(2,1)S(1)}) custom-call(s32[6]{0:T(128)S(1)} %stack.33.where, bf16[3,10,10,16,256]{4,3,2,1,0:T(8,128)(2,1)S(1)} %shard_map.80.wide, bf16[8,8,16,256]{3,2,1,0:T(8,128)(2,1)S(1)} %get-tuple-element.62.grad), custom_call_target="tpu_custom_call" | custom-call | tf_op jit(solution)/shard_map/pallas_call | solution.py:90
  26.5 1.8 %shard_map.86 = (f32[896,256]{1,0:T(8,128)S(1)}, s16[4,240,256]{2,1,0:T(8,128)(2,1)S(1)}) custom-call(s32[6]{0:T(128)S(1)} %stack.33.where, bf16[3,10,10,16,256]{4,3,2,1,0:T(8,128)(2,1)S(1)} %shard_map.80.wide, bf16[8,8,16,256]{3,2,1,0:T(8,128)(2,1)S(1)} %get-tuple-element.62.grad), custom_call_target="tpu_custom_call" | custom-call | tf_op jit(solution)/shard_map/pallas_call | solution.py:90
  28.3 0.6 collective-permute-start.8
  28.9 1.7 %collective-permute-start.11 = (s16[4,240,256]{2,1,0:T(8,128)(2,1)S(1)}, s16[4,240,256]{2,1,0:T(8,128)(2,1)S(1)}, u32[]{:S(2)}, u32[]{:S(2)}) collective-permute-start(s16[4,240,256]{2,1,0:T(8,128)(2,1)S(1)} %shard_map.85), channel_id=1, source_target_pairs={{0,8},{1,9},{2,10},{3,11},{4,7},{5,6},{6,5},{7,4},{8,0},{9,1},{10,... | collective-permute-start | bytes 1474568 | tf_op jit(solution)/shard_map/ppermute | solution.py:428
  30.5 4.6 %collective-permute-start.10 = (s16[4,240,256]{2,1,0:T(8,128)(2,1)S(1)}, s16[4,240,256]{2,1,0:T(8,128)(2,1)S(1)}, u32[]{:S(2)}, u32[]{:S(2)}) collective-permute-start(s16[4,240,256]{2,1,0:T(8,128)(2,1)S(1)} %shard_map.83), channel_id=1, source_target_pairs={{0,104},{1,105},{2,106},{3,107},{4,39},{5,38},{6,37},{7,36},{8,96}... | collective-permute-start | bytes 1474568 | tf_op jit(solution)/shard_map/ppermute | solution.py:428
  36.0 4.8 %shard_map.89 = bf16[2,8,64,256]{3,2,1,0:T(8,128)(2,1)} custom-call(bf16[3,10,10,16,256]{4,3,2,1,0:T(8,128)(2,1)S(1)} %shard_map.80.wide, bf16[27,256,256]{2,1,0:T(8,128)(2,1)S(1)} %copy-done, bf16[8,128,128]{2,1,0:T(8,128)(2,1)S(1)} %get-tuple-element.61.masks), custom_call_target="tpu_custom_call" | custom-call | tf_op jit(solution)/shard_map/pallas_call | solution.py:90
  40.8 6.0 %shard_map.90 = bf16[2,8,64,256]{3,2,1,0:T(8,128)(2,1)} custom-call(s32[2]{0:T(128)S(1)} %pad_add_fusion.1.odd, bf16[3,480,160]{2,1,0:T(8,128)(2,1)S(1)} %shard_map.77.pick, bf16[8,8,16,256]{3,2,1,0:T(8,128)(2,1)S(1)} %get-tuple-element.62.grad, bf16[2,8,16,256]{3,2,1,0:T(8,128)(2,1)S(1)} %collective-permute-done.4.y_a, ...), custom_call_target="tpu_custom_call" | custom-call | tf_op jit(solution)/shard_map/pallas_call | solution.py:90
  46.8 2.0 %collective-permute-done.12.got_3 = s16[4,240,256]{2,1,0:T(8,128)(2,1)S(1)} collective-permute-done((s16[4,240,256]{2,1,0:T(8,128)(2,1)S(1)}, s16[4,240,256]{2,1,0:T(8,128)(2,1)S(1)}, u32[]{:S(2)}, u32[]{:S(2)}) %collective-permute-start.12) | collective-permute-done | bytes 491552 | tf_op jit(solution)/shard_map/ppermute | solution.py:428
  48.8 0.6 shard_map.91
  49.4 1.0 collective-permute-start.13
  50.4 1.5 %collective-permute-start.14 = (s16[1,240,256]{2,1,0:T(8,128)(2,1)S(1)}, s16[1,240,256]{2,1,0:T(8,128)(2,1)S(1)}, u32[]{:S(2)}, u32[]{:S(2)}) collective-permute-start(s16[1,240,256]{2,1,0:T(8,128)(2,1)S(1)} %get-tuple-element.66), channel_id=1, source_target_pairs={{0,1},{1,0},{2,3},{3,2},{4,5},{5,4},{6,7},{7,6},{8,9},{9,8},{10,11... | collective-permute-start | bytes 368648 | tf_op jit(solution)/shard_map/ppermute | solution.py:81
  51.8 1.1 %collective-permute-start.15 = (s16[1,240,256]{2,1,0:T(8,128)(2,1)S(1)}, s16[1,240,256]{2,1,0:T(8,128)(2,1)S(1)}, u32[]{:S(2)}, u32[]{:S(2)}) collective-permute-start(s16[1,240,256]{2,1,0:T(8,128)(2,1)S(1)} %get-tuple-element.67), channel_id=1, source_target_pairs={{0,32},{1,33},{2,34},{3,35},{4,12},{5,13},{6,14},{7,15},{8,40},{9,... | collective-permute-start | bytes 368648 | tf_op jit(solution)/shard_map/ppermute | solution.py:81
  52.9 1.4 %collective-permute-done.13.got_1 = s16[1,240,256]{2,1,0:T(8,128)(2,1)S(1)} collective-permute-done((s16[1,240,256]{2,1,0:T(8,128)(2,1)S(1)}, s16[1,240,256]{2,1,0:T(8,128)(2,1)S(1)}, u32[]{:S(2)}, u32[]{:S(2)}) %collective-permute-start.13) | collective-permute-done | bytes 122912 | tf_op jit(solution)/shard_map/ppermute | solution.py:81
  54.4 2.9 %collective-permute-done.14.got_2 = s16[1,240,256]{2,1,0:T(8,128)(2,1)S(1)} collective-permute-done((s16[1,240,256]{2,1,0:T(8,128)(2,1)S(1)}, s16[1,240,256]{2,1,0:T(8,128)(2,1)S(1)}, u32[]{:S(2)}, u32[]{:S(2)}) %collective-permute-start.14) | collective-permute-done | bytes 122912 | tf_op jit(solution)/shard_map/ppermute | solution.py:81
  57.5 5.1 %collective-permute-start.16 = (s16[1,240,256]{2,1,0:T(8,128)(2,1)S(1)}, s16[1,240,256]{2,1,0:T(8,128)(2,1)S(1)}, u32[]{:S(2)}, u32[]{:S(2)}) collective-permute-start(s16[1,240,256]{2,1,0:T(8,128)(2,1)S(1)} %shard_map.92.own), channel_id=1, source_target_pairs={{0,27},{1,26},{2,25},{3,24},{4,124},{5,125},{6,126},{7,127},{8,19}... | collective-permute-start | bytes 368648 | tf_op jit(solution)/shard_map/ppermute | solution.py:81
  62.6 0.6 collective-permute-start.17
  63.2 1.7 %collective-permute-done.16.got_1 = s16[1,240,256]{2,1,0:T(8,128)(2,1)S(1)} collective-permute-done((s16[1,240,256]{2,1,0:T(8,128)(2,1)S(1)}, s16[1,240,256]{2,1,0:T(8,128)(2,1)S(1)}, u32[]{:S(2)}, u32[]{:S(2)}) %collective-permute-start.16) | collective-permute-done | bytes 122912 | tf_op jit(solution)/shard_map/ppermute | solution.py:81
  64.8 3.0 %collective-permute-done.17.got_2 = s16[1,240,256]{2,1,0:T(8,128)(2,1)S(1)} collective-permute-done((s16[1,240,256]{2,1,0:T(8,128)(2,1)S(1)}, s16[1,240,256]{2,1,0:T(8,128)(2,1)S(1)}, u32[]{:S(2)}, u32[]{:S(2)}) %collective-permute-start.17) | collective-permute-done | bytes 122912 | tf_op jit(solution)/shard_map/ppermute | solution.py:81
  67.8 0.6 collective-permute-done.18.got_3
  68.6 2.3 %collective-permute-start.19 = (s16[1,240,256]{2,1,0:T(8,128)(2,1)S(1)}, s16[1,240,256]{2,1,0:T(8,128)(2,1)S(1)}, u32[]{:S(2)}, u32[]{:S(2)}) collective-permute-start(s16[1,240,256]{2,1,0:T(8,128)(2,1)S(1)} %shard_map.93), channel_id=1, source_target_pairs={{0,33},{1,32},{2,35},{3,34},{4,13},{5,12},{6,15},{7,14},{8,41},{9,... | collective-permute-start | bytes 368648 | tf_op jit(solution)/shard_map/ppermute | solution.py:81
  71.3 3.0 %collective-permute-done.19 = s16[1,240,256]{2,1,0:T(8,128)(2,1)S(1)} collective-permute-done((s16[1,240,256]{2,1,0:T(8,128)(2,1)S(1)}, s16[1,240,256]{2,1,0:T(8,128)(2,1)S(1)}, u32[]{:S(2)}, u32[]{:S(2)}) %collective-permute-start.19) | collective-permute-done | bytes 122912 | tf_op jit(solution)/shard_map/ppermute | solution.py:81
  74.3 1.3 %collective-permute-done.20 = s16[1,240,256]{2,1,0:T(8,128)(2,1)S(1)} collective-permute-done((s16[1,240,256]{2,1,0:T(8,128)(2,1)S(1)}, s16[1,240,256]{2,1,0:T(8,128)(2,1)S(1)}, u32[]{:S(2)}, u32[]{:S(2)}) %collective-permute-start.20) | collective-permute-done | bytes 122912 | tf_op jit(solution)/shard_map/ppermute | solution.py:81
  75.7 2.7 %collective-permute-start.23 = (s16[4,240,256]{2,1,0:T(8,128)(2,1)S(1)}, s16[4,240,256]{2,1,0:T(8,128)(2,1)S(1)}, u32[]{:S(2)}, u32[]{:S(2)}) collective-permute-start(s16[4,240,256]{2,1,0:T(8,128)(2,1)S(1)} %pad_add_fusion.refs_0_), channel_id=1, source_target_pairs={{0,8},{1,9},{2,10},{3,11},{4,7},{5,6},{6,5},{7,4},{8,0},{9,1},{10,... | collective-permute-start | bytes 1474568 | tf_op jit(solution)/shard_map/ppermute | solution.py:81
  78.5 1.1 %collective-permute-start.24 = (s16[4,240,256]{2,1,0:T(8,128)(2,1)S(1)}, s16[4,240,256]{2,1,0:T(8,128)(2,1)S(1)}, u32[]{:S(2)}, u32[]{:S(2)}) collective-permute-start(s16[4,240,256]{2,1,0:T(8,128)(2,1)S(1)} %pad_add_fusion.refs_0_), channel_id=1, source_target_pairs={{0,96},{1,97},{2,98},{3,99},{4,36},{5,37},{6,38},{7,39},{8,104},{9... | collective-permute-start | bytes 1474568 | tf_op jit(solution)/shard_map/ppermute | solution.py:81
  79.6 1.5 %shard_map.94.refs_3_ = f32[27,256,256]{2,1,0:T(8,128)} custom-call(s32[6]{0:T(128)S(1)} %stack.33.where, s16[4,240,256]{2,1,0:T(8,128)(2,1)S(1)} %pad_add_fusion.refs_0_), custom_call_target="tpu_custom_call" | custom-call | tf_op jit(solution)/shard_map/pallas_call | solution.py:223
  81.1 4.7 %collective-permute-done.22.refs_0_ = s16[4,240,256]{2,1,0:T(8,128)(2,1)S(1)} collective-permute-done((s16[4,240,256]{2,1,0:T(8,128)(2,1)S(1)}, s16[4,240,256]{2,1,0:T(8,128)(2,1)S(1)}, u32[]{:S(2)}, u32[]{:S(2)}) %collective-permute-start.22) | collective-permute-done | bytes 491552 | tf_op jit(solution)/shard_map/ppermute | solution.py:81
  85.9 4.4 %collective-permute-done.23.refs_1_ = s16[4,240,256]{2,1,0:T(8,128)(2,1)S(1)} collective-permute-done((s16[4,240,256]{2,1,0:T(8,128)(2,1)S(1)}, s16[4,240,256]{2,1,0:T(8,128)(2,1)S(1)}, u32[]{:S(2)}, u32[]{:S(2)}) %collective-permute-start.23) | collective-permute-done | bytes 491552 | tf_op jit(solution)/shard_map/ppermute | solution.py:81
  90.2 0.9 collective-permute-done.24.refs_2_
  91.1 3.4 %collective-permute-start.25 = (s16[4,240,256]{2,1,0:T(8,128)(2,1)S(1)}, s16[4,240,256]{2,1,0:T(8,128)(2,1)S(1)}, u32[]{:S(2)}, u32[]{:S(2)}) collective-permute-start(s16[4,240,256]{2,1,0:T(8,128)(2,1)S(1)} %pad_add_fusion.refs_0_), channel_id=1, source_target_pairs={{0,4},{1,5},{2,6},{3,7},{4,0},{5,1},{6,2},{7,3},{8,12},{9,13},{10,... | collective-permute-start | bytes 1474568 | tf_op jit(solution)/shard_map/ppermute | solution.py:450
  95.0 2.2 %shard_map.95.refs_4_ = f32[27,256,256]{2,1,0:T(8,128)} custom-call(s32[6]{0:T(128)S(1)} %stack.33.where, s16[4,240,256]{2,1,0:T(8,128)(2,1)S(1)} %collective-permute-done.22.refs_0_, s16[4,240,256]{2,1,0:T(8,128)(2,1)S(1)} %collective-permute-done.23.refs_1_, ...), custom_call_target="tpu_custom_call", output_to_operand_aliasing={{}: (4, {})} | custom-call | tf_op jit(solution)/shard_map/pallas_call | solution.py:223
  97.4 0.7 collective-permute-done.28.refs_3_
  98.1 2.6 %shard_map.96 = f32[27,256,256]{2,1,0:T(8,128)} custom-call(s32[6]{0:T(128)S(1)} %stack.33.where, s16[4,240,256]{2,1,0:T(8,128)(2,1)S(1)} %collective-permute-done.25.refs_0_, s16[4,240,256]{2,1,0:T(8,128)(2,1)S(1)} %collective-permute-done.26.refs_1_, s16[4,240,256]{2,1,0:T(8,128)(2,1)S(1)} %collective-permute-done.27.refs_2_, ...), custom_call_target="tpu_custom_call", output_to_operand_aliasing={{}: (5, {})} | custom-call | tf_op jit(solution)/shard_map/pallas_call | solution.py:223
  (44 shorter events, 4.2 us)
Async XLA Ops:
  0.7 1.0 %copy-start.1 = (bf16[2,8,8,8,256]{4,3,2,1,0:T(8,128)(2,1)S(1)}, bf16[2,8,8,8,256]{4,3,2,1,0:T(8,128)(2,1)}, u32[]{:S(2)}) copy-start(bf16[2,8,8,8,256]{4,3,2,1,0:T(8,128)(2,1)} %param.5) | copy-start | bytes 1572868
  1.8 1.0 %copy-start.2 = (bf16[2,8,8,8,256]{4,3,2,1,0:T(8,128)(2,1)S(1)}, bf16[2,8,8,8,256]{4,3,2,1,0:T(8,128)(2,1)}, u32[]{:S(2)}) copy-start(bf16[2,8,8,8,256]{4,3,2,1,0:T(8,128)(2,1)} %param.6) | copy-start | bytes 1572868
  2.8 0.7 copy-start.3
  4.5 5.0 %collective-permute-start = (bf16[2,8,16,256]{3,2,1,0:T(8,128)(2,1)S(1)}, bf16[2,8,16,256]{3,2,1,0:T(8,128)(2,1)S(1)}, u32[]{:S(2)}, u32[]{:S(2)}) collective-permute-start(bf16[2,8,16,256]{3,2,1,0:T(8,128)(2,1)S(1)} %get-tuple-element.38), channel_id=1, source_target_pairs={{0,4},{4,0},{8,12},{12,8},{16,20},{20,16},{24,28},{28,24},{32,36},... | collective-permute-start | bytes 393224 | tf_op jit(solution)/shard_map/ppermute | solution.py:398
  6.0 8.0 %collective-permute-start.1 = (bf16[2,8,16,256]{3,2,1,0:T(8,128)(2,1)S(1)}, bf16[2,8,16,256]{3,2,1,0:T(8,128)(2,1)S(1)}, u32[]{:S(2)}, u32[]{:S(2)}) collective-permute-start(bf16[2,8,16,256]{3,2,1,0:T(8,128)(2,1)S(1)} %get-tuple-element.40), channel_id=1, source_target_pairs={{4,8},{8,4},{12,16},{16,12},{20,24},{24,20},{28,32},{32,28},{36,40... | collective-permute-start | bytes 393224 | tf_op jit(solution)/shard_map/ppermute | solution.py:398
  9.6 7.9 %collective-permute-start.5 = (bf16[2,8,16,256]{3,2,1,0:T(8,128)(2,1)S(1)}, bf16[2,8,16,256]{3,2,1,0:T(8,128)(2,1)S(1)}, u32[]{:S(2)}, u32[]{:S(2)}) collective-permute-start(bf16[2,8,16,256]{3,2,1,0:T(8,128)(2,1)S(1)} %get-tuple-element.47), channel_id=1, source_target_pairs={{1,2},{2,1},{5,6},{6,5},{9,10},{10,9},{13,14},{14,13},{17,18},{18,... | collective-permute-start | bytes 393224 | tf_op jit(solution)/shard_map/ppermute | solution.py:398
  10.3 7.2 %collective-permute-start.4 = (bf16[2,8,16,256]{3,2,1,0:T(8,128)(2,1)S(1)}, bf16[2,8,16,256]{3,2,1,0:T(8,128)(2,1)S(1)}, u32[]{:S(2)}, u32[]{:S(2)}) collective-permute-start(bf16[2,8,16,256]{3,2,1,0:T(8,128)(2,1)S(1)} %get-tuple-element.45), channel_id=1, source_target_pairs={{0,1},{1,0},{2,3},{3,2},{4,5},{5,4},{6,7},{7,6},{8,9},{9,8},{10,11... | collective-permute-start | bytes 393224 | tf_op jit(solution)/shard_map/ppermute | solution.py:398
  14.6 4.2 %collective-permute-start.2 = (bf16[2,2,16,256]{3,2,1,0:T(8,128)(2,1)S(1)}, bf16[2,2,16,256]{3,2,1,0:T(8,128)(2,1)S(1)}, u32[]{:S(2)}, u32[]{:S(2)}) collective-permute-start(bf16[2,2,16,256]{3,2,1,0:T(8,128)(2,1)S(1)} %get-tuple-element.41), channel_id=1, source_target_pairs={{0,1},{1,0},{2,3},{3,2},{4,5},{5,4},{6,7},{7,6},{8,9},{9,8},{10,11... | collective-permute-start | bytes 98312 | tf_op jit(solution)/shard_map/ppermute | solution.py:398
  14.7 4.1 %collective-permute-start.3 = (bf16[2,2,16,256]{3,2,1,0:T(8,128)(2,1)S(1)}, bf16[2,2,16,256]{3,2,1,0:T(8,128)(2,1)S(1)}, u32[]{:S(2)}, u32[]{:S(2)}) collective-permute-start(bf16[2,2,16,256]{3,2,1,0:T(8,128)(2,1)S(1)} %get-tuple-element.42), channel_id=1, source_target_pairs={{1,2},{2,1},{5,6},{6,5},{9,10},{10,9},{13,14},{14,13},{17,18},{18,... | collective-permute-start | bytes 98312 | tf_op jit(solution)/shard_map/ppermute | solution.py:398
  15.5 0.7 copy-start.4
  21.4 2.5 %collective-permute-start.6 = (s16[4,240,256]{2,1,0:T(8,128)(2,1)S(1)}, s16[4,240,256]{2,1,0:T(8,128)(2,1)S(1)}, u32[]{:S(2)}, u32[]{:S(2)}) collective-permute-start(s16[4,240,256]{2,1,0:T(8,128)(2,1)S(1)} %get-tuple-element.52), channel_id=1, source_target_pairs={{0,4},{1,5},{2,6},{3,7},{4,0},{5,1},{6,2},{7,3},{8,12},{9,13},{10,... | collective-permute-start | bytes 1474568 | tf_op jit(solution)/shard_map/ppermute | solution.py:423
  23.3 12.7 %copy-start = (bf16[27,256,256]{2,1,0:T(8,128)(2,1)S(1)}, bf16[27,256,256]{2,1,0:T(8,128)(2,1)}, u32[]{:S(2)}) copy-start(bf16[27,256,256]{2,1,0:T(8,128)(2,1)} %kernel.3) | copy-start | bytes 10616836
  23.3 2.8 %collective-permute-start.7 = (s16[4,240,256]{2,1,0:T(8,128)(2,1)S(1)}, s16[4,240,256]{2,1,0:T(8,128)(2,1)S(1)}, u32[]{:S(2)}, u32[]{:S(2)}) collective-permute-start(s16[4,240,256]{2,1,0:T(8,128)(2,1)S(1)} %get-tuple-element.55), channel_id=1, source_target_pairs={{0,4},{1,5},{2,6},{3,7},{4,0},{5,1},{6,2},{7,3},{8,12},{9,13},{10,... | collective-permute-start | bytes 1474568 | tf_op jit(solution)/shard_map/ppermute | solution.py:423
  26.0 9.2 %collective-permute-start.9 = (s16[4,240,256]{2,1,0:T(8,128)(2,1)S(1)}, s16[4,240,256]{2,1,0:T(8,128)(2,1)S(1)}, u32[]{:S(2)}, u32[]{:S(2)}) collective-permute-start(s16[4,240,256]{2,1,0:T(8,128)(2,1)S(1)} %get-tuple-element.59), channel_id=1, source_target_pairs={{0,4},{1,5},{2,6},{3,7},{4,0},{5,1},{6,2},{7,3},{8,12},{9,13},{10,... | collective-permute-start | bytes 1474568 | tf_op jit(solution)/shard_map/ppermute | solution.py:423
  28.3 7.5 %collective-permute-start.8 = (s16[4,240,256]{2,1,0:T(8,128)(2,1)S(1)}, s16[4,240,256]{2,1,0:T(8,128)(2,1)S(1)}, u32[]{:S(2)}, u32[]{:S(2)}) collective-permute-start(s16[4,240,256]{2,1,0:T(8,128)(2,1)S(1)} %get-tuple-element.58), channel_id=1, source_target_pairs={{0,4},{1,5},{2,6},{3,7},{4,0},{5,1},{6,2},{7,3},{8,12},{9,13},{10,... | collective-permute-start | bytes 1474568 | tf_op jit(solution)/shard_map/ppermute | solution.py:423
  28.9 17.9 %collective-permute-start.11 = (s16[4,240,256]{2,1,0:T(8,128)(2,1)S(1)}, s16[4,240,256]{2,1,0:T(8,128)(2,1)S(1)}, u32[]{:S(2)}, u32[]{:S(2)}) collective-permute-start(s16[4,240,256]{2,1,0:T(8,128)(2,1)S(1)} %shard_map.85), channel_id=1, source_target_pairs={{0,8},{1,9},{2,10},{3,11},{4,7},{5,6},{6,5},{7,4},{8,0},{9,1},{10,... | collective-permute-start | bytes 1474568 | tf_op jit(solution)/shard_map/ppermute | solution.py:428
  30.5 16.2 %collective-permute-start.10 = (s16[4,240,256]{2,1,0:T(8,128)(2,1)S(1)}, s16[4,240,256]{2,1,0:T(8,128)(2,1)S(1)}, u32[]{:S(2)}, u32[]{:S(2)}) collective-permute-start(s16[4,240,256]{2,1,0:T(8,128)(2,1)S(1)} %shard_map.83), channel_id=1, source_target_pairs={{0,104},{1,105},{2,106},{3,107},{4,39},{5,38},{6,37},{7,36},{8,96}... | collective-permute-start | bytes 1474568 | tf_op jit(solution)/shard_map/ppermute | solution.py:428
  35.6 13.2 %collective-permute-start.12 = (s16[4,240,256]{2,1,0:T(8,128)(2,1)S(1)}, s16[4,240,256]{2,1,0:T(8,128)(2,1)S(1)}, u32[]{:S(2)}, u32[]{:S(2)}) collective-permute-start(s16[4,240,256]{2,1,0:T(8,128)(2,1)S(1)} %shard_map.88), channel_id=1, source_target_pairs={{0,96},{1,97},{2,98},{3,99},{4,36},{5,37},{6,38},{7,39},{8,104},{9... | collective-permute-start | bytes 1474568 | tf_op jit(solution)/shard_map/ppermute | solution.py:428
  49.4 5.0 %collective-permute-start.13 = (s16[1,240,256]{2,1,0:T(8,128)(2,1)S(1)}, s16[1,240,256]{2,1,0:T(8,128)(2,1)S(1)}, u32[]{:S(2)}, u32[]{:S(2)}) collective-permute-start(s16[1,240,256]{2,1,0:T(8,128)(2,1)S(1)} %get-tuple-element.65), channel_id=1, source_target_pairs={{0,33},{1,32},{2,35},{3,34},{4,13},{5,12},{6,15},{7,14},{8,41},{9,... | collective-permute-start | bytes 368648 | tf_op jit(solution)/shard_map/ppermute | solution.py:81
  50.4 6.9 %collective-permute-start.14 = (s16[1,240,256]{2,1,0:T(8,128)(2,1)S(1)}, s16[1,240,256]{2,1,0:T(8,128)(2,1)S(1)}, u32[]{:S(2)}, u32[]{:S(2)}) collective-permute-start(s16[1,240,256]{2,1,0:T(8,128)(2,1)S(1)} %get-tuple-element.66), channel_id=1, source_target_pairs={{0,1},{1,0},{2,3},{3,2},{4,5},{5,4},{6,7},{7,6},{8,9},{9,8},{10,11... | collective-permute-start | bytes 368648 | tf_op jit(solution)/shard_map/ppermute | solution.py:81
  51.8 5.5 %collective-permute-start.15 = (s16[1,240,256]{2,1,0:T(8,128)(2,1)S(1)}, s16[1,240,256]{2,1,0:T(8,128)(2,1)S(1)}, u32[]{:S(2)}, u32[]{:S(2)}) collective-permute-start(s16[1,240,256]{2,1,0:T(8,128)(2,1)S(1)} %get-tuple-element.67), channel_id=1, source_target_pairs={{0,32},{1,33},{2,34},{3,35},{4,12},{5,13},{6,14},{7,15},{8,40},{9,... | collective-permute-start | bytes 368648 | tf_op jit(solution)/shard_map/ppermute | solution.py:81
  57.5 7.4 %collective-permute-start.16 = (s16[1,240,256]{2,1,0:T(8,128)(2,1)S(1)}, s16[1,240,256]{2,1,0:T(8,128)(2,1)S(1)}, u32[]{:S(2)}, u32[]{:S(2)}) collective-permute-start(s16[1,240,256]{2,1,0:T(8,128)(2,1)S(1)} %shard_map.92.own), channel_id=1, source_target_pairs={{0,27},{1,26},{2,25},{3,24},{4,124},{5,125},{6,126},{7,127},{8,19}... | collective-permute-start | bytes 368648 | tf_op jit(solution)/shard_map/ppermute | solution.py:81
  62.6 5.2 %collective-permute-start.17 = (s16[1,240,256]{2,1,0:T(8,128)(2,1)S(1)}, s16[1,240,256]{2,1,0:T(8,128)(2,1)S(1)}, u32[]{:S(2)}, u32[]{:S(2)}) collective-permute-start(s16[1,240,256]{2,1,0:T(8,128)(2,1)S(1)} %shard_map.92.own), channel_id=1, source_target_pairs={{0,3},{1,2},{2,1},{3,0},{4,100},{5,101},{6,102},{7,103},{8,11},{9,... | collective-permute-start | bytes 368648 | tf_op jit(solution)/shard_map/ppermute | solution.py:81
  63.2 5.2 %collective-permute-start.18 = (s16[1,240,256]{2,1,0:T(8,128)(2,1)S(1)}, s16[1,240,256]{2,1,0:T(8,128)(2,1)S(1)}, u32[]{:S(2)}, u32[]{:S(2)}) collective-permute-start(s16[1,240,256]{2,1,0:T(8,128)(2,1)S(1)} %shard_map.92.own), channel_id=1, source_target_pairs={{0,24},{1,25},{2,26},{3,27},{4,28},{5,29},{6,30},{7,31},{8,16},{9,... | collective-permute-start | bytes 368648 | tf_op jit(solution)/shard_map/ppermute | solution.py:81
  68.6 5.7 %collective-permute-start.19 = (s16[1,240,256]{2,1,0:T(8,128)(2,1)S(1)}, s16[1,240,256]{2,1,0:T(8,128)(2,1)S(1)}, u32[]{:S(2)}, u32[]{:S(2)}) collective-permute-start(s16[1,240,256]{2,1,0:T(8,128)(2,1)S(1)} %shard_map.93), channel_id=1, source_target_pairs={{0,33},{1,32},{2,35},{3,34},{4,13},{5,12},{6,15},{7,14},{8,41},{9,... | collective-permute-start | bytes 368648 | tf_op jit(solution)/shard_map/ppermute | solution.py:81
  70.9 4.7 %collective-permute-start.20 = (s16[1,240,256]{2,1,0:T(8,128)(2,1)S(1)}, s16[1,240,256]{2,1,0:T(8,128)(2,1)S(1)}, u32[]{:S(2)}, u32[]{:S(2)}) collective-permute-start(s16[1,240,256]{2,1,0:T(8,128)(2,1)S(1)} %shard_map.93), channel_id=1, source_target_pairs={{0,1},{1,0},{2,3},{3,2},{4,5},{5,4},{6,7},{7,6},{8,9},{9,8},{10,11... | collective-permute-start | bytes 368648 | tf_op jit(solution)/shard_map/ppermute | solution.py:81
  70.9 4.7 %collective-permute-start.21 = (s16[1,240,256]{2,1,0:T(8,128)(2,1)S(1)}, s16[1,240,256]{2,1,0:T(8,128)(2,1)S(1)}, u32[]{:S(2)}, u32[]{:S(2)}) collective-permute-start(s16[1,240,256]{2,1,0:T(8,128)(2,1)S(1)} %shard_map.93), channel_id=1, source_target_pairs={{0,32},{1,33},{2,34},{3,35},{4,12},{5,13},{6,14},{7,15},{8,40},{9,... | collective-permute-start | bytes 368648 | tf_op jit(solution)/shard_map/ppermute | solution.py:81
  75.6 10.2 %collective-permute-start.22 = (s16[4,240,256]{2,1,0:T(8,128)(2,1)S(1)}, s16[4,240,256]{2,1,0:T(8,128)(2,1)S(1)}, u32[]{:S(2)}, u32[]{:S(2)}) collective-permute-start(s16[4,240,256]{2,1,0:T(8,128)(2,1)S(1)} %pad_add_fusion.refs_0_), channel_id=1, source_target_pairs={{0,104},{1,105},{2,106},{3,107},{4,39},{5,38},{6,37},{7,36},{8,96}... | collective-permute-start | bytes 1474568 | tf_op jit(solution)/shard_map/ppermute | solution.py:81
  75.7 14.5 %collective-permute-start.23 = (s16[4,240,256]{2,1,0:T(8,128)(2,1)S(1)}, s16[4,240,256]{2,1,0:T(8,128)(2,1)S(1)}, u32[]{:S(2)}, u32[]{:S(2)}) collective-permute-start(s16[4,240,256]{2,1,0:T(8,128)(2,1)S(1)} %pad_add_fusion.refs_0_), channel_id=1, source_target_pairs={{0,8},{1,9},{2,10},{3,11},{4,7},{5,6},{6,5},{7,4},{8,0},{9,1},{10,... | collective-permute-start | bytes 1474568 | tf_op jit(solution)/shard_map/ppermute | solution.py:81
  78.5 12.6 %collective-permute-start.24 = (s16[4,240,256]{2,1,0:T(8,128)(2,1)S(1)}, s16[4,240,256]{2,1,0:T(8,128)(2,1)S(1)}, u32[]{:S(2)}, u32[]{:S(2)}) collective-permute-start(s16[4,240,256]{2,1,0:T(8,128)(2,1)S(1)} %pad_add_fusion.refs_0_), channel_id=1, source_target_pairs={{0,96},{1,97},{2,98},{3,99},{4,36},{5,37},{6,38},{7,39},{8,104},{9... | collective-permute-start | bytes 1474568 | tf_op jit(solution)/shard_map/ppermute | solution.py:81
  91.1 6.2 %collective-permute-start.25 = (s16[4,240,256]{2,1,0:T(8,128)(2,1)S(1)}, s16[4,240,256]{2,1,0:T(8,128)(2,1)S(1)}, u32[]{:S(2)}, u32[]{:S(2)}) collective-permute-start(s16[4,240,256]{2,1,0:T(8,128)(2,1)S(1)} %pad_add_fusion.refs_0_), channel_id=1, source_target_pairs={{0,4},{1,5},{2,6},{3,7},{4,0},{5,1},{6,2},{7,3},{8,12},{9,13},{10,... | collective-permute-start | bytes 1474568 | tf_op jit(solution)/shard_map/ppermute | solution.py:450
  94.5 2.8 %collective-permute-start.26 = (s16[4,240,256]{2,1,0:T(8,128)(2,1)S(1)}, s16[4,240,256]{2,1,0:T(8,128)(2,1)S(1)}, u32[]{:S(2)}, u32[]{:S(2)}) collective-permute-start(s16[4,240,256]{2,1,0:T(8,128)(2,1)S(1)} %collective-permute-done.22.refs_0_), channel_id=1, source_target_pairs={{0,4},{1,5},{2,6},{3,7},{4,0},{5,1},{6,2},{7,3},{8,12},{9,13},{10,... | collective-permute-start | bytes 1474568 | tf_op jit(solution)/shard_map/ppermute | solution.py:450
  94.5 2.9 %collective-permute-start.27 = (s16[4,240,256]{2,1,0:T(8,128)(2,1)S(1)}, s16[4,240,256]{2,1,0:T(8,128)(2,1)S(1)}, u32[]{:S(2)}, u32[]{:S(2)}) collective-permute-start(s16[4,240,256]{2,1,0:T(8,128)(2,1)S(1)} %collective-permute-done.23.refs_1_), channel_id=1, source_target_pairs={{0,4},{1,5},{2,6},{3,7},{4,0},{5,1},{6,2},{7,3},{8,12},{9,13},{10,... | collective-permute-start | bytes 1474568 | tf_op jit(solution)/shard_map/ppermute | solution.py:450
  95.0 3.1 %collective-permute-start.28 = (s16[4,240,256]{2,1,0:T(8,128)(2,1)S(1)}, s16[4,240,256]{2,1,0:T(8,128)(2,1)S(1)}, u32[]{:S(2)}, u32[]{:S(2)}) collective-permute-start(s16[4,240,256]{2,1,0:T(8,128)(2,1)S(1)} %collective-permute-done.24.refs_2_), channel_id=1, source_target_pairs={{0,4},{1,5},{2,6},{3,7},{4,0},{5,1},{6,2},{7,3},{8,12},{9,13},{10,... | collective-permute-start | bytes 1474568 | tf_op jit(solution)/shard_map/ppermute | solution.py:450

commit v4 on v3

--- a/solution.py
+++ b/solution.py
@@ -28,8 +28,8 @@
 
 FIRST, SECOND = 0, 1
 GROUPS = (
-    ((("z", FIRST), ("y", SECOND)), (("x", FIRST), ("y", FIRST)), (("x", SECOND), ("z", SECOND))),
-    ((("x", SECOND), ("y", FIRST)), (("x", FIRST), ("z", FIRST)), (("y", SECOND), ("z", SECOND))),
+    ((("z", FIRST), ("x", SECOND)), (("x", FIRST), ("y", FIRST)), (("y", SECOND), ("z", SECOND))),
+    ((("y", SECOND), ("z", SECOND)), (("x", FIRST), ("y", FIRST)), (("z", FIRST), ("x", SECOND))),
 )
 
 
@@ -86,7 +86,7 @@
     return lax.optimization_barrier((value, *others))[0]
 
 
-def call(kernel, outs, *args, scratch=(), aliases=None):
+def call(kernel, outs, *args, scratch=(), aliases=None, cost=FREE):
     return pl.pallas_call(
         kernel,
         out_shape=list(outs),
@@ -95,7 +95,7 @@
         scratch_shapes=list(scratch),
         input_output_aliases=aliases or {},
         compiler_params=PARAMS,
-        cost_estimate=FREE,
+        cost_estimate=cost,
     )(*args)
 
 
@@ -397,6 +397,9 @@
     def swap(arrays, axis, pairs):
         return [lax.ppermute(a, axis, p) for a, p in zip(arrays, pairs)]
 
+    busy = pl.CostEstimate(flops=2**31, bytes_accessed=2**22, transcendentals=0)
+    (pick,) = call(picks_kernel, [shape((3, 480, 160), jnp.bfloat16)], neighbors, cost=busy)
+    odd = after(odd, pick)
     cells, grad, masks, x_a, x_b, y_a, y_b = call(
         prepare_kernel,
         [column, column, shape((8, 128, 128), jnp.bfloat16)] + [side] * 4,
@@ -404,52 +407,53 @@
     )
     x_halo = swap((x_a, x_b), "gx", x_pairs)
     y_halo = swap((after(y_a, x_halo[0]), after(y_b, x_halo[0])), "gy", y_pairs)
-    (pick,) = call(picks_kernel, [shape((3, 480, 160), jnp.bfloat16)], after(neighbors, x_halo[0]))
     corners = swap(call(corners_kernel, [corner, corner], odd, *x_halo), "gy", y_pairs)
     (wide,) = call(inner_kernel, [shape(wide_shape, jnp.bfloat16)], odd, pick, cells, *y_halo)
     halo = (*x_halo, *corners)
     (wide,) = call(outer_kernel, [shape(wide_shape, jnp.bfloat16)], odd, pick, *halo, wide, aliases={6: 0})
 
-    sums = {}
-    got = {}
-    before = []
-    for m in (1, 2, 3, 0):
-        own, coded = call(
+    sums, got, before = {}, {}, []
+
+    def part(m, *before):
+        return call(
             functools.partial(part_kernel, m),
             [shape((EACH * HALF, C), jnp.float32), CODED_4],
             where, after(wide, *before), grad,
             scratch=[pltpu.VMEM((EACH * HALF, C), jnp.float32)],
         )
-        other = lax.ppermute(coded, BOTH, other_core())
+
+    def chip_sum(m, own, got):
         out = CODED_4 if m else shape((4, ROWS, C), jnp.float32)
-        (sums[m],) = call(functools.partial(pair_sum_kernel, m == 0), [out], own, other)
+        return call(functools.partial(pair_sum_kernel, m == 0), [out], own, got)[0]
+
+    for m in (0, 1, 2, 3):
+        own, coded = part(m, *before)
+        sums[m] = chip_sum(m, own, lax.ppermute(coded, BOTH, other_core()))
         before = [own] + list(sums.values())[-2:-1]
         if m:
             got[m] = lax.ppermute(sums[m], BOTH, partners(0, m))
-
     brick_rows = shape((2, 8, 64, C), jnp.bfloat16)
     totals = pltpu.VMEM((1024, C), jnp.bfloat16)
-    (forward,) = call(
-        forward_kernel, [brick_rows], after(wide, sums[0], sums[3]), kernel, masks, scratch=[totals]
-    )
-    (backward,) = call(
-        backward_kernel, [brick_rows], odd, pick, after(grad, forward), *y_halo, *halo, kernel, masks,
-        scratch=[totals, pltpu.VMEM(wide_shape, jnp.bfloat16)],
-    )
+    (forward,) = call(forward_kernel, [brick_rows], after(wide, sums[3]), kernel, masks, scratch=[totals])
     keep, *sent = call(
         group_sum_kernel,
         [shape((1, ROWS, C), jnp.float32)] + [CODED_1] * 3,
-        inner.reshape(1).astype(jnp.int32), after(sums[0], backward), got[1], got[2], got[3],
+        inner.reshape(1).astype(jnp.int32), after(sums[0], forward), got[1], got[2], got[3],
     )
-    (part,) = call(last_group_kernel, [CODED_1], keep, *exchange(sent, 1))
-    (whole,) = call(total_kernel, [CODED_1], part, *exchange([part] * 3, 2, (2, 3, 1)))
+    (partial,) = call(last_group_kernel, [CODED_1], keep, *exchange(sent, 1))
+    (whole,) = call(total_kernel, [CODED_1], partial, *exchange([partial] * 3, 2, (2, 3, 1)))
     four = jnp.concatenate([whole] + exchange([whole] * 3, 1, (2, 3, 1)))
     sets = [four] + exchange([four] * 3, 0)
 
+    (backward,) = call(
+        backward_kernel, [brick_rows], odd, pick, after(grad, four), *y_halo, *halo, kernel, masks,
+        scratch=[totals, pltpu.VMEM(wide_shape, jnp.bfloat16)],
+    )
+
     def other(a):
         return lax.ppermute(a, BOTH, other_core())
 
-    done = finish(scale, where, [(0, 0)], [four], None)
+    done = finish(scale, where, [(0, 0)], [after(four, backward)], None)
     *own, done = lax.optimization_barrier((*sets, done))
     far = [other(a) for a in own]
     done = finish(scale, where, [(0, 1), (0, 2), (0, 3)], own[1:], done)

time: 101 us -> 97.9 us (0.969)
  waiting for transfers between devices: 26.7 us -> 22 us
  starting transfers between devices: 38 us -> 41.6 us
  local copies, waits for them, and re-layouts: 3.54 us -> 0.86 us
    ppermute x12, waiting for transfers between devices: 23.8 us -> 16.1 us  [exchange(): lax.ppermute(arrays[m - 1], BOTH, partners(level, m))]
    unnamed x10, local copies, waits for them, and re-layouts: 3.46 us -> 0.77 us
    ppermute x3, starting transfers between devices: 6.59 us -> 8.81 us  [shards(): got[m] = lax.ppermute(sums[m], BOTH, partners(0, m))]
    ppermute x12, starting transfers between devices: 15.9 us -> 17.6 us  [exchange(): lax.ppermute(arrays[m - 1], BOTH, partners(level, m))]
    ppermute x3, waiting for transfers between devices: 2.02 us -> 3.53 us  [shards(): got[m] = lax.ppermute(sums[m], BOTH, partners(0, m))]
    ppermute x6, waiting for transfers between devices: 0.02 us -> 1.5 us  [swap(): return [lax.ppermute(a, axis, p) for a, p in zip(arrays, pairs)]]
  transfers between devices with their start and end apart: 29 -> 29, of which waited for: 13 -> 14; matrix products, arithmetic and copies ran while one was open for 0% -> 0% of each run, Pallas kernels for 24% -> 23%
where the time goes in v4:
time: 97.9 us; the launch traced here: 97.7 us
  starting transfers between devices  41.6 us (42%)
  Pallas kernels  32 us (33%)
  waiting for transfers between devices  22 us (22%)
  between operations  1.14 us (1%)
    pallas_call x18, Pallas kernels, call(): pl.pallas_call(kernel, out_shape=list(outs), in_specs=[SMEM if a.dtype ==...  25.7 us
    ppermute x12, starting transfers between devices, exchange(): lax.ppermute(arrays[m - 1], BOTH, partners(level, m))  17.6 us
    ppermute x12, waiting for transfers between devices, exchange(): lax.ppermute(arrays[m - 1], BOTH, partners(level, m))  16.1 us
    ppermute x6, starting transfers between devices, swap(): return [lax.ppermute(a, axis, p) for a, p in zip(arrays, pairs)]  10.1 us
    ppermute x3, starting transfers between devices, shards(): got[m] = lax.ppermute(sums[m], BOTH, partners(0, m))  8.81 us
    pallas_call x3, Pallas kernels, finish(): pl.pallas_call(functools.partial(finish_kernel, scale, parts), out_shape=...  6.33 us
    ppermute x4, starting transfers between devices, other(): return lax.ppermute(a, BOTH, other_core())  3.75 us
    ppermute x3, waiting for transfers between devices, shards(): got[m] = lax.ppermute(sums[m], BOTH, partners(0, m))  3.53 us
  transfers between devices with their start and end apart: 29, of which 14 were waited for; matrix products, arithmetic and copies ran while one was open for 0% of the time, Pallas kernels for 23%

profile of v4, /device:TPU:1, one launch (start us, length us, event | category | flops | bytes accessed | tf_op | source)
XLA Modules:
  0.0 97.7 jit_solution(4383458970298481433)
XLA Ops:
  0.7 0.8 copy-done.4
  1.4 1.3 %shard_map.76.pick = bf16[3,480,160]{2,1,0:T(8,128)(2,1)S(1)} custom-call(s32[2,27]{1,0:T(2,128)S(1)} %copy-done.4), custom_call_target="tpu_custom_call" | custom-call | flops 2147483648 | bytes 4194304 | tf_op jit(solution)/shard_map/pallas_call | solution.py:90
  2.9 1.7 %shard_map.77 = (bf16[8,8,16,256]{3,2,1,0:T(8,128)(2,1)S(1)}, bf16[8,8,16,256]{3,2,1,0:T(8,128)(2,1)S(1)}, bf16[8,128,128]{2,1,0:T(8,128)(2,1)S(1)}, bf16[2,8,16...) custom-call(s32[2]{0:T(128)S(1)} %pad_add_fusion.1.odd, ...), custom_call_target="tpu_custom_call" | custom-call | tf_op jit(solution)/shard_map/pallas_call | solution.py:90
  4.6 1.4 %collective-permute-start = (bf16[2,8,16,256]{3,2,1,0:T(8,128)(2,1)S(1)}, bf16[2,8,16,256]{3,2,1,0:T(8,128)(2,1)S(1)}, u32[]{:S(2)}, u32[]{:S(2)}) collective-permute-start(bf16[2,8,16,256]{3,2,1,0:T(8,128)(2,1)S(1)} %get-tuple-element.40), channel_id=1, source_target_pairs={{0,4},{4,0},{8,12},{12,8},{16,20},{20,16},{24,28},{28,24},{32,36},... | collective-permute-start | bytes 393224 | tf_op jit(solution)/shard_map/ppermute | solution.py:398
  6.0 3.5 %collective-permute-start.1 = (bf16[2,8,16,256]{3,2,1,0:T(8,128)(2,1)S(1)}, bf16[2,8,16,256]{3,2,1,0:T(8,128)(2,1)S(1)}, u32[]{:S(2)}, u32[]{:S(2)}) collective-permute-start(bf16[2,8,16,256]{3,2,1,0:T(8,128)(2,1)S(1)} %get-tuple-element.41), channel_id=1, source_target_pairs={{4,8},{8,4},{12,16},{16,12},{20,24},{24,20},{28,32},{32,28},{36,40... | collective-permute-start | bytes 393224 | tf_op jit(solution)/shard_map/ppermute | solution.py:398
  9.5 0.7 collective-permute-start.5
  10.2 3.7 %collective-permute-start.4 = (bf16[2,8,16,256]{3,2,1,0:T(8,128)(2,1)S(1)}, bf16[2,8,16,256]{3,2,1,0:T(8,128)(2,1)S(1)}, u32[]{:S(2)}, u32[]{:S(2)}) collective-permute-start(bf16[2,8,16,256]{3,2,1,0:T(8,128)(2,1)S(1)} %get-tuple-element.46), channel_id=1, source_target_pairs={{0,1},{1,0},{2,3},{3,2},{4,5},{5,4},{6,7},{7,6},{8,9},{9,8},{10,11... | collective-permute-start | bytes 393224 | tf_op jit(solution)/shard_map/ppermute | solution.py:398
  13.9 0.6 shard_map.78
  14.6 0.7 collective-permute-start.3
  15.4 1.5 %collective-permute-done.4.y_a = bf16[2,8,16,256]{3,2,1,0:T(8,128)(2,1)S(1)} collective-permute-done((bf16[2,8,16,256]{3,2,1,0:T(8,128)(2,1)S(1)}, bf16[2,8,16,256]{3,2,1,0:T(8,128)(2,1)S(1)}, u32[]{:S(2)}, u32[]{:S(2)}) %collective-permute-start.4) | collective-permute-done | bytes 131104 | tf_op jit(solution)/shard_map/ppermute | solution.py:398
  16.9 1.2 %shard_map.79._ = bf16[3,10,10,16,256]{4,3,2,1,0:T(8,128)(2,1)S(1)} custom-call(s32[2]{0:T(128)S(1)} %pad_add_fusion.1.odd, bf16[3,480,160]{2,1,0:T(8,128)(2,1)S(1)} %shard_map.76.pick, bf16[8,8,16,256]{3,2,1,0:T(8,128)(2,1)S(1)} %get-tuple-element.44.cells, bf16[2,8,16,256]{3,2,1,0:T(8,128)(2,1)S(1)} %collective-permute-done.4.y_a, ...), custom_call_target="tpu_custom_call" | custom-call | tf_op jit(solution)/shard_map/pallas_call | solution.py:90
  18.1 0.8 shard_map.80.wide
  18.9 1.8 %shard_map.81 = (f32[896,256]{1,0:T(8,128)S(1)}, s16[4,240,256]{2,1,0:T(8,128)(2,1)S(1)}) custom-call(s32[6]{0:T(128)S(1)} %stack.30.where, bf16[3,10,10,16,256]{4,3,2,1,0:T(8,128)(2,1)S(1)} %shard_map.80.wide, bf16[8,8,16,256]{3,2,1,0:T(8,128)(2,1)S(1)} %get-tuple-element.68.grad), custom_call_target="tpu_custom_call" | custom-call | tf_op jit(solution)/shard_map/pallas_call | solution.py:90
  20.8 1.8 %shard_map.82 = (f32[896,256]{1,0:T(8,128)S(1)}, s16[4,240,256]{2,1,0:T(8,128)(2,1)S(1)}) custom-call(s32[6]{0:T(128)S(1)} %stack.30.where, bf16[3,10,10,16,256]{4,3,2,1,0:T(8,128)(2,1)S(1)} %shard_map.80.wide, bf16[8,8,16,256]{3,2,1,0:T(8,128)(2,1)S(1)} %get-tuple-element.68.grad), custom_call_target="tpu_custom_call" | custom-call | tf_op jit(solution)/shard_map/pallas_call | solution.py:90
  22.6 0.6 collective-permute-start.7
  23.4 1.8 %shard_map.84 = (f32[896,256]{1,0:T(8,128)S(1)}, s16[4,240,256]{2,1,0:T(8,128)(2,1)S(1)}) custom-call(s32[6]{0:T(128)S(1)} %stack.30.where, bf16[3,10,10,16,256]{4,3,2,1,0:T(8,128)(2,1)S(1)} %shard_map.80.wide, bf16[8,8,16,256]{3,2,1,0:T(8,128)(2,1)S(1)} %get-tuple-element.68.grad), custom_call_target="tpu_custom_call" | custom-call | tf_op jit(solution)/shard_map/pallas_call | solution.py:90
  25.6 1.8 %shard_map.86 = (f32[896,256]{1,0:T(8,128)S(1)}, s16[4,240,256]{2,1,0:T(8,128)(2,1)S(1)}) custom-call(s32[6]{0:T(128)S(1)} %stack.30.where, bf16[3,10,10,16,256]{4,3,2,1,0:T(8,128)(2,1)S(1)} %shard_map.80.wide, bf16[8,8,16,256]{3,2,1,0:T(8,128)(2,1)S(1)} %get-tuple-element.68.grad), custom_call_target="tpu_custom_call" | custom-call | tf_op jit(solution)/shard_map/pallas_call | solution.py:90
  27.4 0.6 collective-permute-start.8
  28.0 5.7 %collective-permute-start.9 = (s16[4,240,256]{2,1,0:T(8,128)(2,1)S(1)}, s16[4,240,256]{2,1,0:T(8,128)(2,1)S(1)}, u32[]{:S(2)}, u32[]{:S(2)}) collective-permute-start(s16[4,240,256]{2,1,0:T(8,128)(2,1)S(1)} %shard_map.85), channel_id=1, source_target_pairs={{0,11},{1,10},{2,9},{3,8},{4,124},{5,125},{6,126},{7,127},{8,3},{9... | collective-permute-start | bytes 1474568 | tf_op jit(solution)/shard_map/ppermute | solution.py:434
  34.1 0.8 collective-permute-start.11
  35.2 2.3 %collective-permute-start.12 = (s16[4,240,256]{2,1,0:T(8,128)(2,1)S(1)}, s16[4,240,256]{2,1,0:T(8,128)(2,1)S(1)}, u32[]{:S(2)}, u32[]{:S(2)}) collective-permute-start(s16[4,240,256]{2,1,0:T(8,128)(2,1)S(1)} %shard_map.87), channel_id=1, source_target_pairs={{0,3},{1,2},{2,1},{3,0},{4,28},{5,29},{6,30},{7,31},{8,11},{9,10},... | collective-permute-start | bytes 1474568 | tf_op jit(solution)/shard_map/ppermute | solution.py:434
  37.5 4.8 %shard_map.88 = bf16[2,8,64,256]{3,2,1,0:T(8,128)(2,1)} custom-call(bf16[3,10,10,16,256]{4,3,2,1,0:T(8,128)(2,1)S(1)} %shard_map.80.wide, bf16[27,256,256]{2,1,0:T(8,128)(2,1)S(1)} %copy-done, bf16[8,128,128]{2,1,0:T(8,128)(2,1)S(1)} %get-tuple-element.61.masks), custom_call_target="tpu_custom_call" | custom-call | tf_op jit(solution)/shard_map/pallas_call | solution.py:90
  42.3 3.5 %collective-permute-done.11.got_2 = s16[4,240,256]{2,1,0:T(8,128)(2,1)S(1)} collective-permute-done((s16[4,240,256]{2,1,0:T(8,128)(2,1)S(1)}, s16[4,240,256]{2,1,0:T(8,128)(2,1)S(1)}, u32[]{:S(2)}, u32[]{:S(2)}) %collective-permute-start.11) | collective-permute-done | bytes 491552 | tf_op jit(solution)/shard_map/ppermute | solution.py:434
  45.9 0.6 shard_map.90
  46.4 4.9 %collective-permute-start.13 = (s16[1,240,256]{2,1,0:T(8,128)(2,1)S(1)}, s16[1,240,256]{2,1,0:T(8,128)(2,1)S(1)}, u32[]{:S(2)}, u32[]{:S(2)}) collective-permute-start(s16[1,240,256]{2,1,0:T(8,128)(2,1)S(1)} %get-tuple-element.65), channel_id=1, source_target_pairs={{0,33},{1,32},{2,35},{3,34},{4,37},{5,36},{6,39},{7,38},{8,41},{9,... | collective-permute-start | bytes 368648 | tf_op jit(solution)/shard_map/ppermute | solution.py:81
  51.8 3.4 %collective-permute-done.13.got_1 = s16[1,240,256]{2,1,0:T(8,128)(2,1)S(1)} collective-permute-done((s16[1,240,256]{2,1,0:T(8,128)(2,1)S(1)}, s16[1,240,256]{2,1,0:T(8,128)(2,1)S(1)}, u32[]{:S(2)}, u32[]{:S(2)}) %collective-permute-start.13) | collective-permute-done | bytes 122912 | tf_op jit(solution)/shard_map/ppermute | solution.py:81
  55.2 1.7 %collective-permute-done.14.got_2 = s16[1,240,256]{2,1,0:T(8,128)(2,1)S(1)} collective-permute-done((s16[1,240,256]{2,1,0:T(8,128)(2,1)S(1)}, s16[1,240,256]{2,1,0:T(8,128)(2,1)S(1)}, u32[]{:S(2)}, u32[]{:S(2)}) %collective-permute-start.14) | collective-permute-done | bytes 122912 | tf_op jit(solution)/shard_map/ppermute | solution.py:81
  56.9 0.9 collective-permute-done.15.got_3
  58.1 1.9 %collective-permute-start.17 = (s16[1,240,256]{2,1,0:T(8,128)(2,1)S(1)}, s16[1,240,256]{2,1,0:T(8,128)(2,1)S(1)}, u32[]{:S(2)}, u32[]{:S(2)}) collective-permute-start(s16[1,240,256]{2,1,0:T(8,128)(2,1)S(1)} %shard_map.91.own), channel_id=1, source_target_pairs={{0,96},{1,97},{2,98},{3,99},{4,12},{5,13},{6,14},{7,15},{8,104},{9... | collective-permute-start | bytes 368648 | tf_op jit(solution)/shard_map/ppermute | solution.py:81
  60.0 2.0 %collective-permute-start.18 = (s16[1,240,256]{2,1,0:T(8,128)(2,1)S(1)}, s16[1,240,256]{2,1,0:T(8,128)(2,1)S(1)}, u32[]{:S(2)}, u32[]{:S(2)}) collective-permute-start(s16[1,240,256]{2,1,0:T(8,128)(2,1)S(1)} %shard_map.91.own), channel_id=1, source_target_pairs={{0,24},{1,25},{2,26},{3,27},{4,7},{5,6},{6,5},{7,4},{8,16},{9,17},... | collective-permute-start | bytes 368648 | tf_op jit(solution)/shard_map/ppermute | solution.py:81
  61.9 2.0 %collective-permute-done.16.got_1 = s16[1,240,256]{2,1,0:T(8,128)(2,1)S(1)} collective-permute-done((s16[1,240,256]{2,1,0:T(8,128)(2,1)S(1)}, s16[1,240,256]{2,1,0:T(8,128)(2,1)S(1)}, u32[]{:S(2)}, u32[]{:S(2)}) %collective-permute-start.16) | collective-permute-done | bytes 122912 | tf_op jit(solution)/shard_map/ppermute | solution.py:81
  63.9 1.3 %collective-permute-done.18.got_3 = s16[1,240,256]{2,1,0:T(8,128)(2,1)S(1)} collective-permute-done((s16[1,240,256]{2,1,0:T(8,128)(2,1)S(1)}, s16[1,240,256]{2,1,0:T(8,128)(2,1)S(1)}, u32[]{:S(2)}, u32[]{:S(2)}) %collective-permute-start.18) | collective-permute-done | bytes 122912 | tf_op jit(solution)/shard_map/ppermute | solution.py:81
  65.9 1.4 %collective-permute-start.20 = (s16[1,240,256]{2,1,0:T(8,128)(2,1)S(1)}, s16[1,240,256]{2,1,0:T(8,128)(2,1)S(1)}, u32[]{:S(2)}, u32[]{:S(2)}) collective-permute-start(s16[1,240,256]{2,1,0:T(8,128)(2,1)S(1)} %shard_map.92), channel_id=1, source_target_pairs={{0,1},{1,0},{2,3},{3,2},{4,5},{5,4},{6,7},{7,6},{8,9},{9,8},{10,11... | collective-permute-start | bytes 368648 | tf_op jit(solution)/shard_map/ppermute | solution.py:81
  67.3 0.8 collective-permute-start.21
  68.2 2.0 %collective-permute-done.19 = s16[1,240,256]{2,1,0:T(8,128)(2,1)S(1)} collective-permute-done((s16[1,240,256]{2,1,0:T(8,128)(2,1)S(1)}, s16[1,240,256]{2,1,0:T(8,128)(2,1)S(1)}, u32[]{:S(2)}, u32[]{:S(2)}) %collective-permute-start.19) | collective-permute-done | bytes 122912 | tf_op jit(solution)/shard_map/ppermute | solution.py:81
  70.2 0.7 collective-permute-done.20
  70.9 0.5 collective-permute-done.21
  71.5 3.5 %collective-permute-start.22 = (s16[4,240,256]{2,1,0:T(8,128)(2,1)S(1)}, s16[4,240,256]{2,1,0:T(8,128)(2,1)S(1)}, u32[]{:S(2)}, u32[]{:S(2)}) collective-permute-start(s16[4,240,256]{2,1,0:T(8,128)(2,1)S(1)} %pad_add_fusion.refs_0_), channel_id=1, source_target_pairs={{0,11},{1,10},{2,9},{3,8},{4,124},{5,125},{6,126},{7,127},{8,3},{9... | collective-permute-start | bytes 1474568 | tf_op jit(solution)/shard_map/ppermute | solution.py:81
  75.0 0.8 collective-permute-start.23
  75.8 1.4 %collective-permute-start.24 = (s16[4,240,256]{2,1,0:T(8,128)(2,1)S(1)}, s16[4,240,256]{2,1,0:T(8,128)(2,1)S(1)}, u32[]{:S(2)}, u32[]{:S(2)}) collective-permute-start(s16[4,240,256]{2,1,0:T(8,128)(2,1)S(1)} %pad_add_fusion.refs_0_), channel_id=1, source_target_pairs={{0,3},{1,2},{2,1},{3,0},{4,28},{5,29},{6,30},{7,31},{8,11},{9,10},... | collective-permute-start | bytes 1474568 | tf_op jit(solution)/shard_map/ppermute | solution.py:81
  77.1 6.0 %shard_map.93 = bf16[2,8,64,256]{3,2,1,0:T(8,128)(2,1)} custom-call(s32[2]{0:T(128)S(1)} %pad_add_fusion.1.odd, bf16[3,480,160]{2,1,0:T(8,128)(2,1)S(1)} %shard_map.76.pick, bf16[8,8,16,256]{3,2,1,0:T(8,128)(2,1)S(1)} %get-tuple-element.68.grad, bf16[2,8,16,256]{3,2,1,0:T(8,128)(2,1)S(1)} %collective-permute-done.4.y_a, ...), custom_call_target="tpu_custom_call" | custom-call | tf_op jit(solution)/shard_map/pallas_call | solution.py:90
  83.1 1.5 %shard_map.94.refs_3_ = f32[27,256,256]{2,1,0:T(8,128)} custom-call(s32[6]{0:T(128)S(1)} %stack.30.where, s16[4,240,256]{2,1,0:T(8,128)(2,1)S(1)} %pad_add_fusion.refs_0_), custom_call_target="tpu_custom_call" | custom-call | tf_op jit(solution)/shard_map/pallas_call | solution.py:223
  84.6 2.9 %collective-permute-done.23.refs_1_ = s16[4,240,256]{2,1,0:T(8,128)(2,1)S(1)} collective-permute-done((s16[4,240,256]{2,1,0:T(8,128)(2,1)S(1)}, s16[4,240,256]{2,1,0:T(8,128)(2,1)S(1)}, u32[]{:S(2)}, u32[]{:S(2)}) %collective-permute-start.23) | collective-permute-done | bytes 491552 | tf_op jit(solution)/shard_map/ppermute | solution.py:81
  87.6 0.6 collective-permute-done.24.refs_2_
  88.1 3.2 %collective-permute-start.25 = (s16[4,240,256]{2,1,0:T(8,128)(2,1)S(1)}, s16[4,240,256]{2,1,0:T(8,128)(2,1)S(1)}, u32[]{:S(2)}, u32[]{:S(2)}) collective-permute-start(s16[4,240,256]{2,1,0:T(8,128)(2,1)S(1)} %pad_add_fusion.refs_0_), channel_id=1, source_target_pairs={{0,4},{1,5},{2,6},{3,7},{4,0},{5,1},{6,2},{7,3},{8,12},{9,13},{10,... | collective-permute-start | bytes 1474568 | tf_op jit(solution)/shard_map/ppermute | solution.py:454
  91.9 2.2 %shard_map.95.refs_4_ = f32[27,256,256]{2,1,0:T(8,128)} custom-call(s32[6]{0:T(128)S(1)} %stack.30.where, s16[4,240,256]{2,1,0:T(8,128)(2,1)S(1)} %collective-permute-done.22.refs_0_, s16[4,240,256]{2,1,0:T(8,128)(2,1)S(1)} %collective-permute-done.23.refs_1_, ...), custom_call_target="tpu_custom_call", output_to_operand_aliasing={{}: (4, {})} | custom-call | tf_op jit(solution)/shard_map/pallas_call | solution.py:223
  94.3 0.7 collective-permute-done.28.refs_3_
  95.0 2.6 %shard_map.96 = f32[27,256,256]{2,1,0:T(8,128)} custom-call(s32[6]{0:T(128)S(1)} %stack.30.where, s16[4,240,256]{2,1,0:T(8,128)(2,1)S(1)} %collective-permute-done.25.refs_0_, s16[4,240,256]{2,1,0:T(8,128)(2,1)S(1)} %collective-permute-done.26.refs_1_, s16[4,240,256]{2,1,0:T(8,128)(2,1)S(1)} %collective-permute-done.27.refs_2_, ...), custom_call_target="tpu_custom_call", output_to_operand_aliasing={{}: (5, {})} | custom-call | tf_op jit(solution)/shard_map/pallas_call | solution.py:223
  (44 shorter events, 3.8 us)
Async XLA Ops:
  0.6 2.2 %copy-start.1 = (bf16[2,8,8,8,256]{4,3,2,1,0:T(8,128)(2,1)S(1)}, bf16[2,8,8,8,256]{4,3,2,1,0:T(8,128)(2,1)}, u32[]{:S(2)}) copy-start(bf16[2,8,8,8,256]{4,3,2,1,0:T(8,128)(2,1)} %param.5) | copy-start | bytes 1572868
  0.6 2.2 %copy-start.2 = (bf16[2,8,8,8,256]{4,3,2,1,0:T(8,128)(2,1)S(1)}, bf16[2,8,8,8,256]{4,3,2,1,0:T(8,128)(2,1)}, u32[]{:S(2)}) copy-start(bf16[2,8,8,8,256]{4,3,2,1,0:T(8,128)(2,1)} %param.6) | copy-start | bytes 1572868
  0.7 2.2 %copy-start.3 = (s32[2,512]{1,0:T(2,128)S(1)}, s32[2,512]{1,0:T(2,128)}, u32[]{:S(2)}) copy-start(s32[2,512]{1,0:T(2,128)} %occupancy.1) | copy-start | bytes 12292
  0.7 0.8 copy-start.4
  4.6 4.9 %collective-permute-start = (bf16[2,8,16,256]{3,2,1,0:T(8,128)(2,1)S(1)}, bf16[2,8,16,256]{3,2,1,0:T(8,128)(2,1)S(1)}, u32[]{:S(2)}, u32[]{:S(2)}) collective-permute-start(bf16[2,8,16,256]{3,2,1,0:T(8,128)(2,1)S(1)} %get-tuple-element.40), channel_id=1, source_target_pairs={{0,4},{4,0},{8,12},{12,8},{16,20},{20,16},{24,28},{28,24},{32,36},... | collective-permute-start | bytes 393224 | tf_op jit(solution)/shard_map/ppermute | solution.py:398
  6.0 7.9 %collective-permute-start.1 = (bf16[2,8,16,256]{3,2,1,0:T(8,128)(2,1)S(1)}, bf16[2,8,16,256]{3,2,1,0:T(8,128)(2,1)S(1)}, u32[]{:S(2)}, u32[]{:S(2)}) collective-permute-start(bf16[2,8,16,256]{3,2,1,0:T(8,128)(2,1)S(1)} %get-tuple-element.41), channel_id=1, source_target_pairs={{4,8},{8,4},{12,16},{16,12},{20,24},{24,20},{28,32},{32,28},{36,40... | collective-permute-start | bytes 393224 | tf_op jit(solution)/shard_map/ppermute | solution.py:398
  9.5 5.9 %collective-permute-start.5 = (bf16[2,8,16,256]{3,2,1,0:T(8,128)(2,1)}, bf16[2,8,16,256]{3,2,1,0:T(8,128)(2,1)S(1)}, u32[]{:S(2)}, u32[]{:S(2)}) collective-permute-start(bf16[2,8,16,256]{3,2,1,0:T(8,128)(2,1)} %get-tuple-element.48), channel_id=1, source_target_pairs={{1,2},{2,1},{5,6},{6,5},{9,10},{10,9},{13,14},{14,13},{17,18},{18,... | collective-permute-start | bytes 393224 | tf_op jit(solution)/shard_map/ppermute | solution.py:398
  10.2 6.7 %collective-permute-start.4 = (bf16[2,8,16,256]{3,2,1,0:T(8,128)(2,1)S(1)}, bf16[2,8,16,256]{3,2,1,0:T(8,128)(2,1)S(1)}, u32[]{:S(2)}, u32[]{:S(2)}) collective-permute-start(bf16[2,8,16,256]{3,2,1,0:T(8,128)(2,1)S(1)} %get-tuple-element.46), channel_id=1, source_target_pairs={{0,1},{1,0},{2,3},{3,2},{4,5},{5,4},{6,7},{7,6},{8,9},{9,8},{10,11... | collective-permute-start | bytes 393224 | tf_op jit(solution)/shard_map/ppermute | solution.py:398
  14.5 3.6 %collective-permute-start.2 = (bf16[2,2,16,256]{3,2,1,0:T(8,128)(2,1)S(1)}, bf16[2,2,16,256]{3,2,1,0:T(8,128)(2,1)S(1)}, u32[]{:S(2)}, u32[]{:S(2)}) collective-permute-start(bf16[2,2,16,256]{3,2,1,0:T(8,128)(2,1)S(1)} %get-tuple-element.42), channel_id=1, source_target_pairs={{0,1},{1,0},{2,3},{3,2},{4,5},{5,4},{6,7},{7,6},{8,9},{9,8},{10,11... | collective-permute-start | bytes 98312 | tf_op jit(solution)/shard_map/ppermute | solution.py:398
  14.6 3.5 %collective-permute-start.3 = (bf16[2,2,16,256]{3,2,1,0:T(8,128)(2,1)S(1)}, bf16[2,2,16,256]{3,2,1,0:T(8,128)(2,1)S(1)}, u32[]{:S(2)}, u32[]{:S(2)}) collective-permute-start(bf16[2,2,16,256]{3,2,1,0:T(8,128)(2,1)S(1)} %get-tuple-element.43), channel_id=1, source_target_pairs={{1,2},{2,1},{5,6},{6,5},{9,10},{10,9},{13,14},{14,13},{17,18},{18,... | collective-permute-start | bytes 98312 | tf_op jit(solution)/shard_map/ppermute | solution.py:398
  20.7 2.5 %collective-permute-start.6 = (s16[4,240,256]{2,1,0:T(8,128)(2,1)S(1)}, s16[4,240,256]{2,1,0:T(8,128)(2,1)S(1)}, u32[]{:S(2)}, u32[]{:S(2)}) collective-permute-start(s16[4,240,256]{2,1,0:T(8,128)(2,1)S(1)} %get-tuple-element.53), channel_id=1, source_target_pairs={{0,4},{1,5},{2,6},{3,7},{4,0},{5,1},{6,2},{7,3},{8,12},{9,13},{10,... | collective-permute-start | bytes 1474568 | tf_op jit(solution)/shard_map/ppermute | solution.py:431
  22.6 14.9 %copy-start = (bf16[27,256,256]{2,1,0:T(8,128)(2,1)S(1)}, bf16[27,256,256]{2,1,0:T(8,128)(2,1)}, u32[]{:S(2)}) copy-start(bf16[27,256,256]{2,1,0:T(8,128)(2,1)} %kernel.3) | copy-start | bytes 10616836
  22.6 2.6 %collective-permute-start.7 = (s16[4,240,256]{2,1,0:T(8,128)(2,1)S(1)}, s16[4,240,256]{2,1,0:T(8,128)(2,1)S(1)}, u32[]{:S(2)}, u32[]{:S(2)}) collective-permute-start(s16[4,240,256]{2,1,0:T(8,128)(2,1)S(1)} %get-tuple-element.56), channel_id=1, source_target_pairs={{0,4},{1,5},{2,6},{3,7},{4,0},{5,1},{6,2},{7,3},{8,12},{9,13},{10,... | collective-permute-start | bytes 1474568 | tf_op jit(solution)/shard_map/ppermute | solution.py:431
  25.1 8.6 %collective-permute-start.10 = (s16[4,240,256]{2,1,0:T(8,128)(2,1)S(1)}, s16[4,240,256]{2,1,0:T(8,128)(2,1)S(1)}, u32[]{:S(2)}, u32[]{:S(2)}) collective-permute-start(s16[4,240,256]{2,1,0:T(8,128)(2,1)S(1)} %get-tuple-element.63), channel_id=1, source_target_pairs={{0,4},{1,5},{2,6},{3,7},{4,0},{5,1},{6,2},{7,3},{8,12},{9,13},{10,... | collective-permute-start | bytes 1474568 | tf_op jit(solution)/shard_map/ppermute | solution.py:431
  27.4 7.4 %collective-permute-start.8 = (s16[4,240,256]{2,1,0:T(8,128)(2,1)S(1)}, s16[4,240,256]{2,1,0:T(8,128)(2,1)S(1)}, u32[]{:S(2)}, u32[]{:S(2)}) collective-permute-start(s16[4,240,256]{2,1,0:T(8,128)(2,1)S(1)} %get-tuple-element.59), channel_id=1, source_target_pairs={{0,4},{1,5},{2,6},{3,7},{4,0},{5,1},{6,2},{7,3},{8,12},{9,13},{10,... | collective-permute-start | bytes 1474568 | tf_op jit(solution)/shard_map/ppermute | solution.py:431
  28.0 14.3 %collective-permute-start.9 = (s16[4,240,256]{2,1,0:T(8,128)(2,1)S(1)}, s16[4,240,256]{2,1,0:T(8,128)(2,1)S(1)}, u32[]{:S(2)}, u32[]{:S(2)}) collective-permute-start(s16[4,240,256]{2,1,0:T(8,128)(2,1)S(1)} %shard_map.85), channel_id=1, source_target_pairs={{0,11},{1,10},{2,9},{3,8},{4,124},{5,125},{6,126},{7,127},{8,3},{9... | collective-permute-start | bytes 1474568 | tf_op jit(solution)/shard_map/ppermute | solution.py:434
  34.1 11.8 %collective-permute-start.11 = (s16[4,240,256]{2,1,0:T(8,128)(2,1)S(1)}, s16[4,240,256]{2,1,0:T(8,128)(2,1)S(1)}, u32[]{:S(2)}, u32[]{:S(2)}) collective-permute-start(s16[4,240,256]{2,1,0:T(8,128)(2,1)S(1)} %shard_map.89), channel_id=1, source_target_pairs={{0,8},{1,9},{2,10},{3,11},{4,100},{5,101},{6,102},{7,103},{8,0},{9... | collective-permute-start | bytes 1474568 | tf_op jit(solution)/shard_map/ppermute | solution.py:434
  35.2 10.7 %collective-permute-start.12 = (s16[4,240,256]{2,1,0:T(8,128)(2,1)S(1)}, s16[4,240,256]{2,1,0:T(8,128)(2,1)S(1)}, u32[]{:S(2)}, u32[]{:S(2)}) collective-permute-start(s16[4,240,256]{2,1,0:T(8,128)(2,1)S(1)} %shard_map.87), channel_id=1, source_target_pairs={{0,3},{1,2},{2,1},{3,0},{4,28},{5,29},{6,30},{7,31},{8,11},{9,10},... | collective-permute-start | bytes 1474568 | tf_op jit(solution)/shard_map/ppermute | solution.py:434
  46.4 8.7 %collective-permute-start.13 = (s16[1,240,256]{2,1,0:T(8,128)(2,1)S(1)}, s16[1,240,256]{2,1,0:T(8,128)(2,1)S(1)}, u32[]{:S(2)}, u32[]{:S(2)}) collective-permute-start(s16[1,240,256]{2,1,0:T(8,128)(2,1)S(1)} %get-tuple-element.65), channel_id=1, source_target_pairs={{0,33},{1,32},{2,35},{3,34},{4,37},{5,36},{6,39},{7,38},{8,41},{9,... | collective-permute-start | bytes 368648 | tf_op jit(solution)/shard_map/ppermute | solution.py:81
  51.4 5.5 %collective-permute-start.14 = (s16[1,240,256]{2,1,0:T(8,128)(2,1)S(1)}, s16[1,240,256]{2,1,0:T(8,128)(2,1)S(1)}, u32[]{:S(2)}, u32[]{:S(2)}) collective-permute-start(s16[1,240,256]{2,1,0:T(8,128)(2,1)S(1)} %get-tuple-element.66), channel_id=1, source_target_pairs={{0,1},{1,0},{2,3},{3,2},{4,5},{5,4},{6,7},{7,6},{8,9},{9,8},{10,11... | collective-permute-start | bytes 368648 | tf_op jit(solution)/shard_map/ppermute | solution.py:81
  51.4 6.4 %collective-permute-start.15 = (s16[1,240,256]{2,1,0:T(8,128)(2,1)S(1)}, s16[1,240,256]{2,1,0:T(8,128)(2,1)S(1)}, u32[]{:S(2)}, u32[]{:S(2)}) collective-permute-start(s16[1,240,256]{2,1,0:T(8,128)(2,1)S(1)} %get-tuple-element.67), channel_id=1, source_target_pairs={{0,32},{1,33},{2,34},{3,35},{4,36},{5,37},{6,38},{7,39},{8,40},{9,... | collective-permute-start | bytes 368648 | tf_op jit(solution)/shard_map/ppermute | solution.py:81
  58.0 5.9 %collective-permute-start.16 = (s16[1,240,256]{2,1,0:T(8,128)(2,1)S(1)}, s16[1,240,256]{2,1,0:T(8,128)(2,1)S(1)}, u32[]{:S(2)}, u32[]{:S(2)}) collective-permute-start(s16[1,240,256]{2,1,0:T(8,128)(2,1)S(1)} %shard_map.91.own), channel_id=1, source_target_pairs={{0,120},{1,121},{2,122},{3,123},{4,15},{5,14},{6,13},{7,12},{8,112... | collective-permute-start | bytes 368648 | tf_op jit(solution)/shard_map/ppermute | solution.py:81
  58.1 5.8 %collective-permute-start.17 = (s16[1,240,256]{2,1,0:T(8,128)(2,1)S(1)}, s16[1,240,256]{2,1,0:T(8,128)(2,1)S(1)}, u32[]{:S(2)}, u32[]{:S(2)}) collective-permute-start(s16[1,240,256]{2,1,0:T(8,128)(2,1)S(1)} %shard_map.91.own), channel_id=1, source_target_pairs={{0,96},{1,97},{2,98},{3,99},{4,12},{5,13},{6,14},{7,15},{8,104},{9... | collective-permute-start | bytes 368648 | tf_op jit(solution)/shard_map/ppermute | solution.py:81
  60.0 5.2 %collective-permute-start.18 = (s16[1,240,256]{2,1,0:T(8,128)(2,1)S(1)}, s16[1,240,256]{2,1,0:T(8,128)(2,1)S(1)}, u32[]{:S(2)}, u32[]{:S(2)}) collective-permute-start(s16[1,240,256]{2,1,0:T(8,128)(2,1)S(1)} %shard_map.91.own), channel_id=1, source_target_pairs={{0,24},{1,25},{2,26},{3,27},{4,7},{5,6},{6,5},{7,4},{8,16},{9,17},... | collective-permute-start | bytes 368648 | tf_op jit(solution)/shard_map/ppermute | solution.py:81
  65.4 4.7 %collective-permute-start.19 = (s16[1,240,256]{2,1,0:T(8,128)(2,1)S(1)}, s16[1,240,256]{2,1,0:T(8,128)(2,1)S(1)}, u32[]{:S(2)}, u32[]{:S(2)}) collective-permute-start(s16[1,240,256]{2,1,0:T(8,128)(2,1)S(1)} %shard_map.92), channel_id=1, source_target_pairs={{0,33},{1,32},{2,35},{3,34},{4,37},{5,36},{6,39},{7,38},{8,41},{9,... | collective-permute-start | bytes 368648 | tf_op jit(solution)/shard_map/ppermute | solution.py:81
  65.9 5.0 %collective-permute-start.20 = (s16[1,240,256]{2,1,0:T(8,128)(2,1)S(1)}, s16[1,240,256]{2,1,0:T(8,128)(2,1)S(1)}, u32[]{:S(2)}, u32[]{:S(2)}) collective-permute-start(s16[1,240,256]{2,1,0:T(8,128)(2,1)S(1)} %shard_map.92), channel_id=1, source_target_pairs={{0,1},{1,0},{2,3},{3,2},{4,5},{5,4},{6,7},{7,6},{8,9},{9,8},{10,11... | collective-permute-start | bytes 368648 | tf_op jit(solution)/shard_map/ppermute | solution.py:81
  67.3 4.1 %collective-permute-start.21 = (s16[1,240,256]{2,1,0:T(8,128)(2,1)S(1)}, s16[1,240,256]{2,1,0:T(8,128)(2,1)S(1)}, u32[]{:S(2)}, u32[]{:S(2)}) collective-permute-start(s16[1,240,256]{2,1,0:T(8,128)(2,1)S(1)} %shard_map.92), channel_id=1, source_target_pairs={{0,32},{1,33},{2,34},{3,35},{4,36},{5,37},{6,38},{7,39},{8,40},{9,... | collective-permute-start | bytes 368648 | tf_op jit(solution)/shard_map/ppermute | solution.py:81
  71.5 13.1 %collective-permute-start.22 = (s16[4,240,256]{2,1,0:T(8,128)(2,1)S(1)}, s16[4,240,256]{2,1,0:T(8,128)(2,1)S(1)}, u32[]{:S(2)}, u32[]{:S(2)}) collective-permute-start(s16[4,240,256]{2,1,0:T(8,128)(2,1)S(1)} %pad_add_fusion.refs_0_), channel_id=1, source_target_pairs={{0,11},{1,10},{2,9},{3,8},{4,124},{5,125},{6,126},{7,127},{8,3},{9... | collective-permute-start | bytes 1474568 | tf_op jit(solution)/shard_map/ppermute | solution.py:81
  75.0 12.6 %collective-permute-start.23 = (s16[4,240,256]{2,1,0:T(8,128)(2,1)S(1)}, s16[4,240,256]{2,1,0:T(8,128)(2,1)S(1)}, u32[]{:S(2)}, u32[]{:S(2)}) collective-permute-start(s16[4,240,256]{2,1,0:T(8,128)(2,1)S(1)} %pad_add_fusion.refs_0_), channel_id=1, source_target_pairs={{0,8},{1,9},{2,10},{3,11},{4,100},{5,101},{6,102},{7,103},{8,0},{9... | collective-permute-start | bytes 1474568 | tf_op jit(solution)/shard_map/ppermute | solution.py:81
  75.8 12.4 %collective-permute-start.24 = (s16[4,240,256]{2,1,0:T(8,128)(2,1)S(1)}, s16[4,240,256]{2,1,0:T(8,128)(2,1)S(1)}, u32[]{:S(2)}, u32[]{:S(2)}) collective-permute-start(s16[4,240,256]{2,1,0:T(8,128)(2,1)S(1)} %pad_add_fusion.refs_0_), channel_id=1, source_target_pairs={{0,3},{1,2},{2,1},{3,0},{4,28},{5,29},{6,30},{7,31},{8,11},{9,10},... | collective-permute-start | bytes 1474568 | tf_op jit(solution)/shard_map/ppermute | solution.py:81
  88.1 6.0 %collective-permute-start.25 = (s16[4,240,256]{2,1,0:T(8,128)(2,1)S(1)}, s16[4,240,256]{2,1,0:T(8,128)(2,1)S(1)}, u32[]{:S(2)}, u32[]{:S(2)}) collective-permute-start(s16[4,240,256]{2,1,0:T(8,128)(2,1)S(1)} %pad_add_fusion.refs_0_), channel_id=1, source_target_pairs={{0,4},{1,5},{2,6},{3,7},{4,0},{5,1},{6,2},{7,3},{8,12},{9,13},{10,... | collective-permute-start | bytes 1474568 | tf_op jit(solution)/shard_map/ppermute | solution.py:454
  91.4 2.8 %collective-permute-start.26 = (s16[4,240,256]{2,1,0:T(8,128)(2,1)S(1)}, s16[4,240,256]{2,1,0:T(8,128)(2,1)S(1)}, u32[]{:S(2)}, u32[]{:S(2)}) collective-permute-start(s16[4,240,256]{2,1,0:T(8,128)(2,1)S(1)} %collective-permute-done.22.refs_0_), channel_id=1, source_target_pairs={{0,4},{1,5},{2,6},{3,7},{4,0},{5,1},{6,2},{7,3},{8,12},{9,13},{10,... | collective-permute-start | bytes 1474568 | tf_op jit(solution)/shard_map/ppermute | solution.py:454
  91.4 2.9 %collective-permute-start.27 = (s16[4,240,256]{2,1,0:T(8,128)(2,1)S(1)}, s16[4,240,256]{2,1,0:T(8,128)(2,1)S(1)}, u32[]{:S(2)}, u32[]{:S(2)}) collective-permute-start(s16[4,240,256]{2,1,0:T(8,128)(2,1)S(1)} %collective-permute-done.23.refs_1_), channel_id=1, source_target_pairs={{0,4},{1,5},{2,6},{3,7},{4,0},{5,1},{6,2},{7,3},{8,12},{9,13},{10,... | collective-permute-start | bytes 1474568 | tf_op jit(solution)/shard_map/ppermute | solution.py:454
  91.9 3.1 %collective-permute-start.28 = (s16[4,240,256]{2,1,0:T(8,128)(2,1)S(1)}, s16[4,240,256]{2,1,0:T(8,128)(2,1)S(1)}, u32[]{:S(2)}, u32[]{:S(2)}) collective-permute-start(s16[4,240,256]{2,1,0:T(8,128)(2,1)S(1)} %collective-permute-done.24.refs_2_), channel_id=1, source_target_pairs={{0,4},{1,5},{2,6},{3,7},{4,0},{5,1},{6,2},{7,3},{8,12},{9,13},{10,... | collective-permute-start | bytes 1474568 | tf_op jit(solution)/shard_map/ppermute | solution.py:454

commit v5 on v4

--- a/solution.py
+++ b/solution.py
@@ -264,24 +264,23 @@
 
 
 def picks_kernel(neighbors, out):
-    r = lax.broadcasted_iota(jnp.int32, (160, 160), 0)
     c = lax.broadcasted_iota(jnp.int32, (160, 160), 1)
+    r = lax.broadcasted_iota(jnp.int32, (160, 1), 0)
     y, s, z = r >> 4, (r >> 3) & 1, r & 7
-    same = y == c >> 4
     side_y = jnp.where(y == 0, 0, jnp.where(y == 9, 2, 1))
     which = side_y * 2 + s
     for ox in range(3):
         for oz in range(3):
             edge = z == (0 if oz == 0 else 7)
-            slot = jnp.full((160, 160), -1, jnp.int32)
+            slot = jnp.full((160, 1), -1, jnp.int32)
             for oy in range(3):
                 for brick in range(2):
                     level = neighbors[brick, 9 * ox + 3 * oy + 1]
                     beyond = neighbors[brick, 9 * ox + 3 * oy + oz]
                     found = jnp.where(edge, beyond, level) if oz != 1 else level
                     slot = jnp.where(which == 2 * oy + brick, found, slot)
-            hit = same & (slot >= 0) & ((c & 15) == slot * 8 + ((z + oz - 1) & 7))
-            out[ox, 160 * oz : 160 * (oz + 1), :] = jnp.where(hit, 1.0, 0.0).astype(jnp.bfloat16)
+            target = jnp.where(slot >= 0, y * 16 + slot * 8 + ((z + oz - 1) & 7), -1)
+            out[ox, 160 * oz : 160 * (oz + 1), :] = jnp.where(c == target, 1.0, 0.0).astype(jnp.bfloat16)
 
 
 def corners_kernel(odd, x_a, x_b, c_a, c_b):

time: 97.9 us -> 97.8 us (level)
  no operation moved by 1% of the time
where the time goes in v5:
time: 97.8 us; the launch traced here: 97.7 us
  starting transfers between devices  41.6 us (43%)
  Pallas kernels  32 us (33%)
  waiting for transfers between devices  22 us (22%)
  between operations  1.14 us (1%)
    pallas_call x18, Pallas kernels, call(): pl.pallas_call(kernel, out_shape=list(outs), in_specs=[SMEM if a.dtype ==...  25.6 us
    ppermute x12, starting transfers between devices, exchange(): lax.ppermute(arrays[m - 1], BOTH, partners(level, m))  17.6 us
    ppermute x12, waiting for transfers between devices, exchange(): lax.ppermute(arrays[m - 1], BOTH, partners(level, m))  16.2 us
    ppermute x6, starting transfers between devices, swap(): return [lax.ppermute(a, axis, p) for a, p in zip(arrays, pairs)]  10.1 us
    ppermute x3, starting transfers between devices, shards(): got[m] = lax.ppermute(sums[m], BOTH, partners(0, m))  8.81 us
    pallas_call x3, Pallas kernels, finish(): pl.pallas_call(functools.partial(finish_kernel, scale, parts), out_shape=...  6.33 us
    ppermute x4, starting transfers between devices, other(): return lax.ppermute(a, BOTH, other_core())  3.75 us
    ppermute x3, waiting for transfers between devices, shards(): got[m] = lax.ppermute(sums[m], BOTH, partners(0, m))  3.53 us
  transfers between devices with their start and end apart: 29, of which 14 were waited for; matrix products, arithmetic and copies ran while one was open for 0% of the time, Pallas kernels for 23%

profile of v5, /device:TPU:1, one launch (start us, length us, event | category | flops | bytes accessed | tf_op | source)
XLA Modules:
  0.0 97.7 jit_solution(14680479780947185928)
XLA Ops:
  0.7 0.8 copy-done.4
  1.4 1.3 %shard_map.76.pick = bf16[3,480,160]{2,1,0:T(8,128)(2,1)S(1)} custom-call(s32[2,27]{1,0:T(2,128)S(1)} %copy-done.4), custom_call_target="tpu_custom_call" | custom-call | flops 2147483648 | bytes 4194304 | tf_op jit(solution)/shard_map/pallas_call | solution.py:90
  2.8 1.7 %shard_map.77 = (bf16[8,8,16,256]{3,2,1,0:T(8,128)(2,1)S(1)}, bf16[8,8,16,256]{3,2,1,0:T(8,128)(2,1)S(1)}, bf16[8,128,128]{2,1,0:T(8,128)(2,1)S(1)}, bf16[2,8,16...) custom-call(s32[2]{0:T(128)S(1)} %pad_add_fusion.1.odd, ...), custom_call_target="tpu_custom_call" | custom-call | tf_op jit(solution)/shard_map/pallas_call | solution.py:90
  4.5 1.4 %collective-permute-start = (bf16[2,8,16,256]{3,2,1,0:T(8,128)(2,1)S(1)}, bf16[2,8,16,256]{3,2,1,0:T(8,128)(2,1)S(1)}, u32[]{:S(2)}, u32[]{:S(2)}) collective-permute-start(bf16[2,8,16,256]{3,2,1,0:T(8,128)(2,1)S(1)} %get-tuple-element.40), channel_id=1, source_target_pairs={{0,4},{4,0},{8,12},{12,8},{16,20},{20,16},{24,28},{28,24},{32,36},... | collective-permute-start | bytes 393224 | tf_op jit(solution)/shard_map/ppermute | solution.py:397
  5.9 3.5 %collective-permute-start.1 = (bf16[2,8,16,256]{3,2,1,0:T(8,128)(2,1)S(1)}, bf16[2,8,16,256]{3,2,1,0:T(8,128)(2,1)S(1)}, u32[]{:S(2)}, u32[]{:S(2)}) collective-permute-start(bf16[2,8,16,256]{3,2,1,0:T(8,128)(2,1)S(1)} %get-tuple-element.41), channel_id=1, source_target_pairs={{4,8},{8,4},{12,16},{16,12},{20,24},{24,20},{28,32},{32,28},{36,40... | collective-permute-start | bytes 393224 | tf_op jit(solution)/shard_map/ppermute | solution.py:397
  9.5 0.7 collective-permute-start.5
  10.1 3.7 %collective-permute-start.4 = (bf16[2,8,16,256]{3,2,1,0:T(8,128)(2,1)S(1)}, bf16[2,8,16,256]{3,2,1,0:T(8,128)(2,1)S(1)}, u32[]{:S(2)}, u32[]{:S(2)}) collective-permute-start(bf16[2,8,16,256]{3,2,1,0:T(8,128)(2,1)S(1)} %get-tuple-element.46), channel_id=1, source_target_pairs={{0,1},{1,0},{2,3},{3,2},{4,5},{5,4},{6,7},{7,6},{8,9},{9,8},{10,11... | collective-permute-start | bytes 393224 | tf_op jit(solution)/shard_map/ppermute | solution.py:397
  13.9 0.6 shard_map.78
  14.5 0.7 collective-permute-start.3
  15.3 1.5 %collective-permute-done.4.y_a = bf16[2,8,16,256]{3,2,1,0:T(8,128)(2,1)S(1)} collective-permute-done((bf16[2,8,16,256]{3,2,1,0:T(8,128)(2,1)S(1)}, bf16[2,8,16,256]{3,2,1,0:T(8,128)(2,1)S(1)}, u32[]{:S(2)}, u32[]{:S(2)}) %collective-permute-start.4) | collective-permute-done | bytes 131104 | tf_op jit(solution)/shard_map/ppermute | solution.py:397
  16.8 1.2 %shard_map.79._ = bf16[3,10,10,16,256]{4,3,2,1,0:T(8,128)(2,1)S(1)} custom-call(s32[2]{0:T(128)S(1)} %pad_add_fusion.1.odd, bf16[3,480,160]{2,1,0:T(8,128)(2,1)S(1)} %shard_map.76.pick, bf16[8,8,16,256]{3,2,1,0:T(8,128)(2,1)S(1)} %get-tuple-element.44.cells, bf16[2,8,16,256]{3,2,1,0:T(8,128)(2,1)S(1)} %collective-permute-done.4.y_a, ...), custom_call_target="tpu_custom_call" | custom-call | tf_op jit(solution)/shard_map/pallas_call | solution.py:90
  18.1 0.8 shard_map.80.wide
  18.9 1.8 %shard_map.81 = (f32[896,256]{1,0:T(8,128)S(1)}, s16[4,240,256]{2,1,0:T(8,128)(2,1)S(1)}) custom-call(s32[6]{0:T(128)S(1)} %stack.30.where, bf16[3,10,10,16,256]{4,3,2,1,0:T(8,128)(2,1)S(1)} %shard_map.80.wide, bf16[8,8,16,256]{3,2,1,0:T(8,128)(2,1)S(1)} %get-tuple-element.68.grad), custom_call_target="tpu_custom_call" | custom-call | tf_op jit(solution)/shard_map/pallas_call | solution.py:90
  20.8 1.8 %shard_map.82 = (f32[896,256]{1,0:T(8,128)S(1)}, s16[4,240,256]{2,1,0:T(8,128)(2,1)S(1)}) custom-call(s32[6]{0:T(128)S(1)} %stack.30.where, bf16[3,10,10,16,256]{4,3,2,1,0:T(8,128)(2,1)S(1)} %shard_map.80.wide, bf16[8,8,16,256]{3,2,1,0:T(8,128)(2,1)S(1)} %get-tuple-element.68.grad), custom_call_target="tpu_custom_call" | custom-call | tf_op jit(solution)/shard_map/pallas_call | solution.py:90
  22.6 0.6 collective-permute-start.7
  23.3 1.8 %shard_map.84 = (f32[896,256]{1,0:T(8,128)S(1)}, s16[4,240,256]{2,1,0:T(8,128)(2,1)S(1)}) custom-call(s32[6]{0:T(128)S(1)} %stack.30.where, bf16[3,10,10,16,256]{4,3,2,1,0:T(8,128)(2,1)S(1)} %shard_map.80.wide, bf16[8,8,16,256]{3,2,1,0:T(8,128)(2,1)S(1)} %get-tuple-element.68.grad), custom_call_target="tpu_custom_call" | custom-call | tf_op jit(solution)/shard_map/pallas_call | solution.py:90
  25.6 1.8 %shard_map.86 = (f32[896,256]{1,0:T(8,128)S(1)}, s16[4,240,256]{2,1,0:T(8,128)(2,1)S(1)}) custom-call(s32[6]{0:T(128)S(1)} %stack.30.where, bf16[3,10,10,16,256]{4,3,2,1,0:T(8,128)(2,1)S(1)} %shard_map.80.wide, bf16[8,8,16,256]{3,2,1,0:T(8,128)(2,1)S(1)} %get-tuple-element.68.grad), custom_call_target="tpu_custom_call" | custom-call | tf_op jit(solution)/shard_map/pallas_call | solution.py:90
  27.4 0.6 collective-permute-start.8
  27.9 5.7 %collective-permute-start.9 = (s16[4,240,256]{2,1,0:T(8,128)(2,1)S(1)}, s16[4,240,256]{2,1,0:T(8,128)(2,1)S(1)}, u32[]{:S(2)}, u32[]{:S(2)}) collective-permute-start(s16[4,240,256]{2,1,0:T(8,128)(2,1)S(1)} %shard_map.85), channel_id=1, source_target_pairs={{0,11},{1,10},{2,9},{3,8},{4,124},{5,125},{6,126},{7,127},{8,3},{9... | collective-permute-start | bytes 1474568 | tf_op jit(solution)/shard_map/ppermute | solution.py:433
  34.0 0.7 collective-permute-start.11
  35.2 2.3 %collective-permute-start.12 = (s16[4,240,256]{2,1,0:T(8,128)(2,1)S(1)}, s16[4,240,256]{2,1,0:T(8,128)(2,1)S(1)}, u32[]{:S(2)}, u32[]{:S(2)}) collective-permute-start(s16[4,240,256]{2,1,0:T(8,128)(2,1)S(1)} %shard_map.87), channel_id=1, source_target_pairs={{0,3},{1,2},{2,1},{3,0},{4,28},{5,29},{6,30},{7,31},{8,11},{9,10},... | collective-permute-start | bytes 1474568 | tf_op jit(solution)/shard_map/ppermute | solution.py:433
  37.5 4.8 %shard_map.88 = bf16[2,8,64,256]{3,2,1,0:T(8,128)(2,1)} custom-call(bf16[3,10,10,16,256]{4,3,2,1,0:T(8,128)(2,1)S(1)} %shard_map.80.wide, bf16[27,256,256]{2,1,0:T(8,128)(2,1)S(1)} %copy-done, bf16[8,128,128]{2,1,0:T(8,128)(2,1)S(1)} %get-tuple-element.61.masks), custom_call_target="tpu_custom_call" | custom-call | tf_op jit(solution)/shard_map/pallas_call | solution.py:90
  42.3 3.5 %collective-permute-done.11.got_2 = s16[4,240,256]{2,1,0:T(8,128)(2,1)S(1)} collective-permute-done((s16[4,240,256]{2,1,0:T(8,128)(2,1)S(1)}, s16[4,240,256]{2,1,0:T(8,128)(2,1)S(1)}, u32[]{:S(2)}, u32[]{:S(2)}) %collective-permute-start.11) | collective-permute-done | bytes 491552 | tf_op jit(solution)/shard_map/ppermute | solution.py:433
  45.8 0.6 shard_map.90
  46.4 4.9 %collective-permute-start.13 = (s16[1,240,256]{2,1,0:T(8,128)(2,1)S(1)}, s16[1,240,256]{2,1,0:T(8,128)(2,1)S(1)}, u32[]{:S(2)}, u32[]{:S(2)}) collective-permute-start(s16[1,240,256]{2,1,0:T(8,128)(2,1)S(1)} %get-tuple-element.65), channel_id=1, source_target_pairs={{0,33},{1,32},{2,35},{3,34},{4,37},{5,36},{6,39},{7,38},{8,41},{9,... | collective-permute-start | bytes 368648 | tf_op jit(solution)/shard_map/ppermute | solution.py:81
  51.7 3.4 %collective-permute-done.13.got_1 = s16[1,240,256]{2,1,0:T(8,128)(2,1)S(1)} collective-permute-done((s16[1,240,256]{2,1,0:T(8,128)(2,1)S(1)}, s16[1,240,256]{2,1,0:T(8,128)(2,1)S(1)}, u32[]{:S(2)}, u32[]{:S(2)}) %collective-permute-start.13) | collective-permute-done | bytes 122912 | tf_op jit(solution)/shard_map/ppermute | solution.py:81
  55.1 1.7 %collective-permute-done.14.got_2 = s16[1,240,256]{2,1,0:T(8,128)(2,1)S(1)} collective-permute-done((s16[1,240,256]{2,1,0:T(8,128)(2,1)S(1)}, s16[1,240,256]{2,1,0:T(8,128)(2,1)S(1)}, u32[]{:S(2)}, u32[]{:S(2)}) %collective-permute-start.14) | collective-permute-done | bytes 122912 | tf_op jit(solution)/shard_map/ppermute | solution.py:81
  56.9 0.9 collective-permute-done.15.got_3
  58.1 1.9 %collective-permute-start.17 = (s16[1,240,256]{2,1,0:T(8,128)(2,1)S(1)}, s16[1,240,256]{2,1,0:T(8,128)(2,1)S(1)}, u32[]{:S(2)}, u32[]{:S(2)}) collective-permute-start(s16[1,240,256]{2,1,0:T(8,128)(2,1)S(1)} %shard_map.91.own), channel_id=1, source_target_pairs={{0,96},{1,97},{2,98},{3,99},{4,12},{5,13},{6,14},{7,15},{8,104},{9... | collective-permute-start | bytes 368648 | tf_op jit(solution)/shard_map/ppermute | solution.py:81
  60.0 2.0 %collective-permute-start.18 = (s16[1,240,256]{2,1,0:T(8,128)(2,1)S(1)}, s16[1,240,256]{2,1,0:T(8,128)(2,1)S(1)}, u32[]{:S(2)}, u32[]{:S(2)}) collective-permute-start(s16[1,240,256]{2,1,0:T(8,128)(2,1)S(1)} %shard_map.91.own), channel_id=1, source_target_pairs={{0,24},{1,25},{2,26},{3,27},{4,7},{5,6},{6,5},{7,4},{8,16},{9,17},... | collective-permute-start | bytes 368648 | tf_op jit(solution)/shard_map/ppermute | solution.py:81
  61.9 2.0 %collective-permute-done.16.got_1 = s16[1,240,256]{2,1,0:T(8,128)(2,1)S(1)} collective-permute-done((s16[1,240,256]{2,1,0:T(8,128)(2,1)S(1)}, s16[1,240,256]{2,1,0:T(8,128)(2,1)S(1)}, u32[]{:S(2)}, u32[]{:S(2)}) %collective-permute-start.16) | collective-permute-done | bytes 122912 | tf_op jit(solution)/shard_map/ppermute | solution.py:81
  63.9 1.3 %collective-permute-done.18.got_3 = s16[1,240,256]{2,1,0:T(8,128)(2,1)S(1)} collective-permute-done((s16[1,240,256]{2,1,0:T(8,128)(2,1)S(1)}, s16[1,240,256]{2,1,0:T(8,128)(2,1)S(1)}, u32[]{:S(2)}, u32[]{:S(2)}) %collective-permute-start.18) | collective-permute-done | bytes 122912 | tf_op jit(solution)/shard_map/ppermute | solution.py:81
  65.9 1.4 %collective-permute-start.20 = (s16[1,240,256]{2,1,0:T(8,128)(2,1)S(1)}, s16[1,240,256]{2,1,0:T(8,128)(2,1)S(1)}, u32[]{:S(2)}, u32[]{:S(2)}) collective-permute-start(s16[1,240,256]{2,1,0:T(8,128)(2,1)S(1)} %shard_map.92), channel_id=1, source_target_pairs={{0,1},{1,0},{2,3},{3,2},{4,5},{5,4},{6,7},{7,6},{8,9},{9,8},{10,11... | collective-permute-start | bytes 368648 | tf_op jit(solution)/shard_map/ppermute | solution.py:81
  67.3 0.8 collective-permute-start.21
  68.1 2.0 %collective-permute-done.19 = s16[1,240,256]{2,1,0:T(8,128)(2,1)S(1)} collective-permute-done((s16[1,240,256]{2,1,0:T(8,128)(2,1)S(1)}, s16[1,240,256]{2,1,0:T(8,128)(2,1)S(1)}, u32[]{:S(2)}, u32[]{:S(2)}) %collective-permute-start.19) | collective-permute-done | bytes 122912 | tf_op jit(solution)/shard_map/ppermute | solution.py:81
  70.1 0.7 collective-permute-done.20
  70.9 0.5 collective-permute-done.21
  71.5 3.5 %collective-permute-start.22 = (s16[4,240,256]{2,1,0:T(8,128)(2,1)S(1)}, s16[4,240,256]{2,1,0:T(8,128)(2,1)S(1)}, u32[]{:S(2)}, u32[]{:S(2)}) collective-permute-start(s16[4,240,256]{2,1,0:T(8,128)(2,1)S(1)} %pad_add_fusion.refs_0_), channel_id=1, source_target_pairs={{0,11},{1,10},{2,9},{3,8},{4,124},{5,125},{6,126},{7,127},{8,3},{9... | collective-permute-start | bytes 1474568 | tf_op jit(solution)/shard_map/ppermute | solution.py:81
  74.9 0.8 collective-permute-start.23
  75.7 1.4 %collective-permute-start.24 = (s16[4,240,256]{2,1,0:T(8,128)(2,1)S(1)}, s16[4,240,256]{2,1,0:T(8,128)(2,1)S(1)}, u32[]{:S(2)}, u32[]{:S(2)}) collective-permute-start(s16[4,240,256]{2,1,0:T(8,128)(2,1)S(1)} %pad_add_fusion.refs_0_), channel_id=1, source_target_pairs={{0,3},{1,2},{2,1},{3,0},{4,28},{5,29},{6,30},{7,31},{8,11},{9,10},... | collective-permute-start | bytes 1474568 | tf_op jit(solution)/shard_map/ppermute | solution.py:81
  77.1 6.0 %shard_map.93 = bf16[2,8,64,256]{3,2,1,0:T(8,128)(2,1)} custom-call(s32[2]{0:T(128)S(1)} %pad_add_fusion.1.odd, bf16[3,480,160]{2,1,0:T(8,128)(2,1)S(1)} %shard_map.76.pick, bf16[8,8,16,256]{3,2,1,0:T(8,128)(2,1)S(1)} %get-tuple-element.68.grad, bf16[2,8,16,256]{3,2,1,0:T(8,128)(2,1)S(1)} %collective-permute-done.4.y_a, ...), custom_call_target="tpu_custom_call" | custom-call | tf_op jit(solution)/shard_map/pallas_call | solution.py:90
  83.0 1.5 %shard_map.94.refs_3_ = f32[27,256,256]{2,1,0:T(8,128)} custom-call(s32[6]{0:T(128)S(1)} %stack.30.where, s16[4,240,256]{2,1,0:T(8,128)(2,1)S(1)} %pad_add_fusion.refs_0_), custom_call_target="tpu_custom_call" | custom-call | tf_op jit(solution)/shard_map/pallas_call | solution.py:223
  84.6 3.0 %collective-permute-done.23.refs_1_ = s16[4,240,256]{2,1,0:T(8,128)(2,1)S(1)} collective-permute-done((s16[4,240,256]{2,1,0:T(8,128)(2,1)S(1)}, s16[4,240,256]{2,1,0:T(8,128)(2,1)S(1)}, u32[]{:S(2)}, u32[]{:S(2)}) %collective-permute-start.23) | collective-permute-done | bytes 491552 | tf_op jit(solution)/shard_map/ppermute | solution.py:81
  87.5 0.6 collective-permute-done.24.refs_2_
  88.1 3.2 %collective-permute-start.25 = (s16[4,240,256]{2,1,0:T(8,128)(2,1)S(1)}, s16[4,240,256]{2,1,0:T(8,128)(2,1)S(1)}, u32[]{:S(2)}, u32[]{:S(2)}) collective-permute-start(s16[4,240,256]{2,1,0:T(8,128)(2,1)S(1)} %pad_add_fusion.refs_0_), channel_id=1, source_target_pairs={{0,4},{1,5},{2,6},{3,7},{4,0},{5,1},{6,2},{7,3},{8,12},{9,13},{10,... | collective-permute-start | bytes 1474568 | tf_op jit(solution)/shard_map/ppermute | solution.py:453
  91.8 2.2 %shard_map.95.refs_4_ = f32[27,256,256]{2,1,0:T(8,128)} custom-call(s32[6]{0:T(128)S(1)} %stack.30.where, s16[4,240,256]{2,1,0:T(8,128)(2,1)S(1)} %collective-permute-done.22.refs_0_, s16[4,240,256]{2,1,0:T(8,128)(2,1)S(1)} %collective-permute-done.23.refs_1_, ...), custom_call_target="tpu_custom_call", output_to_operand_aliasing={{}: (4, {})} | custom-call | tf_op jit(solution)/shard_map/pallas_call | solution.py:223
  94.2 0.7 collective-permute-done.28.refs_3_
  94.9 2.6 %shard_map.96 = f32[27,256,256]{2,1,0:T(8,128)} custom-call(s32[6]{0:T(128)S(1)} %stack.30.where, s16[4,240,256]{2,1,0:T(8,128)(2,1)S(1)} %collective-permute-done.25.refs_0_, s16[4,240,256]{2,1,0:T(8,128)(2,1)S(1)} %collective-permute-done.26.refs_1_, s16[4,240,256]{2,1,0:T(8,128)(2,1)S(1)} %collective-permute-done.27.refs_2_, ...), custom_call_target="tpu_custom_call", output_to_operand_aliasing={{}: (5, {})} | custom-call | tf_op jit(solution)/shard_map/pallas_call | solution.py:223
  (44 shorter events, 3.8 us)
Async XLA Ops:
  0.6 2.2 %copy-start.1 = (bf16[2,8,8,8,256]{4,3,2,1,0:T(8,128)(2,1)S(1)}, bf16[2,8,8,8,256]{4,3,2,1,0:T(8,128)(2,1)}, u32[]{:S(2)}) copy-start(bf16[2,8,8,8,256]{4,3,2,1,0:T(8,128)(2,1)} %param.5) | copy-start | bytes 1572868
  0.6 2.2 %copy-start.2 = (bf16[2,8,8,8,256]{4,3,2,1,0:T(8,128)(2,1)S(1)}, bf16[2,8,8,8,256]{4,3,2,1,0:T(8,128)(2,1)}, u32[]{:S(2)}) copy-start(bf16[2,8,8,8,256]{4,3,2,1,0:T(8,128)(2,1)} %param.6) | copy-start | bytes 1572868
  0.7 2.2 %copy-start.3 = (s32[2,512]{1,0:T(2,128)S(1)}, s32[2,512]{1,0:T(2,128)}, u32[]{:S(2)}) copy-start(s32[2,512]{1,0:T(2,128)} %occupancy.1) | copy-start | bytes 12292
  0.7 0.8 copy-start.4
  4.5 4.9 %collective-permute-start = (bf16[2,8,16,256]{3,2,1,0:T(8,128)(2,1)S(1)}, bf16[2,8,16,256]{3,2,1,0:T(8,128)(2,1)S(1)}, u32[]{:S(2)}, u32[]{:S(2)}) collective-permute-start(bf16[2,8,16,256]{3,2,1,0:T(8,128)(2,1)S(1)} %get-tuple-element.40), channel_id=1, source_target_pairs={{0,4},{4,0},{8,12},{12,8},{16,20},{20,16},{24,28},{28,24},{32,36},... | collective-permute-start | bytes 393224 | tf_op jit(solution)/shard_map/ppermute | solution.py:397
  5.9 7.9 %collective-permute-start.1 = (bf16[2,8,16,256]{3,2,1,0:T(8,128)(2,1)S(1)}, bf16[2,8,16,256]{3,2,1,0:T(8,128)(2,1)S(1)}, u32[]{:S(2)}, u32[]{:S(2)}) collective-permute-start(bf16[2,8,16,256]{3,2,1,0:T(8,128)(2,1)S(1)} %get-tuple-element.41), channel_id=1, source_target_pairs={{4,8},{8,4},{12,16},{16,12},{20,24},{24,20},{28,32},{32,28},{36,40... | collective-permute-start | bytes 393224 | tf_op jit(solution)/shard_map/ppermute | solution.py:397
  9.5 5.9 %collective-permute-start.5 = (bf16[2,8,16,256]{3,2,1,0:T(8,128)(2,1)}, bf16[2,8,16,256]{3,2,1,0:T(8,128)(2,1)S(1)}, u32[]{:S(2)}, u32[]{:S(2)}) collective-permute-start(bf16[2,8,16,256]{3,2,1,0:T(8,128)(2,1)} %get-tuple-element.48), channel_id=1, source_target_pairs={{1,2},{2,1},{5,6},{6,5},{9,10},{10,9},{13,14},{14,13},{17,18},{18,... | collective-permute-start | bytes 393224 | tf_op jit(solution)/shard_map/ppermute | solution.py:397
  10.1 6.7 %collective-permute-start.4 = (bf16[2,8,16,256]{3,2,1,0:T(8,128)(2,1)S(1)}, bf16[2,8,16,256]{3,2,1,0:T(8,128)(2,1)S(1)}, u32[]{:S(2)}, u32[]{:S(2)}) collective-permute-start(bf16[2,8,16,256]{3,2,1,0:T(8,128)(2,1)S(1)} %get-tuple-element.46), channel_id=1, source_target_pairs={{0,1},{1,0},{2,3},{3,2},{4,5},{5,4},{6,7},{7,6},{8,9},{9,8},{10,11... | collective-permute-start | bytes 393224 | tf_op jit(solution)/shard_map/ppermute | solution.py:397
  14.4 3.6 %collective-permute-start.2 = (bf16[2,2,16,256]{3,2,1,0:T(8,128)(2,1)S(1)}, bf16[2,2,16,256]{3,2,1,0:T(8,128)(2,1)S(1)}, u32[]{:S(2)}, u32[]{:S(2)}) collective-permute-start(bf16[2,2,16,256]{3,2,1,0:T(8,128)(2,1)S(1)} %get-tuple-element.42), channel_id=1, source_target_pairs={{0,1},{1,0},{2,3},{3,2},{4,5},{5,4},{6,7},{7,6},{8,9},{9,8},{10,11... | collective-permute-start | bytes 98312 | tf_op jit(solution)/shard_map/ppermute | solution.py:397
  14.5 3.5 %collective-permute-start.3 = (bf16[2,2,16,256]{3,2,1,0:T(8,128)(2,1)S(1)}, bf16[2,2,16,256]{3,2,1,0:T(8,128)(2,1)S(1)}, u32[]{:S(2)}, u32[]{:S(2)}) collective-permute-start(bf16[2,2,16,256]{3,2,1,0:T(8,128)(2,1)S(1)} %get-tuple-element.43), channel_id=1, source_target_pairs={{1,2},{2,1},{5,6},{6,5},{9,10},{10,9},{13,14},{14,13},{17,18},{18,... | collective-permute-start | bytes 98312 | tf_op jit(solution)/shard_map/ppermute | solution.py:397
  20.7 2.5 %collective-permute-start.6 = (s16[4,240,256]{2,1,0:T(8,128)(2,1)S(1)}, s16[4,240,256]{2,1,0:T(8,128)(2,1)S(1)}, u32[]{:S(2)}, u32[]{:S(2)}) collective-permute-start(s16[4,240,256]{2,1,0:T(8,128)(2,1)S(1)} %get-tuple-element.53), channel_id=1, source_target_pairs={{0,4},{1,5},{2,6},{3,7},{4,0},{5,1},{6,2},{7,3},{8,12},{9,13},{10,... | collective-permute-start | bytes 1474568 | tf_op jit(solution)/shard_map/ppermute | solution.py:430
  22.6 14.9 %copy-start = (bf16[27,256,256]{2,1,0:T(8,128)(2,1)S(1)}, bf16[27,256,256]{2,1,0:T(8,128)(2,1)}, u32[]{:S(2)}) copy-start(bf16[27,256,256]{2,1,0:T(8,128)(2,1)} %kernel.3) | copy-start | bytes 10616836
  22.6 2.6 %collective-permute-start.7 = (s16[4,240,256]{2,1,0:T(8,128)(2,1)S(1)}, s16[4,240,256]{2,1,0:T(8,128)(2,1)S(1)}, u32[]{:S(2)}, u32[]{:S(2)}) collective-permute-start(s16[4,240,256]{2,1,0:T(8,128)(2,1)S(1)} %get-tuple-element.56), channel_id=1, source_target_pairs={{0,4},{1,5},{2,6},{3,7},{4,0},{5,1},{6,2},{7,3},{8,12},{9,13},{10,... | collective-permute-start | bytes 1474568 | tf_op jit(solution)/shard_map/ppermute | solution.py:430
  25.1 8.6 %collective-permute-start.10 = (s16[4,240,256]{2,1,0:T(8,128)(2,1)S(1)}, s16[4,240,256]{2,1,0:T(8,128)(2,1)S(1)}, u32[]{:S(2)}, u32[]{:S(2)}) collective-permute-start(s16[4,240,256]{2,1,0:T(8,128)(2,1)S(1)} %get-tuple-element.63), channel_id=1, source_target_pairs={{0,4},{1,5},{2,6},{3,7},{4,0},{5,1},{6,2},{7,3},{8,12},{9,13},{10,... | collective-permute-start | bytes 1474568 | tf_op jit(solution)/shard_map/ppermute | solution.py:430
  27.4 7.4 %collective-permute-start.8 = (s16[4,240,256]{2,1,0:T(8,128)(2,1)S(1)}, s16[4,240,256]{2,1,0:T(8,128)(2,1)S(1)}, u32[]{:S(2)}, u32[]{:S(2)}) collective-permute-start(s16[4,240,256]{2,1,0:T(8,128)(2,1)S(1)} %get-tuple-element.59), channel_id=1, source_target_pairs={{0,4},{1,5},{2,6},{3,7},{4,0},{5,1},{6,2},{7,3},{8,12},{9,13},{10,... | collective-permute-start | bytes 1474568 | tf_op jit(solution)/shard_map/ppermute | solution.py:430
  27.9 14.3 %collective-permute-start.9 = (s16[4,240,256]{2,1,0:T(8,128)(2,1)S(1)}, s16[4,240,256]{2,1,0:T(8,128)(2,1)S(1)}, u32[]{:S(2)}, u32[]{:S(2)}) collective-permute-start(s16[4,240,256]{2,1,0:T(8,128)(2,1)S(1)} %shard_map.85), channel_id=1, source_target_pairs={{0,11},{1,10},{2,9},{3,8},{4,124},{5,125},{6,126},{7,127},{8,3},{9... | collective-permute-start | bytes 1474568 | tf_op jit(solution)/shard_map/ppermute | solution.py:433
  34.0 11.8 %collective-permute-start.11 = (s16[4,240,256]{2,1,0:T(8,128)(2,1)S(1)}, s16[4,240,256]{2,1,0:T(8,128)(2,1)S(1)}, u32[]{:S(2)}, u32[]{:S(2)}) collective-permute-start(s16[4,240,256]{2,1,0:T(8,128)(2,1)S(1)} %shard_map.89), channel_id=1, source_target_pairs={{0,8},{1,9},{2,10},{3,11},{4,100},{5,101},{6,102},{7,103},{8,0},{9... | collective-permute-start | bytes 1474568 | tf_op jit(solution)/shard_map/ppermute | solution.py:433
  35.2 10.7 %collective-permute-start.12 = (s16[4,240,256]{2,1,0:T(8,128)(2,1)S(1)}, s16[4,240,256]{2,1,0:T(8,128)(2,1)S(1)}, u32[]{:S(2)}, u32[]{:S(2)}) collective-permute-start(s16[4,240,256]{2,1,0:T(8,128)(2,1)S(1)} %shard_map.87), channel_id=1, source_target_pairs={{0,3},{1,2},{2,1},{3,0},{4,28},{5,29},{6,30},{7,31},{8,11},{9,10},... | collective-permute-start | bytes 1474568 | tf_op jit(solution)/shard_map/ppermute | solution.py:433
  46.4 8.7 %collective-permute-start.13 = (s16[1,240,256]{2,1,0:T(8,128)(2,1)S(1)}, s16[1,240,256]{2,1,0:T(8,128)(2,1)S(1)}, u32[]{:S(2)}, u32[]{:S(2)}) collective-permute-start(s16[1,240,256]{2,1,0:T(8,128)(2,1)S(1)} %get-tuple-element.65), channel_id=1, source_target_pairs={{0,33},{1,32},{2,35},{3,34},{4,37},{5,36},{6,39},{7,38},{8,41},{9,... | collective-permute-start | bytes 368648 | tf_op jit(solution)/shard_map/ppermute | solution.py:81
  51.3 5.5 %collective-permute-start.14 = (s16[1,240,256]{2,1,0:T(8,128)(2,1)S(1)}, s16[1,240,256]{2,1,0:T(8,128)(2,1)S(1)}, u32[]{:S(2)}, u32[]{:S(2)}) collective-permute-start(s16[1,240,256]{2,1,0:T(8,128)(2,1)S(1)} %get-tuple-element.66), channel_id=1, source_target_pairs={{0,1},{1,0},{2,3},{3,2},{4,5},{5,4},{6,7},{7,6},{8,9},{9,8},{10,11... | collective-permute-start | bytes 368648 | tf_op jit(solution)/shard_map/ppermute | solution.py:81
  51.3 6.4 %collective-permute-start.15 = (s16[1,240,256]{2,1,0:T(8,128)(2,1)S(1)}, s16[1,240,256]{2,1,0:T(8,128)(2,1)S(1)}, u32[]{:S(2)}, u32[]{:S(2)}) collective-permute-start(s16[1,240,256]{2,1,0:T(8,128)(2,1)S(1)} %get-tuple-element.67), channel_id=1, source_target_pairs={{0,32},{1,33},{2,34},{3,35},{4,36},{5,37},{6,38},{7,39},{8,40},{9,... | collective-permute-start | bytes 368648 | tf_op jit(solution)/shard_map/ppermute | solution.py:81
  58.0 5.9 %collective-permute-start.16 = (s16[1,240,256]{2,1,0:T(8,128)(2,1)S(1)}, s16[1,240,256]{2,1,0:T(8,128)(2,1)S(1)}, u32[]{:S(2)}, u32[]{:S(2)}) collective-permute-start(s16[1,240,256]{2,1,0:T(8,128)(2,1)S(1)} %shard_map.91.own), channel_id=1, source_target_pairs={{0,120},{1,121},{2,122},{3,123},{4,15},{5,14},{6,13},{7,12},{8,112... | collective-permute-start | bytes 368648 | tf_op jit(solution)/shard_map/ppermute | solution.py:81
  58.1 5.8 %collective-permute-start.17 = (s16[1,240,256]{2,1,0:T(8,128)(2,1)S(1)}, s16[1,240,256]{2,1,0:T(8,128)(2,1)S(1)}, u32[]{:S(2)}, u32[]{:S(2)}) collective-permute-start(s16[1,240,256]{2,1,0:T(8,128)(2,1)S(1)} %shard_map.91.own), channel_id=1, source_target_pairs={{0,96},{1,97},{2,98},{3,99},{4,12},{5,13},{6,14},{7,15},{8,104},{9... | collective-permute-start | bytes 368648 | tf_op jit(solution)/shard_map/ppermute | solution.py:81
  60.0 5.2 %collective-permute-start.18 = (s16[1,240,256]{2,1,0:T(8,128)(2,1)S(1)}, s16[1,240,256]{2,1,0:T(8,128)(2,1)S(1)}, u32[]{:S(2)}, u32[]{:S(2)}) collective-permute-start(s16[1,240,256]{2,1,0:T(8,128)(2,1)S(1)} %shard_map.91.own), channel_id=1, source_target_pairs={{0,24},{1,25},{2,26},{3,27},{4,7},{5,6},{6,5},{7,4},{8,16},{9,17},... | collective-permute-start | bytes 368648 | tf_op jit(solution)/shard_map/ppermute | solution.py:81
  65.4 4.7 %collective-permute-start.19 = (s16[1,240,256]{2,1,0:T(8,128)(2,1)S(1)}, s16[1,240,256]{2,1,0:T(8,128)(2,1)S(1)}, u32[]{:S(2)}, u32[]{:S(2)}) collective-permute-start(s16[1,240,256]{2,1,0:T(8,128)(2,1)S(1)} %shard_map.92), channel_id=1, source_target_pairs={{0,33},{1,32},{2,35},{3,34},{4,37},{5,36},{6,39},{7,38},{8,41},{9,... | collective-permute-start | bytes 368648 | tf_op jit(solution)/shard_map/ppermute | solution.py:81
  65.9 5.0 %collective-permute-start.20 = (s16[1,240,256]{2,1,0:T(8,128)(2,1)S(1)}, s16[1,240,256]{2,1,0:T(8,128)(2,1)S(1)}, u32[]{:S(2)}, u32[]{:S(2)}) collective-permute-start(s16[1,240,256]{2,1,0:T(8,128)(2,1)S(1)} %shard_map.92), channel_id=1, source_target_pairs={{0,1},{1,0},{2,3},{3,2},{4,5},{5,4},{6,7},{7,6},{8,9},{9,8},{10,11... | collective-permute-start | bytes 368648 | tf_op jit(solution)/shard_map/ppermute | solution.py:81
  67.3 4.1 %collective-permute-start.21 = (s16[1,240,256]{2,1,0:T(8,128)(2,1)S(1)}, s16[1,240,256]{2,1,0:T(8,128)(2,1)S(1)}, u32[]{:S(2)}, u32[]{:S(2)}) collective-permute-start(s16[1,240,256]{2,1,0:T(8,128)(2,1)S(1)} %shard_map.92), channel_id=1, source_target_pairs={{0,32},{1,33},{2,34},{3,35},{4,36},{5,37},{6,38},{7,39},{8,40},{9,... | collective-permute-start | bytes 368648 | tf_op jit(solution)/shard_map/ppermute | solution.py:81
  71.5 13.1 %collective-permute-start.22 = (s16[4,240,256]{2,1,0:T(8,128)(2,1)S(1)}, s16[4,240,256]{2,1,0:T(8,128)(2,1)S(1)}, u32[]{:S(2)}, u32[]{:S(2)}) collective-permute-start(s16[4,240,256]{2,1,0:T(8,128)(2,1)S(1)} %pad_add_fusion.refs_0_), channel_id=1, source_target_pairs={{0,11},{1,10},{2,9},{3,8},{4,124},{5,125},{6,126},{7,127},{8,3},{9... | collective-permute-start | bytes 1474568 | tf_op jit(solution)/shard_map/ppermute | solution.py:81
  74.9 12.6 %collective-permute-start.23 = (s16[4,240,256]{2,1,0:T(8,128)(2,1)S(1)}, s16[4,240,256]{2,1,0:T(8,128)(2,1)S(1)}, u32[]{:S(2)}, u32[]{:S(2)}) collective-permute-start(s16[4,240,256]{2,1,0:T(8,128)(2,1)S(1)} %pad_add_fusion.refs_0_), channel_id=1, source_target_pairs={{0,8},{1,9},{2,10},{3,11},{4,100},{5,101},{6,102},{7,103},{8,0},{9... | collective-permute-start | bytes 1474568 | tf_op jit(solution)/shard_map/ppermute | solution.py:81
  75.7 12.4 %collective-permute-start.24 = (s16[4,240,256]{2,1,0:T(8,128)(2,1)S(1)}, s16[4,240,256]{2,1,0:T(8,128)(2,1)S(1)}, u32[]{:S(2)}, u32[]{:S(2)}) collective-permute-start(s16[4,240,256]{2,1,0:T(8,128)(2,1)S(1)} %pad_add_fusion.refs_0_), channel_id=1, source_target_pairs={{0,3},{1,2},{2,1},{3,0},{4,28},{5,29},{6,30},{7,31},{8,11},{9,10},... | collective-permute-start | bytes 1474568 | tf_op jit(solution)/shard_map/ppermute | solution.py:81
  88.1 6.0 %collective-permute-start.25 = (s16[4,240,256]{2,1,0:T(8,128)(2,1)S(1)}, s16[4,240,256]{2,1,0:T(8,128)(2,1)S(1)}, u32[]{:S(2)}, u32[]{:S(2)}) collective-permute-start(s16[4,240,256]{2,1,0:T(8,128)(2,1)S(1)} %pad_add_fusion.refs_0_), channel_id=1, source_target_pairs={{0,4},{1,5},{2,6},{3,7},{4,0},{5,1},{6,2},{7,3},{8,12},{9,13},{10,... | collective-permute-start | bytes 1474568 | tf_op jit(solution)/shard_map/ppermute | solution.py:453
  91.3 2.8 %collective-permute-start.26 = (s16[4,240,256]{2,1,0:T(8,128)(2,1)S(1)}, s16[4,240,256]{2,1,0:T(8,128)(2,1)S(1)}, u32[]{:S(2)}, u32[]{:S(2)}) collective-permute-start(s16[4,240,256]{2,1,0:T(8,128)(2,1)S(1)} %collective-permute-done.22.refs_0_), channel_id=1, source_target_pairs={{0,4},{1,5},{2,6},{3,7},{4,0},{5,1},{6,2},{7,3},{8,12},{9,13},{10,... | collective-permute-start | bytes 1474568 | tf_op jit(solution)/shard_map/ppermute | solution.py:453
  91.3 2.9 %collective-permute-start.27 = (s16[4,240,256]{2,1,0:T(8,128)(2,1)S(1)}, s16[4,240,256]{2,1,0:T(8,128)(2,1)S(1)}, u32[]{:S(2)}, u32[]{:S(2)}) collective-permute-start(s16[4,240,256]{2,1,0:T(8,128)(2,1)S(1)} %collective-permute-done.23.refs_1_), channel_id=1, source_target_pairs={{0,4},{1,5},{2,6},{3,7},{4,0},{5,1},{6,2},{7,3},{8,12},{9,13},{10,... | collective-permute-start | bytes 1474568 | tf_op jit(solution)/shard_map/ppermute | solution.py:453
  91.8 3.1 %collective-permute-start.28 = (s16[4,240,256]{2,1,0:T(8,128)(2,1)S(1)}, s16[4,240,256]{2,1,0:T(8,128)(2,1)S(1)}, u32[]{:S(2)}, u32[]{:S(2)}) collective-permute-start(s16[4,240,256]{2,1,0:T(8,128)(2,1)S(1)} %collective-permute-done.24.refs_2_), channel_id=1, source_target_pairs={{0,4},{1,5},{2,6},{3,7},{4,0},{5,1},{6,2},{7,3},{8,12},{9,13},{10,... | collective-permute-start | bytes 1474568 | tf_op jit(solution)/shard_map/ppermute | solution.py:453
